TPU v7x, 32 devices: a whole 2x2x4 slice. The times are simulated.
32 devices in a mesh: inp: 4 (over x, core), chan: 8 (over z, y).
Axes of the slice: x: 2, y: 2, z: 4, core: 2. Of those that a mesh axis runs over, the one named last changes fastest.
Arguments:
- voltages: bfloat16 [2, 512, 77824], P(None, ('inp', 'chan')), may hold values from -6 to 6
- filter_taps: float32 [16, 4096], replicated, may hold values from -1.5 to 1.5
- pairing: int32 [3], replicated, may hold values from 1 to 3, as said below
Outputs:
- visibilities: float32 [2, 3, 32, 512, 128], P(None, None, 'chan', 'inp')
- autos: float32 [2, 64, 512, 128], P(None, 'chan', 'inp')
Inputs may be any that keep to these rules, and one draw needn't show every extreme that they name: Every value from 1 to 3 appears exactly once; in round r block a is paired with block a XOR pairing[r].
All inputs are finite; a program needn't handle non-finite values.
Results may differ from a plain program's by a relative error of at most 0.004.
Values may be sent and summed in bfloat16 or wider, within the bound.
No kernel may reach another device: no remote copies, remote signals or barrier semaphores. Data moves between devices by JAX's collectives and lax.ppermute only.
A program may use at most 64 MiB of HBM per device.

v0:
```python
import math

import jax
import jax.numpy as jnp
from jax import lax
from jax.sharding import PartitionSpec as P

AVG = 64


def phase_table(row_count, col_count, modulus):
    product = (
        jnp.arange(row_count, dtype=jnp.int32)[:, None]
        * jnp.arange(col_count, dtype=jnp.int32)[None, :]
        % modulus
    )
    angle = product.astype(jnp.float32) * (2.0 * math.pi / modulus)
    return (jnp.cos(angle), jnp.sin(angle))


def transform(filtered):
    signals = filtered.shape[1]
    spectra_count = filtered.shape[2]
    fine_count = filtered.shape[3]
    inner = 128
    outer = fine_count // inner
    highest = lax.Precision.HIGHEST
    shaped = filtered.reshape(2, signals, spectra_count, outer, inner)
    cos_first, sin_first = phase_table(outer, outer, outer)
    real_first = jnp.einsum("nspq,pk->nskq", shaped[0], cos_first, precision=highest) + jnp.einsum(
        "nspq,pk->nskq", shaped[1], sin_first, precision=highest
    )
    imag_first = jnp.einsum("nspq,pk->nskq", shaped[1], cos_first, precision=highest) - jnp.einsum(
        "nspq,pk->nskq", shaped[0], sin_first, precision=highest
    )
    cos_twist, sin_twist = phase_table(outer, inner, fine_count)
    real_twist = real_first * cos_twist + imag_first * sin_twist
    imag_twist = imag_first * cos_twist - real_first * sin_twist
    cos_last, sin_last = phase_table(inner, inner, inner)
    real_last = jnp.einsum("nskq,qm->nsmk", real_twist, cos_last, precision=highest) + jnp.einsum(
        "nskq,qm->nsmk", imag_twist, sin_last, precision=highest
    )
    imag_last = jnp.einsum("nskq,qm->nsmk", imag_twist, cos_last, precision=highest) - jnp.einsum(
        "nskq,qm->nsmk", real_twist, sin_last, precision=highest
    )
    stacked = jnp.stack([real_last, imag_last]).reshape(2, signals, spectra_count, fine_count)
    return stacked * fine_count ** (-0.5)


def correlate(left_side, right_side):
    signals = left_side.shape[1]
    spectra_count = left_side.shape[2]
    groups = left_side.shape[3] // AVG

    def arrange(values):
        shaped = values.reshape(2, signals, spectra_count, groups, AVG)
        return shaped.transpose(0, 3, 1, 2, 4).reshape(2, groups, signals, spectra_count * AVG)

    left_rows = arrange(left_side)
    right_rows = arrange(right_side)
    first_rows = jnp.concatenate([left_rows[0], left_rows[1]], -1)
    second_rows = jnp.concatenate([left_rows[1], -left_rows[0]], -1)
    other_rows = jnp.concatenate([right_rows[0], right_rows[1]], -1)
    real_part = jnp.einsum(
        "gik,gjk->gij", first_rows, other_rows, preferred_element_type=jnp.float32
    )
    imag_part = jnp.einsum(
        "gik,gjk->gij", second_rows, other_rows, preferred_element_type=jnp.float32
    )
    return jnp.stack([real_part, imag_part]) / (spectra_count * AVG)


def on_device(voltages, filter_taps, pairing):
    tap_count = filter_taps.shape[0]
    fine_count = filter_taps.shape[1]
    signals = voltages.shape[1]
    frame_count = voltages.shape[2] // fine_count
    spectra_count = frame_count - tap_count + 1
    frames = voltages.reshape(2, signals, frame_count, fine_count)
    filtered = filter_taps[0] * frames[:, :, 0:spectra_count, :].astype(jnp.float32)
    for tap_index in range(1, tap_count):
        filtered = filtered + filter_taps[tap_index] * frames[
            :, :, tap_index : tap_index + spectra_count, :
        ].astype(jnp.float32)
    spectra = transform(filtered).astype(jnp.bfloat16)
    channel_block = lax.all_to_all(spectra, "chan", split_axis=3, concat_axis=1, tiled=True)
    autos = correlate(channel_block, channel_block)
    own_index = lax.axis_index("inp")
    inp_count = lax.axis_size("inp")
    half_width = channel_block.shape[3] // 2
    round_count = pairing.shape[0]
    partners = []
    own_halves = []
    outgoing = []
    for round_index in range(round_count):
        partner = jnp.bitwise_xor(own_index, pairing[round_index])
        upper = (own_index > partner).astype(jnp.int32)
        own_halves.append(
            lax.dynamic_slice_in_dim(channel_block, upper * half_width, half_width, 3)
        )
        outgoing.append(
            lax.dynamic_slice_in_dim(channel_block, (1 - upper) * half_width, half_width, 3)
        )
        partners.append(partner)
    moving_all = jnp.stack(outgoing, axis=0)
    slot_ids = jnp.arange(inp_count, dtype=jnp.int32)
    partner_ids = jnp.stack(partners)
    matches = slot_ids[:, None] == partner_ids[None, :]
    round_of_slot = jnp.argmax(matches.astype(jnp.int32), axis=1)
    filled = jnp.any(matches, axis=1)[:, None, None, None, None]
    slots = jnp.where(
        filled, jnp.take(moving_all, round_of_slot, axis=0), jnp.zeros((), jnp.bfloat16)
    )
    received = lax.all_to_all(slots, "inp", split_axis=0, concat_axis=0, tiled=True)
    incoming = jnp.take(received, partner_ids, axis=0)
    results = [
        correlate(own_halves[round_index], incoming[round_index])
        for round_index in range(round_count)
    ]
    visibilities = jnp.stack(results, axis=1)
    return (visibilities, autos)


def solution(mesh):
    in_specs = (P(None, ("inp", "chan"), None), P(), P())
    out_specs = (P(None, None, "chan", "inp", None), P(None, "chan", "inp", None))
    return jax.shard_map(
        on_device, mesh=mesh, in_specs=in_specs, out_specs=out_specs, check_vma=False
    )
```

profile of v0, /device:TPU:0, one launch (start us, length us, event | category | flops | bytes accessed | tf_op | source)
XLA Modules:
  0.0 179.7 jit_solution(6270544077959165294)
XLA Ops:
  0.7 2.3 %fusion.123 = (f32[1,4096]{1,0:T(1,128)S(1)}, f32[1,4096]{1,0:T(1,128)S(1)}, f32[1,4096]{1,0:T(1,128)S(1)}, f32[1,4096]{1,0:T(1,128)S(1)}, f32[1,4096]{1,0:T(1,1...) fusion(f32[16,4096]{1,0:T(8,128)} %param.4), kind=kLoop, calls=%fused_computation.170 | loop fusion | bytes 524288 | tf_op jit(solution)/shard_map/slice | solution.py:80
  3.0 7.1 %reshape.358 = bf16[2,16,19,4096]{3,2,1,0:T(8,128)(2,1)} reshape(bf16[2,16,77824]{2,1,0:T(8,128)(2,1)} %param.3) | data formatting | bytes 9961472 | tf_op jit(solution)/shard_map/reshape | solution.py:79
  10.1 23.6 %multiply_add_fusion = f32[2,16,4,4096]{3,2,1,0:T(4,128)S(1)} fusion(bf16[2,16,19,4096]{3,2,1,0:T(8,128)(2,1)} %reshape.358, f32[4096]{0:T(1024)S(1)} %bitcast.187, f32[4096]{0:T(1024)S(1)} %bitcast.188, f32[4096]{0:T(1024)S(1)} %bitcast.174, f32[4096]{0:T(1024)S(1)} %bitcast.175, f32[4096]{0:T(1024)S(1)} %bitcast.176, f32[4096]{0:T(1024)S(1)} %bitcast.177, ...), kind=kLoop, calls=%fused_computation.5 | loop fusion | flops 24641536 | bytes 19136512 | tf_op jit(solution)/shard_map/add | solution.py:82
  33.8 0.7 squeeze.70
  34.6 2.1 %fusion.54 = f32[32,16,4,128]{3,0,2,1:T(8,128)} fusion(f32[16,4,32,128]{3,2,1,0:T(8,128)S(1)} %squeeze.70), kind=kOutput, calls=%fused_computation.92 | convolution fusion | flops 100677632 | bytes 2097152 | tf_op jit(solution)/shard_map/nspq,pk->nskq/dot_general | solution.py:33
  36.6 0.7 squeeze.69
  37.4 1.1 fusion.56
  38.6 1.1 convolution_subtract_fusion.1
  39.7 1.1 convolution_add_fusion.1
  40.8 1.2 fusion.10
  42.0 2.2 %fusion.6 = f32[128,16,4,32]{0,3,2,1:T(8,128)} fusion(f32[32,16,4,128]{3,0,2,1:T(8,128)S(1)} %convolution_add_fusion.1, f32[32,16,4,128]{3,0,2,1:T(8,128)S(1)} %convolution_subtract_fusion.1, f32[32,128]{1,0:T(8,128)S(1)} %get-tuple-element.50, f32[32,128]{1,0:T(8,128)S(1)} %get-tuple-element.51), kind=kOutput, calls=%fused_computation.28 | convolution fusion | flops 403668992 | bytes 3178496 | tf_op jit(solution)/shard_map/nskq,qm->nsmk/dot_general | solution.py:43
  44.2 1.2 fusion.2
  45.4 2.7 %copy.185 = f32[16,4,128,32]{3,2,0,1:T(8,128)} copy(f32[16,4,128,32]{2,3,1,0:T(8,128)S(1)} %fusion.2) | data formatting | bytes 2097152 | tf_op jit(solution)/shard_map/add | solution.py:40
  48.1 3.7 %stack.83 = f32[1,16,4,4096]{3,1,2,0:T(8,128)S(1)} reshape(f32[16,4,128,32]{3,2,0,1:T(8,128)} %copy.185) | data formatting | bytes 2097152 | tf_op jit(solution)/shard_map/stack | solution.py:46
  51.8 3.4 %fusion.1 = f32[16,4,128,32]{2,3,1,0:T(8,128)} fusion(f32[128,16,4,32]{0,3,2,1:T(8,128)} %fusion.6, f32[32,16,4,128]{3,0,2,1:T(8,128)S(1)} %convolution_subtract_fusion.1, f32[32,16,4,128]{3,0,2,1:T(8,128)S(1)} %convolution_add_fusion.1, f32[32,128]{1,0:T(8,128)S(1)} %get-tuple-element.50, f32[32,128]{1,0:T(8,128)S(1)} %get-tuple-element.51), kind=kOutput, calls=%fused_computation.10 | convolution fusion | flops 403931136 | bytes 4227072 | tf_op jit(solution)/shard_map/nskq,qm->nsmk/dot_general | solution.py:43
  55.3 3.6 %copy.186 = f32[16,4,128,32]{3,2,0,1:T(8,128)} copy(f32[16,4,128,32]{2,3,1,0:T(8,128)} %fusion.1) | data formatting | bytes 2097152 | tf_op jit(solution)/shard_map/sub | solution.py:43
  58.9 3.5 %stack.84 = f32[1,16,4,4096]{3,1,2,0:T(8,128)S(1)} reshape(f32[16,4,128,32]{3,2,0,1:T(8,128)} %copy.186) | data formatting | bytes 2097152 | tf_op jit(solution)/shard_map/stack | solution.py:46
  62.6 8.8 %copy.187 = bf16[2,16,4,4096]{1,2,0,3:T(4,128)(2,1)} copy(bf16[2,16,4,4096]{3,1,2,0:T(8,128)(2,1)S(1)} %fusion) | data formatting | bytes 2097152 | tf_op jit(solution)/shard_map/convert_element_type | solution.py:85
  71.3 11.2 %reshape.384 = bf16[8,2,32768]{2,1,0:T(2,128)(2,1)} reshape(bf16[4096,2,4,16]{3,2,1,0:T(4,128)(2,1)} %bitcast.148) | data formatting | bytes 2097152
  82.6 7.4 %all-to-all-start = ((bf16[8,2,32768]{2,1,0:T(2,128)(2,1)}), bf16[8,2,32768]{2,1,0:T(2,128)(2,1)S(1)}, u32[]{:S(2)}, u32[]{:S(2)}) async-start(bf16[8,2,32768]{2,1,0:T(2,128)(2,1)} %reshape.384), calls=%async_computation | async-start | bytes 2097152 | tf_op jit(solution)/shard_map/all_to_all | solution.py:86
  90.0 0.6 fusion.124
  92.7 0.6 iota_reduce_fusion
  93.3 22.4 %all-to-all-done = bf16[8,2,32768]{2,1,0:T(2,128)(2,1)S(1)} async-done(((bf16[8,2,32768]{2,1,0:T(2,128)(2,1)}), bf16[8,2,32768]{2,1,0:T(2,128)(2,1)S(1)}, u32[]{:S(2)}, u32[]{:S(2)}) %all-to-all-start) | async-done | bytes 1048608 | tf_op jit(solution)/shard_map/all_to_all | solution.py:86
  115.8 7.6 %reshape.385 = bf16[4096,2,4,16]{3,2,1,0:T(4,128)(2,1)} reshape(bf16[8,2,32768]{2,1,0:T(2,128)(2,1)S(1)} %all-to-all-done) | data formatting | bytes 2097152
  123.3 10.8 %copy.238 = bf16[2,16,4,8,512]{4,1,3,2,0:T(8,128)(2,1)S(1)} copy(bf16[2,16,4,8,512]{1,2,0,4,3:T(4,128)(2,1)} %bitcast.149) | data formatting | bytes 2097152 | tf_op jit(solution)/shard_map/all_to_all | solution.py:86
  134.1 1.2 constant_dynamic-slice_fusion.2
  135.3 0.2 pad_maximum_fusion
  135.5 2.0 %gather_fusion = bf16[4,2,128,4,256]{4,2,3,1,0:T(8,128)(2,1)} fusion(bf16[3,2,128,4,256]{4,2,3,1,0:T(8,128)(2,1)S(1)} %pad_maximum_fusion, s32[1024]{0:T(1024)S(1)} %pad_clamp_fusion.1), kind=kCustom, calls=%fused_computation | custom fusion | bytes 4194320 | tf_op jit(solution)/shard_map/jit(_take)/gather | solution.py:112
  137.5 3.2 %select_select_fusion = bf16[4,2,128,4,256]{4,2,3,1,0:T(8,128)(2,1)} fusion(bf16[4,2,128,4,256]{4,2,3,1,0:T(8,128)(2,1)} %gather_fusion, pred[4]{0:T(512)(128)(4,1)S(1)} %compare_and_fusion, pred[4]{0:T(512)(128)(4,1)S(1)} %fusion.72), kind=kLoop, calls=%fused_computation.4 | loop fusion | flops 2097152 | bytes 4194312 | tf_op jit(solution)/shard_map/jit(_where)/select_n | solution.py:111
  140.7 4.7 %all-to-all-start.1 = ((bf16[4,2,128,4,256]{4,2,3,1,0:T(8,128)(2,1)}), bf16[4,2,128,4,256]{4,2,3,1,0:T(8,128)(2,1)}, u32[]{:S(2)}, u32[]{:S(2)}) async-start(bf16[4,2,128,4,256]{4,2,3,1,0:T(8,128)(2,1)} %select_select_fusion), calls=%async_computation.1 | async-start | bytes 4194304 | tf_op jit(solution)/shard_map/all_to_all | solution.py:114
  145.5 1.1 reshape.362
  146.6 1.1 fusion.114
  147.7 1.9 %copy.227 = bf16[1,8,128,4,64]{2,4,3,1,0:T(8,128)(2,1)S(1)} copy(bf16[1,8,128,4,64]{4,1,2,3,0:T(8,128)(2,1)} %get-tuple-element.7) | data formatting | bytes 1048576 | tf_op jit(solution)/shard_map/slice | solution.py:61
  149.7 0.2 copy.229
  149.9 0.8 copy.228
  150.7 1.0 copy.230
  151.8 0.3 copy.190
  152.3 0.9 copy.194
  153.2 0.8 neg.12
  154.0 0.3 copy.202
  154.5 0.9 copy.206
  155.4 0.8 neg.13
  156.1 0.3 copy.214
  156.7 0.8 copy.218
  157.5 0.7 neg.14
  158.3 0.4 convolution_bitcast_fusion.1
  158.7 0.4 convolution_bitcast_fusion
  159.1 1.1 maximum_multiply_fusion.1
  160.2 10.7 %all-to-all-done.1 = bf16[4,2,128,4,256]{4,2,3,1,0:T(8,128)(2,1)} async-done(((bf16[4,2,128,4,256]{4,2,3,1,0:T(8,128)(2,1)}), bf16[4,2,128,4,256]{4,2,3,1,0:T(8,128)(2,1)}, u32[]{:S(2)}, u32[]{:S(2)}) %all-to-all-start.1) | async-done | bytes 2097184 | tf_op jit(solution)/shard_map/all_to_all | solution.py:114
  170.9 2.2 %gather_fusion.1 = bf16[3,2,128,4,256]{4,2,3,1,0:T(8,128)(2,1)S(1)} fusion(bf16[4,2,128,4,256]{4,2,3,1,0:T(8,128)(2,1)} %all-to-all-done.1, s32[1024]{0:T(1024)S(1)} %pad_clamp_fusion), kind=kCustom, calls=%fused_computation.1 | custom fusion | bytes 3145740 | tf_op jit(solution)/shard_map/jit(_take)/gather | solution.py:115
  173.2 0.2 broadcast_select_fusion
  173.6 0.3 copy.195
  174.2 0.3 copy-done.9
  174.5 0.3 convolution_bitcast_fusion.7
  174.8 0.3 convolution_bitcast_fusion.6
  175.2 0.3 copy.207
  175.8 0.3 copy-done.7
  176.1 0.3 convolution_bitcast_fusion.5
  176.4 0.3 convolution_bitcast_fusion.4
  176.8 0.3 copy.219
  177.4 0.3 copy-done.5
  177.7 0.3 convolution_bitcast_fusion.3
  178.0 0.3 convolution_bitcast_fusion.2
  178.5 1.2 pad_maximum_fusion.1
  (63 shorter events, 3.1 us)
Async XLA Ops:
  37.4 1.2 copy-start
  82.6 7.4 %copy-start.11 = (s32[3]{0:T(128)S(1)}, s32[3]{0:T(128)}, u32[]{:S(2)}) copy-start(s32[3]{0:T(128)} %param.5) | copy-start | bytes 40
  82.6 33.2 %all-to-all-start = ((bf16[8,2,32768]{2,1,0:T(2,128)(2,1)}), bf16[8,2,32768]{2,1,0:T(2,128)(2,1)S(1)}, u32[]{:S(2)}, u32[]{:S(2)}) async-start(bf16[8,2,32768]{2,1,0:T(2,128)(2,1)} %reshape.384), calls=%async_computation | async-start | bytes 2097152 | tf_op jit(solution)/shard_map/all_to_all | solution.py:86
  140.7 30.2 %all-to-all-start.1 = ((bf16[4,2,128,4,256]{4,2,3,1,0:T(8,128)(2,1)}), bf16[4,2,128,4,256]{4,2,3,1,0:T(8,128)(2,1)}, u32[]{:S(2)}, u32[]{:S(2)}) async-start(bf16[4,2,128,4,256]{4,2,3,1,0:T(8,128)(2,1)} %select_select_fusion), calls=%async_computation.1 | async-start | bytes 4194304 | tf_op jit(solution)/shard_map/all_to_all | solution.py:114
  149.9 1.9 %copy-start.3 = (bf16[2,128,4,256]{3,1,2,0:T(8,128)(2,1)S(1)}, bf16[2,128,4,256]{3,1,2,0:T(8,128)(2,1)}, u32[]{:S(2)}) copy-start(bf16[2,128,4,256]{3,1,2,0:T(8,128)(2,1)} %get-tuple-element.13) | copy-start | bytes 1572868
  152.1 1.9 %copy-start.2 = (bf16[2,128,4,256]{3,1,2,0:T(8,128)(2,1)S(1)}, bf16[2,128,4,256]{3,1,2,0:T(8,128)(2,1)}, u32[]{:S(2)}) copy-start(bf16[2,128,4,256]{3,1,2,0:T(8,128)(2,1)} %get-tuple-element.15) | copy-start | bytes 1572868
  154.3 1.9 %copy-start.1 = (bf16[2,128,4,256]{3,1,2,0:T(8,128)(2,1)S(1)}, bf16[2,128,4,256]{3,1,2,0:T(8,128)(2,1)}, u32[]{:S(2)}) copy-start(bf16[2,128,4,256]{3,1,2,0:T(8,128)(2,1)} %get-tuple-element.14) | copy-start | bytes 1572868
  156.4 1.9 %copy-start.4 = (bf16[8,128,256]{2,1,0:T(8,128)(2,1)S(1)}, bf16[8,128,256]{2,1,0:T(8,128)(2,1)}, u32[]{:S(2)}) copy-start(bf16[8,128,256]{2,1,0:T(8,128)(2,1)} %copy.230) | copy-start | bytes 1572868
  173.5 1.0 copy-start.9
  173.9 1.0 copy-start.10
  175.1 1.0 copy-start.7
  175.5 1.0 copy-start.8
  176.7 1.0 copy-start.5
  177.1 1.0 copy-start.6
where the time goes:
time: 181 us; the launch traced here: 180 us
  local copies, waits for them, and re-layouts  82.2 us (45%)
  waiting for transfers between devices  33.2 us (18%)
  other arithmetic  33.1 us (18%)
  matrix products  16 us (9%)
  starting transfers between devices  12.1 us (7%)
  between operations  3.09 us (2%)
    add x1, other arithmetic, on_device(): filtered + filter_taps[tap_index] * frames[:, :, tap_index:tap_index + sp...  23.6 us
    all_to_all x1, waiting for transfers between devices, on_device(): lax.all_to_all(spectra, 'chan', split_axis=3, concat_axis=1, tiled=True)  22.4 us
    unnamed x26, local copies, waits for them, and re-layouts  19.9 us
    all_to_all x1, local copies, waits for them, and re-layouts, on_device(): lax.all_to_all(spectra, 'chan', split_axis=3, concat_axis=1, tiled=True)  10.8 us
    all_to_all x1, waiting for transfers between devices, on_device(): lax.all_to_all(slots, 'inp', split_axis=0, concat_axis=0, tiled=True)  10.7 us
    convert_element_type x1, local copies, waits for them, and re-layouts, on_device(): spectra = transform(filtered).astype(jnp.bfloat16)  8.79 us
    all_to_all x1, starting transfers between devices, on_device(): lax.all_to_all(spectra, 'chan', split_axis=3, concat_axis=1, tiled=True)  7.41 us
    another operation x2, local copies, waits for them, and re-layouts, transform(): jnp.stack([real_last, imag_last])  7.23 us
  transfers between devices with their start and end apart: 2, of which 2 were waited for; matrix products, arithmetic and copies ran while one was open for 9% of the time, Pallas kernels for 0%

commit v1 on v0

v1 whole, which is shorter than its diff:
```python
import functools
import math

import jax
import jax.numpy as jnp
import numpy as np
from jax import lax
from jax.experimental import pallas as pl
from jax.experimental.pallas import tpu as pltpu
from jax.sharding import PartitionSpec as P

AVG = 64
LANES = 128
OUTER = 32
ROWS = 16
VMEM_LIMIT = 56 * 1024 * 1024


def twiddle_table():
    fine = OUTER * LANES
    k1 = np.arange(OUTER)[None, :, None]
    odd = np.arange(2)[:, None, None]
    q = np.arange(LANES)[None, None, :]
    turned = k1 + OUTER * ((-4 * k1 - 2 * odd) % LANES)
    angle = (turned * q % fine) * (2.0 * math.pi / fine)
    return np.stack([np.cos(angle), np.sin(angle)], axis=1).astype(np.float32)


def lane_matrix():
    fine = OUTER * LANES
    q = np.arange(LANES)
    angle = (q[:, None] * q[None, :] % LANES) * (2.0 * math.pi / LANES)
    cos, sin = np.cos(angle), np.sin(angle)
    full = (np.block([[cos, -sin], [sin, cos]]) * fine**-0.5).astype(np.float32)
    high = full.astype(jnp.bfloat16)
    low = (full - high.astype(np.float32)).astype(jnp.bfloat16)
    return np.stack([high, low])


def add(x, y):
    return (x[0] + y[0], x[1] + y[1])


def sub(x, y):
    return (x[0] - y[0], x[1] - y[1])


def minus_i(x):
    return (x[1], -x[0])


def turn(x, step, count):
    step %= count
    if step == 0:
        return x
    if 4 * step == count:
        return minus_i(x)
    if 8 * step == count:
        half = math.sqrt(0.5)
        return ((x[0] + x[1]) * half, (x[1] - x[0]) * half)
    if 8 * step == 3 * count:
        half = math.sqrt(0.5)
        return ((x[1] - x[0]) * half, (x[0] + x[1]) * -half)
    cos, sin = math.cos(2 * math.pi * step / count), math.sin(2 * math.pi * step / count)
    return (x[0] * cos + x[1] * sin, x[1] * cos - x[0] * sin)


def four(x):
    even, odd = add(x[0], x[2]), sub(x[0], x[2])
    other, last = add(x[1], x[3]), minus_i(sub(x[1], x[3]))
    return [add(even, other), add(odd, last), sub(even, other), sub(odd, last)]


def eight(x):
    even, odd = four(x[0::2]), four(x[1::2])
    odd = [turn(value, k, 8) for k, value in enumerate(odd)]
    return [add(e, o) for e, o in zip(even, odd)] + [sub(e, o) for e, o in zip(even, odd)]


def spectra_kernel(
    chan_count, spectra_count, volt_ref, taps_ref, twist_ref, matrix_ref, *refs
):
    outs = refs[:chan_count]
    filtered, first, last, pieces, sems = refs[chan_count:]
    tap_count, fine = taps_ref.shape
    frame_count = spectra_count + tap_count - 1

    def filter_column(p, carry):
        column = pl.multiple_of(p * LANES, LANES)
        taps = [taps_ref[pl.ds(t, 1), pl.ds(column, LANES)] for t in range(tap_count)]
        for part in range(2):
            sums = [None] * spectra_count
            for frame in range(frame_count):
                at = pl.multiple_of(frame * fine + column, LANES)
                values = volt_ref[part, :, pl.ds(at, LANES)].astype(jnp.float32)
                for s in range(spectra_count):
                    t = frame - s
                    if 0 <= t < tap_count:
                        term = taps[t] * values
                        sums[s] = term if sums[s] is None else sums[s] + term
            for s in range(spectra_count):
                filtered[s, part, p] = sums[s]
        return carry

    lax.fori_loop(0, OUTER, filter_column, 0)

    def transform(s, carry):
        for a in range(8):
            values = four([(filtered[s, 0, a + 8 * b], filtered[s, 1, a + 8 * b]) for b in range(4)])
            for r in range(4):
                real, imag = turn(values[r], a * r, OUTER)
                first[0, r, a] = real
                first[1, r, a] = imag
        odd = lax.rem(s, 2)
        for r in range(4):
            values = eight([(first[0, r, a], first[1, r, a]) for a in range(8)])
            highs, lows = [], []
            for t in range(8):
                k1 = r + 4 * t
                cos = twist_ref[odd, 0, pl.ds(k1, 1), :]
                sin = twist_ref[odd, 1, pl.ds(k1, 1), :]
                real, imag = values[t]
                row = jnp.concatenate([real * cos + imag * sin, imag * cos - real * sin], axis=1)
                high = row.astype(jnp.bfloat16)
                highs.append(high)
                lows.append((row - high.astype(jnp.float32)).astype(jnp.bfloat16))
            high = jnp.concatenate(highs, axis=0)
            low = jnp.concatenate(lows, axis=0)
            dot = functools.partial(jnp.dot, preferred_element_type=jnp.float32)
            result = dot(high, matrix_ref[0]) + (dot(low, matrix_ref[0]) + dot(high, matrix_ref[1]))
            result = result.astype(jnp.bfloat16)
            for t in range(8):
                rows = result[t * ROWS : (t + 1) * ROWS]
                last[s, 0, r + 4 * t] = rows[:, :LANES]
                last[s, 1, r + 4 * t] = rows[:, LANES:]
        return carry

    lax.fori_loop(0, spectra_count, transform, 0)

    lane = lax.broadcasted_iota(jnp.int32, (ROWS, LANES), 1)
    bits = [(lane >> bit) & 1 == 1 for bit in range(7)]
    group_count = pieces.shape[1]

    def regroup(part, carry):
        for pair in range(spectra_count // 2):
            even = [last[2 * pair, part, k1] for k1 in range(OUTER)]
            odd = [last[2 * pair + 1, part, k1] for k1 in range(OUTER)]
            mixed = [
                [jnp.where(bits[1], odd[v], even[v]) for v in range(OUTER)],
                [jnp.where(bits[1], even[v], odd[v - 1]) for v in range(OUTER)],
            ]
            for which in range(2):
                tiles = [mixed[which][-v % OUTER] for v in range(OUTER)]
                for bit in range(5):
                    tiles = [
                        jnp.where(bits[2 + bit], tiles[v - (1 << bit)], tiles[v])
                        for v in range(OUTER)
                    ]
                for u in range(OUTER):
                    chan, group = divmod(2 * u + which, group_count)
                    pieces[chan, group, part * (spectra_count // 2) + pair] = tiles[u]
        return carry

    lax.fori_loop(0, 2, regroup, 0)
    own = lax.axis_index("chan")
    copies = [
        pltpu.make_async_copy(pieces.at[jnp.bitwise_xor(own, k)], outs[k], sems.at[k])
        for k in range(chan_count)
    ]
    for copy in copies:
        copy.start()
    for copy in copies:
        copy.wait()


def spectra_pieces(voltages, filter_taps, chan_count):
    tap_count, fine = filter_taps.shape
    signals = voltages.shape[1]
    spectra_count = voltages.shape[2] // fine - tap_count + 1
    padded = -signals % ROWS
    if padded:
        voltages = jnp.pad(voltages, ((0, 0), (0, padded), (0, 0)))
    group_count = fine // AVG // chan_count
    slices = spectra_count
    piece = (group_count, slices, ROWS, LANES)
    outs = pl.pallas_call(
        functools.partial(spectra_kernel, chan_count, spectra_count),
        out_shape=[jax.ShapeDtypeStruct(piece, jnp.bfloat16)] * chan_count,
        in_specs=[pl.BlockSpec(memory_space=pltpu.VMEM)] * 4,
        out_specs=[pl.BlockSpec(memory_space=pl.ANY)] * chan_count,
        scratch_shapes=[
            pltpu.VMEM((spectra_count, 2, OUTER, ROWS, LANES), jnp.float32),
            pltpu.VMEM((2, 4, 8, ROWS, LANES), jnp.float32),
            pltpu.VMEM((spectra_count, 2, OUTER, ROWS, LANES), jnp.bfloat16),
            pltpu.VMEM((chan_count,) + piece, jnp.bfloat16),
            pltpu.SemaphoreType.DMA((chan_count,)),
        ],
        compiler_params=pltpu.CompilerParams(vmem_limit_bytes=VMEM_LIMIT),
        name="spectra",
    )(voltages, filter_taps, jnp.asarray(twiddle_table()), jnp.asarray(lane_matrix()))
    return [out[:, :, :signals] for out in outs]


def products(left, right):
    slices = left.shape[0]
    real_first = [left[i] for i in range(slices)]
    turned = real_first[slices // 2 :] + [-value for value in real_first[: slices // 2]]
    other = jnp.concatenate([right[i] for i in range(slices)], axis=1)
    contract = (((1,), (1,)), ((), ()))
    scale = 2.0 / (slices * LANES)
    results = []
    for side in (real_first, turned):
        rows = jnp.concatenate(side, axis=1)
        results.append(
            lax.dot_general(rows, other, contract, preferred_element_type=jnp.float32) * scale
        )
    return results


def autos_kernel(chan_count, inp_count, *refs):
    pieces = refs[:chan_count]
    block, autos, lower, upper = refs[chan_count:]
    own = lax.axis_index("chan")
    for k, piece in enumerate(pieces):
        source = jnp.bitwise_xor(own, k)
        rows = piece.shape[2]
        if rows == block.shape[2]:
            block[...] = piece[...]
        else:
            block[:, :, pl.ds(pl.multiple_of(source * rows, rows), rows), :] = piece[...]
    group_count = block.shape[0]
    half = group_count // 2
    lower[...] = block[:half]
    upper[...] = block[half:]

    def correlate(group, carry):
        rows = block[group]
        autos[0, group], autos[1, group] = products(rows, rows)
        return carry

    lax.fori_loop(0, group_count, correlate, 0)


def cross_kernel(order_ref, upper_ref, block, *refs):
    received = refs[:-1]
    visibilities = refs[-1]
    half = block.shape[0] // 2

    def correlate(group, carry):
        for index, other in enumerate(received):
            rows = block[upper_ref[index] * half + group]
            real, imag = products(rows, other[group])
            visibilities[0, order_ref[index], group] = real
            visibilities[1, order_ref[index], group] = imag
        return carry

    lax.fori_loop(0, half, correlate, 0)


def on_device(voltages, filter_taps, pairing):
    chan_count = lax.axis_size("chan")
    inp_count = lax.axis_size("inp")
    own_block = lax.axis_index("inp")

    def exchange(value, axis, mask):
        count = lax.axis_size(axis)
        return lax.ppermute(value, axis, [(i, i ^ mask) for i in range(count)])

    pieces = spectra_pieces(voltages, filter_taps, chan_count)
    pieces = [
        piece if k == 0 else exchange(piece, "chan", k) for k, piece in enumerate(pieces)
    ]
    group_count, slices, signals, _ = pieces[0].shape
    rows = signals * chan_count
    if signals % ROWS:
        order = jnp.bitwise_xor(lax.axis_index("chan"), jnp.arange(chan_count))
        whole = jnp.take(jnp.stack(pieces), order, axis=0)
        pieces = [whole.transpose(1, 2, 0, 3, 4).reshape(group_count, slices, rows, LANES)]
    half = group_count // 2
    block, autos, lower, upper = pl.pallas_call(
        functools.partial(autos_kernel, len(pieces), inp_count),
        out_shape=[
            jax.ShapeDtypeStruct((group_count, slices, rows, LANES), jnp.bfloat16),
            jax.ShapeDtypeStruct((2, group_count, rows, rows), jnp.float32),
            jax.ShapeDtypeStruct((half, slices, rows, LANES), jnp.bfloat16),
            jax.ShapeDtypeStruct((half, slices, rows, LANES), jnp.bfloat16),
        ],
        in_specs=[pl.BlockSpec(memory_space=pltpu.VMEM)] * len(pieces),
        out_specs=[pl.BlockSpec(memory_space=pltpu.VMEM)] * 4,
        compiler_params=pltpu.CompilerParams(vmem_limit_bytes=VMEM_LIMIT),
        name="autos",
    )(*pieces)
    masks = list(range(1, inp_count))
    is_upper = [(own_block >> (mask.bit_length() - 1)) & 1 for mask in masks]
    received = {}
    for mask, up in zip(masks, is_upper):
        if mask == 1 or mask % 2 == 0:
            received[mask] = exchange(jnp.where(up == 1, lower, upper), "inp", mask)
        else:
            received[mask] = exchange(received[mask - 1], "inp", 1)
    order = jnp.argmax(pairing[None, :] == jnp.array(masks, jnp.int32)[:, None], axis=1)
    visibilities = pl.pallas_call(
        cross_kernel,
        out_shape=jax.ShapeDtypeStruct((2, len(masks), half, rows, rows), jnp.float32),
        in_specs=[pl.BlockSpec(memory_space=pltpu.SMEM)] * 2
        + [pl.BlockSpec(memory_space=pltpu.VMEM)] * (1 + len(masks)),
        out_specs=pl.BlockSpec(memory_space=pltpu.VMEM),
        compiler_params=pltpu.CompilerParams(vmem_limit_bytes=VMEM_LIMIT),
        name="cross",
    )(
        order.astype(jnp.int32),
        jnp.stack(is_upper).astype(jnp.int32),
        block,
        *[received[mask] for mask in masks],
    )
    return (visibilities, autos)


def solution(mesh):
    in_specs = (P(None, ("inp", "chan"), None), P(), P())
    out_specs = (P(None, None, "chan", "inp", None), P(None, "chan", "inp", None))
    return jax.shard_map(
        on_device, mesh=mesh, in_specs=in_specs, out_specs=out_specs, check_vma=False
    )
```

time: 181 us -> 66.2 us (0.37)
  the two profiles are of different devices: /device:TPU:0 before, /device:TPU:17 now
where the time goes in v1:
time: 66.2 us; the launch traced here: 66 us
  waiting for transfers between devices  29.9 us (45%)
  Pallas kernels  18 us (27%)
  starting transfers between devices  13.4 us (20%)
  other arithmetic  2.56 us (4%)
  local copies, waits for them, and re-layouts  1.45 us (2%)
  between operations  0.71 us (1%)
    ppermute x10, waiting for transfers between devices, exchange(): return lax.ppermute(value, axis, [(i, i ^ mask) for i in range(count)])  29.9 us
    ppermute x10, starting transfers between devices, exchange(): return lax.ppermute(value, axis, [(i, i ^ mask) for i in range(count)])  13.4 us
    pallas_call x1, Pallas kernels, spectra_pieces(): pl.pallas_call(functools.partial(spectra_kernel, chan_count, spectra_coun...  8.88 us
    pallas_call x1, Pallas kernels, on_device(): pl.pallas_call(functools.partial(autos_kernel, len(pieces), inp_count), o...  4.79 us
    pallas_call x1, Pallas kernels, on_device(): pl.pallas_call(cross_kernel, out_shape=jax.ShapeDtypeStruct((2, len(masks...  4.31 us
    unnamed x24, local copies, waits for them, and re-layouts  1.45 us
  transfers between devices with their start and end apart: 10, of which 7 were waited for; matrix products, arithmetic and copies ran while one was open for 2% of the time, Pallas kernels for 0%

profile of v1, /device:TPU:17, one launch (start us, length us, event | category | flops | bytes accessed | tf_op | source)
XLA Modules:
  0.0 66.0 jit_solution(12451767336015727239)
XLA Ops:
  0.6 0.0 copy-start.11
  0.6 0.0 copy-start.10
  0.7 8.9 %spectra.1 = (bf16[8,4,16,128]{3,2,1,0:T(8,128)(2,1)}, bf16[8,4,16,128]{3,2,1,0:T(8,128)(2,1)}, bf16[8,4,16,128]{3,2,1,0:T(8,128)(2,1)}, bf16[8,4,16,128]{3,2,1,...) custom-call(bf16[2,16,77824]{2,1,0:T(8,128)(2,1)} %volt_ref.1, ...), custom_call_target="tpu_custom_call" | custom-call | tf_op jit(solution)/shard_map/spectra/pallas_call | solution.py:186
  9.5 1.3 %collective-permute-start = (bf16[8,4,16,128]{3,2,1,0:T(8,128)(2,1)}, bf16[8,4,16,128]{3,2,1,0:T(8,128)(2,1)S(1)}, u32[]{:S(2)}, u32[]{:S(2)}) collective-permute-start(bf16[8,4,16,128]{3,2,1,0:T(8,128)(2,1)} %get-tuple-element.17), channel_id=1, source_target_pairs={{0,1},{1,0},{2,3},{3,2},{4,5},{5,4},{6,7},{7,6},{8,9},{9,8},{10,11... | collective-permute-start | bytes 393224 | tf_op jit(solution)/shard_map/ppermute | solution.py:267
  10.8 1.3 %collective-permute-start.1 = (bf16[8,4,16,128]{3,2,1,0:T(8,128)(2,1)}, bf16[8,4,16,128]{3,2,1,0:T(8,128)(2,1)S(1)}, u32[]{:S(2)}, u32[]{:S(2)}) collective-permute-start(bf16[8,4,16,128]{3,2,1,0:T(8,128)(2,1)} %get-tuple-element.18), channel_id=1, source_target_pairs={{0,2},{1,3},{2,0},{3,1},{4,6},{5,7},{6,4},{7,5},{8,10},{9,11},{10,... | collective-permute-start | bytes 393224 | tf_op jit(solution)/shard_map/ppermute | solution.py:267
  12.1 0.1 collective-permute-start.2
  12.3 0.0 collective-permute-start.3
  12.3 3.3 %collective-permute-start.4 = (bf16[8,4,16,128]{3,2,1,0:T(8,128)(2,1)}, bf16[8,4,16,128]{3,2,1,0:T(8,128)(2,1)S(1)}, u32[]{:S(2)}, u32[]{:S(2)}) collective-permute-start(bf16[8,4,16,128]{3,2,1,0:T(8,128)(2,1)} %get-tuple-element.21), channel_id=1, source_target_pairs={{0,5},{1,4},{2,7},{3,6},{4,1},{5,0},{6,3},{7,2},{8,13},{9,12},{10,... | collective-permute-start | bytes 393224 | tf_op jit(solution)/shard_map/ppermute | solution.py:267
  15.6 0.0 collective-permute-done.refs_1_
  15.6 0.0 copy-start.3
  15.6 0.2 collective-permute-start.5
  15.8 0.0 collective-permute-done.1.refs_2_
  15.8 0.0 copy-start.4
  15.8 1.2 %collective-permute-start.6 = (bf16[8,4,16,128]{3,2,1,0:T(8,128)(2,1)}, bf16[8,4,16,128]{3,2,1,0:T(8,128)(2,1)S(1)}, u32[]{:S(2)}, u32[]{:S(2)}) collective-permute-start(bf16[8,4,16,128]{3,2,1,0:T(8,128)(2,1)} %get-tuple-element.23), channel_id=1, source_target_pairs={{0,7},{1,6},{2,5},{3,4},{4,3},{5,2},{6,1},{7,0},{8,15},{9,14},{10,... | collective-permute-start | bytes 393224 | tf_op jit(solution)/shard_map/ppermute | solution.py:267
  17.0 3.0 %collective-permute-done.2.refs_3_ = bf16[8,4,16,128]{3,2,1,0:T(8,128)(2,1)S(1)} collective-permute-done((bf16[8,4,16,128]{3,2,1,0:T(8,128)(2,1)}, bf16[8,4,16,128]{3,2,1,0:T(8,128)(2,1)S(1)}, u32[]{:S(2)}, u32[]{:S(2)}) %collective-permute-start.2) | collective-permute-done | bytes 131104 | tf_op jit(solution)/shard_map/ppermute | solution.py:267
  20.0 0.0 copy-start.5
  20.0 0.5 collective-permute-done.3.refs_4_
  20.5 0.0 copy-start.6
  20.5 2.6 %collective-permute-done.4.refs_5_ = bf16[8,4,16,128]{3,2,1,0:T(8,128)(2,1)S(1)} collective-permute-done((bf16[8,4,16,128]{3,2,1,0:T(8,128)(2,1)}, bf16[8,4,16,128]{3,2,1,0:T(8,128)(2,1)S(1)}, u32[]{:S(2)}, u32[]{:S(2)}) %collective-permute-start.4) | collective-permute-done | bytes 131104 | tf_op jit(solution)/shard_map/ppermute | solution.py:267
  23.2 0.0 copy-start.7
  23.2 10.6 %collective-permute-done.5.refs_6_ = bf16[8,4,16,128]{3,2,1,0:T(8,128)(2,1)S(1)} collective-permute-done((bf16[8,4,16,128]{3,2,1,0:T(8,128)(2,1)}, bf16[8,4,16,128]{3,2,1,0:T(8,128)(2,1)S(1)}, u32[]{:S(2)}, u32[]{:S(2)}) %collective-permute-start.5) | collective-permute-done | bytes 131104 | tf_op jit(solution)/shard_map/ppermute | solution.py:267
  33.8 0.0 copy-start.8
  33.8 4.5 %collective-permute-done.6.refs_7_ = bf16[8,4,16,128]{3,2,1,0:T(8,128)(2,1)S(1)} collective-permute-done((bf16[8,4,16,128]{3,2,1,0:T(8,128)(2,1)}, bf16[8,4,16,128]{3,2,1,0:T(8,128)(2,1)S(1)}, u32[]{:S(2)}, u32[]{:S(2)}) %collective-permute-start.6) | collective-permute-done | bytes 131104 | tf_op jit(solution)/shard_map/ppermute | solution.py:267
  38.3 0.0 copy-start.9
  38.3 0.0 copy-done.3
  38.3 0.0 copy-done.4
  38.3 0.0 copy-done.5
  38.3 0.0 copy-done.6
  38.3 0.0 copy-done.7
  38.3 0.0 copy-done.8
  38.3 0.6 copy-done.9
  38.9 4.8 %autos.1 = (bf16[8,4,128,128]{3,2,1,0:T(8,128)(2,1)}, f32[2,8,128,128]{3,2,1,0:T(8,128)}, bf16[4,4,128,128]{3,2,1,0:T(8,128)(2,1)}, bf16[4,4,128,128]{3,2,1,0:T(8,128)(2,1)}) custom-call(bf16[8,4,16,128]{3,2,1,0:T(8,128)(2,1)} %get-tuple-element.16.refs_0_, bf16[8,4,16,128]{3,2,1,0:T(8,128)(2,1)} %copy-done.3, bf16[8,4,16,128]{3,2,1,0:T(8,128)(2,1)} %copy-done.4, ...), custom_call_target="tpu_custom_call" | custom-call | tf_op jit(solution)/shard_map/autos/pallas_call | solution.py:280
  43.7 1.3 %broadcast_select_fusion = (bf16[4,4,128,128]{3,2,1,0:T(8,128)(2,1)S(1)}, bf16[4,4,128,128]{3,2,1,0:T(8,128)(2,1)S(1)}) fusion(bf16[4,4,128,128]{3,2,1,0:T(8,128)(2,1)} %get-tuple-element.25, bf16[4,4,128,128]{3,2,1,0:T(8,128)(2,1)} %get-tuple-element.26, pred[]{:T(512)S(6)} %eq.25, pred[]{:T(512)S(6)} %eq.24), kind=kLoop, calls=%fused_computation | loop fusion | flops 524288 | bytes 2097154 | tf_op jit(solution)/shard_map/jit(_where)/select_n | solution.py:298
  45.0 1.3 %collective-permute-start.8 = (bf16[4,4,128,128]{3,2,1,0:T(8,128)(2,1)S(1)}, bf16[4,4,128,128]{3,2,1,0:T(8,128)(2,1)S(1)}, u32[]{:S(2)}, u32[]{:S(2)}) collective-permute-start(bf16[4,4,128,128]{3,2,1,0:T(8,128)(2,1)S(1)} %get-tuple-element.28), channel_id=1, source_target_pairs={{0,16},{8,24},{16,0},{24,8},{1,17},{9,25},{17,1},{25,9},{2,18},{10... | collective-permute-start | bytes 1572872 | tf_op jit(solution)/shard_map/ppermute | solution.py:267
  46.3 2.0 %collective-permute-start.7 = (bf16[4,4,128,128]{3,2,1,0:T(8,128)(2,1)S(1)}, bf16[4,4,128,128]{3,2,1,0:T(8,128)(2,1)S(1)}, u32[]{:S(2)}, u32[]{:S(2)}) collective-permute-start(bf16[4,4,128,128]{3,2,1,0:T(8,128)(2,1)S(1)} %get-tuple-element.29), channel_id=1, source_target_pairs={{0,8},{8,0},{16,24},{24,16},{1,9},{9,1},{17,25},{25,17},{2,10},{10... | collective-permute-start | bytes 1572872 | tf_op jit(solution)/shard_map/ppermute | solution.py:267
  48.3 8.4 %collective-permute-done.8.refs_1_ = bf16[4,4,128,128]{3,2,1,0:T(8,128)(2,1)S(1)} collective-permute-done((bf16[4,4,128,128]{3,2,1,0:T(8,128)(2,1)S(1)}, bf16[4,4,128,128]{3,2,1,0:T(8,128)(2,1)S(1)}, u32[]{:S(2)}, u32[]{:S(2)}) %collective-permute-start.8) | collective-permute-done | bytes 524320 | tf_op jit(solution)/shard_map/ppermute | solution.py:267
  56.7 0.0 copy-start
  56.7 2.7 %collective-permute-start.9 = (bf16[4,4,128,128]{3,2,1,0:T(8,128)(2,1)S(1)}, bf16[4,4,128,128]{3,2,1,0:T(8,128)(2,1)S(1)}, u32[]{:S(2)}, u32[]{:S(2)}) collective-permute-start(bf16[4,4,128,128]{3,2,1,0:T(8,128)(2,1)S(1)} %collective-permute-done.8.refs_1_), channel_id=1, source_target_pairs={{0,8},{8,0},{16,24},{24,16},{1,9},{9,1},{17,25},{25,17},{2,10},{10... | collective-permute-start | bytes 1572872 | tf_op jit(solution)/shard_map/ppermute | solution.py:267
  59.4 0.6 pad_add_fusion.upper_ref
  60.0 0.0 copy-done.11
  60.0 0.0 copy-done.10
  60.0 0.7 %iota_reduce_fusion = (pred[3]{0:T(512)(128)(4,1)}, s32[3]{0:T(128)}) fusion(s32[3]{0:T(128)S(1)} %copy-done.10, s32[3]{0:T(128)S(1)} %copy-done.11), kind=kLoop, calls=%fused_computation.2 | loop fusion | flops 51 | bytes 39 | tf_op jit(solution)/shard_map/on_device/reduce | solution.py:301
  60.7 0.0 collective-permute-done.7.refs_0_
  60.7 0.0 copy-start.1
  60.7 0.2 collective-permute-done.9.refs_2_
  60.9 0.0 copy-start.2
  60.9 0.0 copy-done
  60.9 0.6 copy-done.1
  61.5 0.2 copy-done.2
  61.7 4.3 %cross.1 = f32[2,3,4,128,128]{4,3,2,1,0:T(8,128)} custom-call(s32[3]{0:T(128)} %get-tuple-element.15.order_ref, s32[3]{0:T(128)} %pad_add_fusion.upper_ref, bf16[8,4,128,128]{3,2,1,0:T(8,128)(2,1)} %get-tuple-element.24.block, bf16[4,4,128,128]{3,2,1,0:T(8,128)(2,1)} %copy-done.1, bf16[4,4,128,128]{3,2,1,0:T(8,128)(2,1)} %copy-done, ...), custom_call_target="tpu_custom_call" | custom-call | tf_op jit(solution)/shard_map/cross/pallas_call | solution.py:302
Async XLA Ops:
  0.6 59.3 %copy-start.11 = (s32[3]{0:T(128)S(1)}, s32[3]{0:T(128)}, u32[]{:S(2)}) copy-start(s32[3]{0:T(128)} %constant.22.clone) | copy-start | bytes 40
  0.6 59.3 %copy-start.10 = (s32[3]{0:T(128)S(1)}, s32[3]{0:T(128)}, u32[]{:S(2)}) copy-start(s32[3]{0:T(128)} %param.8) | copy-start | bytes 40
  9.5 6.0 %collective-permute-start = (bf16[8,4,16,128]{3,2,1,0:T(8,128)(2,1)}, bf16[8,4,16,128]{3,2,1,0:T(8,128)(2,1)S(1)}, u32[]{:S(2)}, u32[]{:S(2)}) collective-permute-start(bf16[8,4,16,128]{3,2,1,0:T(8,128)(2,1)} %get-tuple-element.17), channel_id=1, source_target_pairs={{0,1},{1,0},{2,3},{3,2},{4,5},{5,4},{6,7},{7,6},{8,9},{9,8},{10,11... | collective-permute-start | bytes 393224 | tf_op jit(solution)/shard_map/ppermute | solution.py:267
  10.8 4.9 %collective-permute-start.1 = (bf16[8,4,16,128]{3,2,1,0:T(8,128)(2,1)}, bf16[8,4,16,128]{3,2,1,0:T(8,128)(2,1)S(1)}, u32[]{:S(2)}, u32[]{:S(2)}) collective-permute-start(bf16[8,4,16,128]{3,2,1,0:T(8,128)(2,1)} %get-tuple-element.18), channel_id=1, source_target_pairs={{0,2},{1,3},{2,0},{3,1},{4,6},{5,7},{6,4},{7,5},{8,10},{9,11},{10,... | collective-permute-start | bytes 393224 | tf_op jit(solution)/shard_map/ppermute | solution.py:267
  12.1 7.8 %collective-permute-start.2 = (bf16[8,4,16,128]{3,2,1,0:T(8,128)(2,1)}, bf16[8,4,16,128]{3,2,1,0:T(8,128)(2,1)S(1)}, u32[]{:S(2)}, u32[]{:S(2)}) collective-permute-start(bf16[8,4,16,128]{3,2,1,0:T(8,128)(2,1)} %get-tuple-element.19), channel_id=1, source_target_pairs={{0,3},{1,2},{2,1},{3,0},{4,7},{5,6},{6,5},{7,4},{8,11},{9,10},{10,... | collective-permute-start | bytes 393224 | tf_op jit(solution)/shard_map/ppermute | solution.py:267
  12.3 8.3 %collective-permute-start.3 = (bf16[8,4,16,128]{3,2,1,0:T(8,128)(2,1)}, bf16[8,4,16,128]{3,2,1,0:T(8,128)(2,1)S(1)}, u32[]{:S(2)}, u32[]{:S(2)}) collective-permute-start(bf16[8,4,16,128]{3,2,1,0:T(8,128)(2,1)} %get-tuple-element.20), channel_id=1, source_target_pairs={{0,4},{1,5},{2,6},{3,7},{4,0},{5,1},{6,2},{7,3},{8,12},{9,13},{10,... | collective-permute-start | bytes 393224 | tf_op jit(solution)/shard_map/ppermute | solution.py:267
  12.3 10.9 %collective-permute-start.4 = (bf16[8,4,16,128]{3,2,1,0:T(8,128)(2,1)}, bf16[8,4,16,128]{3,2,1,0:T(8,128)(2,1)S(1)}, u32[]{:S(2)}, u32[]{:S(2)}) collective-permute-start(bf16[8,4,16,128]{3,2,1,0:T(8,128)(2,1)} %get-tuple-element.21), channel_id=1, source_target_pairs={{0,5},{1,4},{2,7},{3,6},{4,1},{5,0},{6,3},{7,2},{8,13},{9,12},{10,... | collective-permute-start | bytes 393224 | tf_op jit(solution)/shard_map/ppermute | solution.py:267
  15.6 22.7 %copy-start.3 = (bf16[8,4,16,128]{3,2,1,0:T(8,128)(2,1)}, bf16[8,4,16,128]{3,2,1,0:T(8,128)(2,1)S(1)}, u32[]{:S(2)}) copy-start(bf16[8,4,16,128]{3,2,1,0:T(8,128)(2,1)S(1)} %collective-permute-done.refs_1_) | copy-start | bytes 393220
  15.6 18.2 %collective-permute-start.5 = (bf16[8,4,16,128]{3,2,1,0:T(8,128)(2,1)}, bf16[8,4,16,128]{3,2,1,0:T(8,128)(2,1)S(1)}, u32[]{:S(2)}, u32[]{:S(2)}) collective-permute-start(bf16[8,4,16,128]{3,2,1,0:T(8,128)(2,1)} %get-tuple-element.22), channel_id=1, source_target_pairs={{0,6},{1,7},{2,4},{3,5},{4,2},{5,3},{6,0},{7,1},{8,14},{9,15},{10,... | collective-permute-start | bytes 393224 | tf_op jit(solution)/shard_map/ppermute | solution.py:267
  15.8 22.5 %copy-start.4 = (bf16[8,4,16,128]{3,2,1,0:T(8,128)(2,1)}, bf16[8,4,16,128]{3,2,1,0:T(8,128)(2,1)S(1)}, u32[]{:S(2)}) copy-start(bf16[8,4,16,128]{3,2,1,0:T(8,128)(2,1)S(1)} %collective-permute-done.1.refs_2_) | copy-start | bytes 393220
  15.8 22.5 %collective-permute-start.6 = (bf16[8,4,16,128]{3,2,1,0:T(8,128)(2,1)}, bf16[8,4,16,128]{3,2,1,0:T(8,128)(2,1)S(1)}, u32[]{:S(2)}, u32[]{:S(2)}) collective-permute-start(bf16[8,4,16,128]{3,2,1,0:T(8,128)(2,1)} %get-tuple-element.23), channel_id=1, source_target_pairs={{0,7},{1,6},{2,5},{3,4},{4,3},{5,2},{6,1},{7,0},{8,15},{9,14},{10,... | collective-permute-start | bytes 393224 | tf_op jit(solution)/shard_map/ppermute | solution.py:267
  20.0 18.3 %copy-start.5 = (bf16[8,4,16,128]{3,2,1,0:T(8,128)(2,1)}, bf16[8,4,16,128]{3,2,1,0:T(8,128)(2,1)S(1)}, u32[]{:S(2)}) copy-start(bf16[8,4,16,128]{3,2,1,0:T(8,128)(2,1)S(1)} %collective-permute-done.2.refs_3_) | copy-start | bytes 393220
  20.5 17.7 %copy-start.6 = (bf16[8,4,16,128]{3,2,1,0:T(8,128)(2,1)}, bf16[8,4,16,128]{3,2,1,0:T(8,128)(2,1)S(1)}, u32[]{:S(2)}) copy-start(bf16[8,4,16,128]{3,2,1,0:T(8,128)(2,1)S(1)} %collective-permute-done.3.refs_4_) | copy-start | bytes 393220
  23.2 15.1 %copy-start.7 = (bf16[8,4,16,128]{3,2,1,0:T(8,128)(2,1)}, bf16[8,4,16,128]{3,2,1,0:T(8,128)(2,1)S(1)}, u32[]{:S(2)}) copy-start(bf16[8,4,16,128]{3,2,1,0:T(8,128)(2,1)S(1)} %collective-permute-done.4.refs_5_) | copy-start | bytes 393220
  33.8 4.5 %copy-start.8 = (bf16[8,4,16,128]{3,2,1,0:T(8,128)(2,1)}, bf16[8,4,16,128]{3,2,1,0:T(8,128)(2,1)S(1)}, u32[]{:S(2)}) copy-start(bf16[8,4,16,128]{3,2,1,0:T(8,128)(2,1)S(1)} %collective-permute-done.5.refs_6_) | copy-start | bytes 393220
  38.3 0.7 %copy-start.9 = (bf16[8,4,16,128]{3,2,1,0:T(8,128)(2,1)}, bf16[8,4,16,128]{3,2,1,0:T(8,128)(2,1)S(1)}, u32[]{:S(2)}) copy-start(bf16[8,4,16,128]{3,2,1,0:T(8,128)(2,1)S(1)} %collective-permute-done.6.refs_7_) | copy-start | bytes 393220
  45.0 11.7 %collective-permute-start.8 = (bf16[4,4,128,128]{3,2,1,0:T(8,128)(2,1)S(1)}, bf16[4,4,128,128]{3,2,1,0:T(8,128)(2,1)S(1)}, u32[]{:S(2)}, u32[]{:S(2)}) collective-permute-start(bf16[4,4,128,128]{3,2,1,0:T(8,128)(2,1)S(1)} %get-tuple-element.28), channel_id=1, source_target_pairs={{0,16},{8,24},{16,0},{24,8},{1,17},{9,25},{17,1},{25,9},{2,18},{10... | collective-permute-start | bytes 1572872 | tf_op jit(solution)/shard_map/ppermute | solution.py:267
  46.3 14.4 %collective-permute-start.7 = (bf16[4,4,128,128]{3,2,1,0:T(8,128)(2,1)S(1)}, bf16[4,4,128,128]{3,2,1,0:T(8,128)(2,1)S(1)}, u32[]{:S(2)}, u32[]{:S(2)}) collective-permute-start(bf16[4,4,128,128]{3,2,1,0:T(8,128)(2,1)S(1)} %get-tuple-element.29), channel_id=1, source_target_pairs={{0,8},{8,0},{16,24},{24,16},{1,9},{9,1},{17,25},{25,17},{2,10},{10... | collective-permute-start | bytes 1572872 | tf_op jit(solution)/shard_map/ppermute | solution.py:267
  56.7 4.2 %copy-start = (bf16[4,4,128,128]{3,2,1,0:T(8,128)(2,1)}, bf16[4,4,128,128]{3,2,1,0:T(8,128)(2,1)S(1)}, u32[]{:S(2)}) copy-start(bf16[4,4,128,128]{3,2,1,0:T(8,128)(2,1)S(1)} %collective-permute-done.8.refs_1_) | copy-start | bytes 1572868
  56.7 4.2 %collective-permute-start.9 = (bf16[4,4,128,128]{3,2,1,0:T(8,128)(2,1)S(1)}, bf16[4,4,128,128]{3,2,1,0:T(8,128)(2,1)S(1)}, u32[]{:S(2)}, u32[]{:S(2)}) collective-permute-start(bf16[4,4,128,128]{3,2,1,0:T(8,128)(2,1)S(1)} %collective-permute-done.8.refs_1_), channel_id=1, source_target_pairs={{0,8},{8,0},{16,24},{24,16},{1,9},{9,1},{17,25},{25,17},{2,10},{10... | collective-permute-start | bytes 1572872 | tf_op jit(solution)/shard_map/ppermute | solution.py:267
  60.7 0.8 %copy-start.1 = (bf16[4,4,128,128]{3,2,1,0:T(8,128)(2,1)}, bf16[4,4,128,128]{3,2,1,0:T(8,128)(2,1)S(1)}, u32[]{:S(2)}) copy-start(bf16[4,4,128,128]{3,2,1,0:T(8,128)(2,1)S(1)} %collective-permute-done.7.refs_0_) | copy-start | bytes 1572868
  60.9 0.8 %copy-start.2 = (bf16[4,4,128,128]{3,2,1,0:T(8,128)(2,1)}, bf16[4,4,128,128]{3,2,1,0:T(8,128)(2,1)S(1)}, u32[]{:S(2)}) copy-start(bf16[4,4,128,128]{3,2,1,0:T(8,128)(2,1)S(1)} %collective-permute-done.9.refs_2_) | copy-start | bytes 1572868

commit v2 on v1

v2 whole, which is shorter than its diff:
```python
import functools
import math

import jax
import jax.numpy as jnp
import numpy as np
from jax import lax
from jax.experimental import pallas as pl
from jax.experimental.pallas import tpu as pltpu
from jax.sharding import PartitionSpec as P

AVG = 64
LANES = 128
OUTER = 32
ROWS = 16
MIB = 1024 * 1024


def twiddle_table():
    fine = OUTER * LANES
    k1 = np.arange(OUTER)[None, :, None]
    odd = np.arange(2)[:, None, None]
    q = np.arange(LANES)[None, None, :]
    turned = k1 + OUTER * ((-4 * k1 - 2 * odd) % LANES)
    angle = (turned * q % fine) * (2.0 * math.pi / fine)
    return np.concatenate([np.cos(angle), np.sin(angle)], axis=2).astype(np.float32)


def lane_matrix():
    fine = OUTER * LANES
    q = np.arange(LANES)
    angle = (q[:, None] * q[None, :] % LANES) * (2.0 * math.pi / LANES)
    cos, sin = np.cos(angle), np.sin(angle)
    return (np.block([[cos, -sin], [sin, cos]]) * fine**-0.5).astype(np.float32)


def add(x, y):
    return (x[0] + y[0], x[1] + y[1])


def sub(x, y):
    return (x[0] - y[0], x[1] - y[1])


def minus_i(x):
    return (x[1], -x[0])


def turn(x, step, count):
    step %= count
    if step == 0:
        return x
    if 4 * step == count:
        return minus_i(x)
    if 8 * step == count:
        half = math.sqrt(0.5)
        return ((x[0] + x[1]) * half, (x[1] - x[0]) * half)
    if 8 * step == 3 * count:
        half = math.sqrt(0.5)
        return ((x[1] - x[0]) * half, (x[0] + x[1]) * -half)
    cos, sin = math.cos(2 * math.pi * step / count), math.sin(2 * math.pi * step / count)
    return (x[0] * cos + x[1] * sin, x[1] * cos - x[0] * sin)


def four(x):
    even, odd = add(x[0], x[2]), sub(x[0], x[2])
    other, last = add(x[1], x[3]), minus_i(sub(x[1], x[3]))
    return [add(even, other), add(odd, last), sub(even, other), sub(odd, last)]


def eight(x):
    even, odd = four(x[0::2]), four(x[1::2])
    odd = [turn(value, k, 8) for k, value in enumerate(odd)]
    return [add(e, o) for e, o in zip(even, odd)] + [sub(e, o) for e, o in zip(even, odd)]


def bit_of(value, bit):
    return lax.rem(lax.div(value, 1 << bit), 2)


def top_bit(count):
    return count.bit_length() - 1


def spectra_kernel(chan_count, spectra_count, volt_hbm, taps_hbm, table_hbm, *refs):
    outs, scratch = refs[:-10], refs[-10:]
    volt_ref, taps_ref, table_ref, matrix_ref = scratch[:4]
    filtered, first, last, pieces, volt_sems, table_sems = scratch[4:]
    tap_count, fine = taps_ref.shape
    frame_count = spectra_count + tap_count - 1
    volt_copies = [
        pltpu.make_async_copy(volt_hbm.at[part], volt_ref.at[part], volt_sems.at[part])
        for part in range(2)
    ]
    table_copies = [
        pltpu.make_async_copy(source, target, table_sems.at[at])
        for at, (source, target) in enumerate(
            [(taps_hbm, taps_ref), (table_hbm, table_ref)]
        )
    ]
    table_copies[0].start()
    volt_copies[0].start()
    volt_copies[1].start()
    table_copies[1].start()
    table_copies[0].wait()
    for part in range(2):
        volt_copies[part].wait()

        def filter_column(p, carry, part=part):
            column = pl.multiple_of(p * LANES, LANES)
            taps = [taps_ref[pl.ds(t, 1), pl.ds(column, LANES)] for t in range(tap_count)]
            sums = [None] * spectra_count
            for frame in range(frame_count):
                at = pl.multiple_of(frame * fine + column, LANES)
                values = volt_ref[part, :, pl.ds(at, LANES)].astype(jnp.float32)
                for s in range(spectra_count):
                    t = frame - s
                    if 0 <= t < tap_count:
                        term = taps[t] * values
                        sums[s] = term if sums[s] is None else sums[s] + term
            for s in range(spectra_count):
                filtered[s, part, p] = sums[s]
            return carry

        lax.fori_loop(0, OUTER, filter_column, 0)
    table_copies[1].wait()
    table = table_ref[pl.ds(0, 2 * LANES), :]
    matrix_ref[0] = table.astype(jnp.bfloat16)
    matrix_ref[1] = (table - matrix_ref[0].astype(jnp.float32)).astype(jnp.bfloat16)

    def transform(s, carry):
        for a in range(8):
            values = four([(filtered[s, 0, a + 8 * b], filtered[s, 1, a + 8 * b]) for b in range(4)])
            for r in range(4):
                real, imag = turn(values[r], a * r, OUTER)
                first[0, r, a] = real
                first[1, r, a] = imag
        odd = lax.rem(s, 2)
        for r in range(4):
            values = eight([(first[0, r, a], first[1, r, a]) for a in range(8)])
            highs, lows = [], []
            for t in range(8):
                k1 = r + 4 * t
                factors = table_ref[pl.ds(2 * LANES + odd * OUTER + k1, 1), :]
                cos, sin = factors[:, :LANES], factors[:, LANES:]
                real, imag = values[t]
                row = jnp.concatenate([real * cos + imag * sin, imag * cos - real * sin], axis=1)
                high = row.astype(jnp.bfloat16)
                highs.append(high)
                lows.append((row - high.astype(jnp.float32)).astype(jnp.bfloat16))
            high = jnp.concatenate(highs, axis=0)
            low = jnp.concatenate(lows, axis=0)
            dot = functools.partial(jnp.dot, preferred_element_type=jnp.float32)
            result = dot(high, matrix_ref[0]) + (dot(low, matrix_ref[0]) + dot(high, matrix_ref[1]))
            result = result.astype(jnp.bfloat16)
            for t in range(8):
                rows = result[t * ROWS : (t + 1) * ROWS]
                last[s, 0, r + 4 * t] = rows[:, :LANES]
                last[s, 1, r + 4 * t] = rows[:, LANES:]
        return carry

    lax.fori_loop(0, spectra_count, transform, 0)

    lane = lax.broadcasted_iota(jnp.int32, (ROWS, LANES), 1)
    bits = [(lane >> bit) & 1 == 1 for bit in range(7)]
    group_count = pieces.shape[1]

    def regroup(part, carry):
        for pair in range(spectra_count // 2):
            even = [last[2 * pair, part, k1] for k1 in range(OUTER)]
            odd = [last[2 * pair + 1, part, k1] for k1 in range(OUTER)]
            mixed = [
                [jnp.where(bits[1], odd[v], even[v]) for v in range(OUTER)],
                [jnp.where(bits[1], even[v], odd[v - 1]) for v in range(OUTER)],
            ]
            for which in range(2):
                tiles = [mixed[which][-v % OUTER] for v in range(OUTER)]
                for bit in range(5):
                    tiles = [
                        jnp.where(bits[2 + bit], tiles[v - (1 << bit)], tiles[v])
                        for v in range(OUTER)
                    ]
                for u in range(OUTER):
                    chan, group = divmod(2 * u + which, group_count)
                    pieces[chan, group, part * (spectra_count // 2) + pair] = tiles[u]
        return carry

    lax.fori_loop(0, 2, regroup, 0)
    own = lax.axis_index("chan")
    top = bit_of(lax.axis_index("inp"), top_bit(lax.axis_size("inp")) - 1)
    half = group_count // 2
    moving, other = pl.ds((1 - top) * half, half), pl.ds(top * half, half)
    own_moving, own_other, *direct, held, relay_moving, relay_other = outs
    own_moving[...] = pieces[own, moving]
    own_other[...] = pieces[own, other]
    for index in range(chan_count // 2):
        chan = jnp.bitwise_xor(own, 2 * index)
        if index:
            direct[index - 1][...] = pieces[chan, moving]
            held[index - 1] = pieces[chan, other]
        relay_moving[index] = pieces[jnp.bitwise_xor(chan, 1), moving]
        relay_other[index] = pieces[jnp.bitwise_xor(chan, 1), other]


def spectra_pieces(voltages, filter_taps, chan_count):
    tap_count, fine = filter_taps.shape
    signals = voltages.shape[1]
    spectra_count = voltages.shape[2] // fine - tap_count + 1
    padded = -signals % ROWS
    if padded:
        voltages = jnp.pad(voltages, ((0, 0), (0, padded), (0, 0)))
    group_count = fine // AVG // chan_count
    slices = spectra_count
    piece = (group_count, slices, ROWS, LANES)
    part = (group_count // 2, slices, ROWS, LANES)
    half_count = chan_count // 2
    shapes = [part] * (half_count + 1) + [(half_count - 1,) + part] + [(half_count,) + part] * 2
    table = np.concatenate([lane_matrix(), twiddle_table().reshape(-1, 2 * LANES)])
    outs = pl.pallas_call(
        functools.partial(spectra_kernel, chan_count, spectra_count),
        out_shape=[jax.ShapeDtypeStruct(shape, jnp.bfloat16) for shape in shapes],
        in_specs=[pl.BlockSpec(memory_space=pltpu.HBM)] * 3,
        out_specs=[pl.BlockSpec(memory_space=pltpu.VMEM)] * len(shapes),
        scratch_shapes=[
            pltpu.VMEM(voltages.shape, jnp.bfloat16),
            pltpu.VMEM(filter_taps.shape, jnp.float32),
            pltpu.VMEM(table.shape, jnp.float32),
            pltpu.VMEM((2, 2 * LANES, 2 * LANES), jnp.bfloat16),
            pltpu.VMEM((spectra_count, 2, OUTER, ROWS, LANES), jnp.float32),
            pltpu.VMEM((2, 4, 8, ROWS, LANES), jnp.float32),
            pltpu.VMEM((spectra_count, 2, OUTER, ROWS, LANES), jnp.bfloat16),
            pltpu.VMEM((chan_count,) + piece, jnp.bfloat16),
            pltpu.SemaphoreType.DMA((2,)),
            pltpu.SemaphoreType.DMA((2,)),
        ],
        compiler_params=pltpu.CompilerParams(vmem_limit_bytes=53 * MIB),
        name="spectra",
    )(voltages, filter_taps, jnp.asarray(table))
    outs = [out[..., :signals, :] for out in outs]
    return outs[:2] + [outs[2:-3]] + outs[-3:]


def vmem_call(name, kernel, out_shapes, operands, after=()):
    count = len(operands)
    operands = list(operands) + list(after)

    def body(*refs):
        kernel(*refs[:count], *refs[len(operands) :])

    return pl.pallas_call(
        body,
        out_shape=[jax.ShapeDtypeStruct(shape, jnp.bfloat16) for shape in out_shapes],
        in_specs=[pl.BlockSpec(memory_space=pltpu.VMEM)] * count
        + [pl.BlockSpec(memory_space=pl.ANY)] * len(after),
        out_specs=[pl.BlockSpec(memory_space=pltpu.VMEM)] * len(out_shapes),
        compiler_params=pltpu.CompilerParams(vmem_limit_bytes=8 * MIB),
        name=name,
    )(*operands)


def split_kernel(relayed, *outs):
    for index, out in enumerate(outs):
        out[...] = relayed[index + 1]


def hand_on_kernel(held, relayed, *outs):
    for index, out in enumerate(outs):
        out[0] = held[index]
        out[1] = relayed[index + 1]


def lay(out, pieces):
    count = len(pieces)
    if count == 1:
        out[...] = pieces[0][...]
        return
    own = lax.axis_index("chan")
    rows = out.shape[2] // count
    for k, piece in enumerate(pieces):
        source = jnp.bitwise_xor(lax.div(own, 2), k)
        span = pl.ds(pl.multiple_of(source * rows, rows), rows)
        out[:, :, span, :] = piece[...]


def lay_kernel(*refs):
    lay(refs[-1], refs[:-1])


def lay_relayed_kernel(relayed, *refs):
    lay(refs[-1], [relayed.at[0], *refs[:-1]])


def lay_rest_kernel(rest_count, near_moving, far_moving, own_other, relayed, *refs):
    rest, outs = refs[:rest_count], refs[rest_count:]
    near = [own_other] + [value.at[0] for value in rest]
    far = [relayed.at[0]] + [value.at[1] for value in rest]
    lay_other_kernel(len(near), near_moving, far_moving, *near, *far, *outs)


def lay_other_kernel(piece_count, near_moving, far_moving, *refs):
    near, far = refs[:piece_count], refs[piece_count : 2 * piece_count]
    near_other, far_other, *sends = refs[2 * piece_count :]
    lay(near_other, near)
    lay(far_other, far)
    block = lax.axis_index("inp")
    top = bit_of(block, len(sends))
    for bit, out in enumerate(sends):
        same = bit_of(block, bit) == top

        @pl.when(same)
        def _(out=out):
            out[0] = near_moving[...]
            out[1] = far_moving[...]

        @pl.when(jnp.logical_not(same))
        def _(out=out):
            out[0] = near_other[...]
            out[1] = far_other[...]


def products(left, right):
    slices = left.shape[0]
    real_first = [left[i] for i in range(slices)]
    turned = real_first[slices // 2 :] + [-value for value in real_first[: slices // 2]]
    other = jnp.concatenate([right[i] for i in range(slices)], axis=1)
    contract = (((1,), (1,)), ((), ()))
    scale = 2.0 / (slices * LANES)
    results = []
    for side in (real_first, turned):
        rows = jnp.concatenate(side, axis=1)
        results.append(
            lax.dot_general(rows, other, contract, preferred_element_type=jnp.float32) * scale
        )
    return results


def fill(target, parts, chan_count):
    if len(parts) == 1:
        target[...] = parts[0][...]
        return
    own = lax.rem(lax.axis_index("chan"), 2)
    rows = target.shape[2] // chan_count
    for parity, part in enumerate(parts):
        first = own if parity == 0 else 1 - own
        for source in range(chan_count // 2):
            span = pl.ds(pl.multiple_of((2 * source + first) * rows, rows), rows)
            target[:, :, span, :] = part[:, :, pl.ds(source * rows, rows), :]


def correlate_kernel(chan_count, block_bits, masks, layout, with_autos, pairing_ref, *refs):
    inputs = []
    at = 0
    for kind in layout:
        if kind == "stack":
            inputs.append([refs[at].at[0], refs[at].at[1]])
            at += 1
        else:
            count = 2 if kind == "pair" else 1
            inputs.append(list(refs[at : at + count]))
            at += count
    if not with_autos:
        at += 1
    refs = refs[at:]
    vis_hbm, refs = refs[0], refs[1:]
    if with_autos:
        autos_hbm, block, others, vis, vis_sems, autos, auto_sems = refs
    else:
        block, others, vis, vis_sems = refs
    top = bit_of(lax.axis_index("inp"), block_bits - 1)
    half = block.shape[1]
    for slot in range(2):
        fill(block.at[slot], inputs[slot], chan_count)
    for index in range(len(masks)):
        fill(others.at[index], inputs[2 + index], chan_count)
    places = []
    for mask in masks:
        at = jnp.int32(0)
        for turn_at in range(pairing_ref.shape[0]):
            at = jnp.where(pairing_ref[turn_at] == mask, turn_at, at)
        places.append(at)
    copies = []

    def store(source, target, sem):
        copy = pltpu.make_async_copy(source, target, sem)
        copy.start()
        copies.append(copy)

    for group in range(half):
        for index, mask in enumerate(masks):
            bit = top_bit(mask)
            slot = 1
            if bit != block_bits - 1:
                slot = (bit_of(lax.axis_index("inp"), bit) == top).astype(jnp.int32)
            left = block[slot, group]
            vis[0, index, group], vis[1, index, group] = products(left, others[index, group])
            for part in range(2):
                store(
                    vis.at[part, index, group],
                    vis_hbm.at[part, places[index], group],
                    vis_sems.at[part, index, group],
                )
        for slot in range(2 * with_autos):
            left = block[slot, group]
            at = half * (slot * top + (1 - slot) * (1 - top)) + group
            autos[0, slot, group], autos[1, slot, group] = products(left, left)
            for part in range(2):
                store(
                    autos.at[part, slot, group],
                    autos_hbm.at[part, at],
                    auto_sems.at[part, slot, group],
                )
    for copy in copies:
        copy.wait()


def correlate(pairing, entries, masks, chan_count, block_bits, before=None):
    half, slices, rows = entries[0][1][0].shape[-4:-1]
    operands, layout = [], []
    for kind, values in entries:
        layout.append(kind)
        operands += values
    if layout[0] != "whole":
        rows *= 2
    with_autos = before is None
    round_count = pairing.shape[0]
    vis_shape = (2, len(masks), half, rows, rows)
    auto_shape = (2, 2, half, rows, rows)
    outs = [jax.ShapeDtypeStruct((2, round_count, half, rows, rows), jnp.float32)]
    scratch = [
        pltpu.VMEM((2, half, slices, rows, LANES), jnp.bfloat16),
        pltpu.VMEM((len(masks), half, slices, rows, LANES), jnp.bfloat16),
        pltpu.VMEM(vis_shape, jnp.float32),
        pltpu.SemaphoreType.DMA(vis_shape[:3]),
    ]
    specs = [pl.BlockSpec(memory_space=pltpu.SMEM)]
    specs += [pl.BlockSpec(memory_space=pltpu.VMEM)] * len(operands)
    aliases = {}
    if with_autos:
        outs.append(jax.ShapeDtypeStruct((2, 2 * half, rows, rows), jnp.float32))
        scratch += [pltpu.VMEM(auto_shape, jnp.float32), pltpu.SemaphoreType.DMA(auto_shape[:3])]
    else:
        aliases = {len(specs): 0}
        specs.append(pl.BlockSpec(memory_space=pltpu.HBM))
        operands = operands + [before]
    flops = 16 * len(masks) * half * rows * rows * slices * LANES
    return pl.pallas_call(
        functools.partial(
            correlate_kernel, chan_count, block_bits, masks, tuple(layout), with_autos
        ),
        out_shape=outs,
        in_specs=specs,
        out_specs=[pl.BlockSpec(memory_space=pltpu.HBM)] * len(outs),
        scratch_shapes=scratch,
        input_output_aliases=aliases,
        compiler_params=pltpu.CompilerParams(vmem_limit_bytes=24 * MIB),
        cost_estimate=pl.CostEstimate(flops=flops, bytes_accessed=4 << 20, transcendentals=0),
        name="correlate" if with_autos else "correlate_rest",
    )(pairing, *operands)


def on_device(voltages, filter_taps, pairing):
    chan_count = lax.axis_size("chan")
    inp_count = lax.axis_size("inp")
    block_bits = top_bit(inp_count)
    own_chan = lax.axis_index("chan")
    signals = voltages.shape[1]

    def exchange(value, axis, mask):
        count = lax.axis_size(axis)
        return lax.ppermute(value, axis, [(i, i ^ mask) for i in range(count)])

    evens = list(range(2, chan_count, 2))
    own_moving, own_other, direct, held, relay_moving, relay_other = spectra_pieces(
        voltages, filter_taps, chan_count
    )
    part = own_moving.shape
    half = part[0]
    relay_moving = exchange(relay_moving, "chan", 1)
    direct = [exchange(value, "chan", k) for value, k in zip(direct, evens)]
    relay_other = exchange(relay_other, "chan", 1)
    onward = vmem_call(
        "split", split_kernel, [part] * len(evens), [relay_moving], []
    )
    onward = [exchange(value, "chan", k) for value, k in zip(onward, evens)]
    near, far = [own_moving] + direct, [relay_moving[0]] + onward
    laid = part[:2] + (chan_count // 2 * signals, LANES)
    whole_tiles = signals % ROWS == 0
    if whole_tiles:
        (near,) = vmem_call("near", lay_kernel, [laid], near, [])
        (far,) = vmem_call("far", lay_relayed_kernel, [laid], [relay_moving] + onward, [])
    else:
        sources = jnp.bitwise_xor(own_chan // 2, jnp.arange(chan_count // 2))

        def merge(parts):
            return jnp.take(jnp.stack(parts, axis=2), sources, axis=2).reshape(laid)

        near, far = merge(near), merge(far)
    top_mask = inp_count // 2
    crossed = [exchange(value, "inp", top_mask) for value in (near, far)]
    rest = vmem_call(
        "hand_on",
        hand_on_kernel,
        [(2,) + part] * len(evens),
        [held, relay_other],
        [near],
    )
    rest = [exchange(value, "chan", k) for value, k in zip(rest, evens)]
    if whole_tiles:
        other_kernel = functools.partial(lay_rest_kernel, len(evens))
        others = [own_other, relay_other] + rest
    else:
        other_kernel = functools.partial(lay_other_kernel, 1)
        others = [
            merge([own_other] + [value[0] for value in rest]),
            merge([relay_other[0]] + [value[1] for value in rest]),
        ]
    near_other, far_other, *sends = vmem_call(
        "other",
        other_kernel,
        [laid] * 2 + [(2,) + laid] * (block_bits - 1),
        [near, far] + others,
        [],
    )
    masks = list(range(1, inp_count))
    received = {top_mask: ("pair", crossed)}
    for mask in masks:
        bit = top_bit(mask)
        if mask == top_mask:
            continue
        if mask > 1 and mask % 2:
            kind, values = received[mask - 1]
            received[mask] = (kind, [exchange(value, "inp", 1) for value in values])
        else:
            kind, values = "pair", [near, far]
            if bit != block_bits - 1:
                kind, values = "stack", [sends[bit]]
            received[mask] = (kind, [exchange(value, "inp", mask) for value in values])
    block = [("pair", [near, far]), ("pair", [near_other, far_other])]
    if not whole_tiles:
        parities = jnp.bitwise_xor(own_chan % 2, jnp.arange(2))

        def interleave(entry):
            kind, values = entry
            if kind == "stack":
                values = [values[0][0], values[0][1]]
            shaped = [value.reshape(half, -1, chan_count // 2, signals, LANES) for value in values]
            ordered = jnp.take(jnp.stack(shaped, axis=3), parities, axis=3)
            return ("whole", [ordered.reshape(half, -1, chan_count * signals, LANES)])

        block = [interleave(entry) for entry in block]
        received = {mask: interleave(entry) for mask, entry in received.items()}
    early = [mask for mask in masks if top_bit(mask) == block_bits - 1]
    late = [mask for mask in masks if top_bit(mask) != block_bits - 1]
    visibilities, autos = correlate(
        pairing, block + [received[mask] for mask in early], early, chan_count, block_bits
    )
    (visibilities,) = correlate(
        pairing,
        block + [received[mask] for mask in late],
        late,
        chan_count,
        block_bits,
        visibilities,
    )
    return (visibilities, autos)


def solution(mesh):
    in_specs = (P(None, ("inp", "chan"), None), P(), P())
    out_specs = (P(None, None, "chan", "inp", None), P(None, "chan", "inp", None))
    return jax.shard_map(
        on_device, mesh=mesh, in_specs=in_specs, out_specs=out_specs, check_vma=False
    )
```

time: 66.2 us -> 47.2 us (0.71)
  the two profiles are of different devices: /device:TPU:17 before, /device:TPU:0 now
where the time goes in v2:
time: 47.2 us; the launch traced here: 47.1 us
  starting transfers between devices  20.8 us (44%)
  Pallas kernels  13.4 us (28%)
  waiting for transfers between devices  12.2 us (26%)
  between operations  0.73 us (2%)
    ppermute x16, starting transfers between devices, exchange(): return lax.ppermute(value, axis, [(i, i ^ mask) for i in range(count)])  20.8 us
    ppermute x16, waiting for transfers between devices, exchange(): return lax.ppermute(value, axis, [(i, i ^ mask) for i in range(count)])  12.2 us
    pallas_call x1, Pallas kernels, spectra_pieces(): pl.pallas_call(functools.partial(spectra_kernel, chan_count, spectra_coun...  8.36 us
    pallas_call x2, Pallas kernels, correlate(): pl.pallas_call(functools.partial(correlate_kernel, chan_count, block_bits...  4.8 us
  transfers between devices with their start and end apart: 16, of which 6 were waited for; matrix products, arithmetic and copies ran while one was open for 0% of the time, Pallas kernels for 7%

profile of v2, /device:TPU:0, one launch (start us, length us, event | category | flops | bytes accessed | tf_op | source)
XLA Modules:
  0.0 47.1 jit_solution(8998279950386283421)
XLA Ops:
  0.6 8.4 %spectra.1 = (bf16[4,4,16,128]{3,2,1,0:T(8,128)(2,1)S(1)}, bf16[4,4,16,128]{3,2,1,0:T(8,128)(2,1)S(1)}, bf16[4,4,16,128]{3,2,1,0:T(8,128)(2,1)S(1)}, bf16[4,4,16...) custom-call(bf16[2,16,77824]{2,1,0:T(8,128)(2,1)} %volt_hbm.1, ...), custom_call_target="tpu_custom_call" | custom-call | tf_op jit(solution)/shard_map/spectra/pallas_call | solution.py:219
  9.0 3.0 %collective-permute-start.3 = (bf16[4,4,4,16,128]{4,3,2,1,0:T(8,128)(2,1)S(1)}, bf16[4,4,4,16,128]{4,3,2,1,0:T(8,128)(2,1)S(1)}, u32[]{:S(2)}, u32[]{:S(2)}) collective-permute-start(bf16[4,4,4,16,128]{4,3,2,1,0:T(8,128)(2,1)S(1)} %get-tuple-element.25), channel_id=1, source_target_pairs={{0,1},{1,0},{2,3},{3,2},{4,5},{5,4},{6,7},{7,6},{8,9},{9,8},{10,11... | collective-permute-start | bytes 786440 | tf_op jit(solution)/shard_map/ppermute | solution.py:470
  12.0 0.1 collective-permute-start.7
  12.1 2.0 %collective-permute-start = (bf16[4,4,16,128]{3,2,1,0:T(8,128)(2,1)S(1)}, bf16[4,4,16,128]{3,2,1,0:T(8,128)(2,1)S(1)}, u32[]{:S(2)}, u32[]{:S(2)}) collective-permute-start(bf16[4,4,16,128]{3,2,1,0:T(8,128)(2,1)S(1)} %get-tuple-element.22), channel_id=1, source_target_pairs={{0,2},{1,3},{2,0},{3,1},{4,6},{5,7},{6,4},{7,5},{8,10},{9,11},{10,... | collective-permute-start | bytes 196616 | tf_op jit(solution)/shard_map/ppermute | solution.py:470
  14.1 2.6 %collective-permute-start.1 = (bf16[4,4,16,128]{3,2,1,0:T(8,128)(2,1)S(1)}, bf16[4,4,16,128]{3,2,1,0:T(8,128)(2,1)S(1)}, u32[]{:S(2)}, u32[]{:S(2)}) collective-permute-start(bf16[4,4,16,128]{3,2,1,0:T(8,128)(2,1)S(1)} %get-tuple-element.23), channel_id=1, source_target_pairs={{0,4},{1,5},{2,6},{3,7},{4,0},{5,1},{6,2},{7,3},{8,12},{9,13},{10,... | collective-permute-start | bytes 196616 | tf_op jit(solution)/shard_map/ppermute | solution.py:470
  16.7 0.0 collective-permute-start.2
  16.7 2.5 %collective-permute-done.3.refs_0_ = bf16[4,4,4,16,128]{4,3,2,1,0:T(8,128)(2,1)S(1)} collective-permute-done((bf16[4,4,4,16,128]{4,3,2,1,0:T(8,128)(2,1)S(1)}, bf16[4,4,4,16,128]{4,3,2,1,0:T(8,128)(2,1)S(1)}, u32[]{:S(2)}, u32[]{:S(2)}) %collective-permute-start.3) | collective-permute-done | bytes 262176 | tf_op jit(solution)/shard_map/ppermute | solution.py:470
  19.2 2.2 %collective-permute-start.4 = (bf16[4,4,16,128]{3,2,1,0:T(8,128)(2,1)S(1)}, bf16[4,4,16,128]{3,2,1,0:T(8,128)(2,1)S(1)}, u32[]{:S(2)}, u32[]{:S(2)}) collective-permute-start(bf16[4,4,16,128]{3,2,1,0:T(8,128)(2,1)S(1)} %get-tuple-element.26), channel_id=1, source_target_pairs={{0,2},{1,3},{2,0},{3,1},{4,6},{5,7},{6,4},{7,5},{8,10},{9,11},{10,... | collective-permute-start | bytes 196616 | tf_op jit(solution)/shard_map/ppermute | solution.py:470
  21.4 0.0 collective-permute-done.refs_1_
  21.4 2.6 %collective-permute-start.5 = (bf16[4,4,16,128]{3,2,1,0:T(8,128)(2,1)S(1)}, bf16[4,4,16,128]{3,2,1,0:T(8,128)(2,1)S(1)}, u32[]{:S(2)}, u32[]{:S(2)}) collective-permute-start(bf16[4,4,16,128]{3,2,1,0:T(8,128)(2,1)S(1)} %get-tuple-element.27), channel_id=1, source_target_pairs={{0,4},{1,5},{2,6},{3,7},{4,0},{5,1},{6,2},{7,3},{8,12},{9,13},{10,... | collective-permute-start | bytes 196616 | tf_op jit(solution)/shard_map/ppermute | solution.py:470
  24.0 0.0 collective-permute-done.1.refs_2_
  24.0 0.0 collective-permute-start.6
  24.0 0.0 collective-permute-done.2.refs_3_
  24.0 0.0 copy-start
  24.0 0.0 collective-permute-done.7.refs_1_.refs_3_
  24.1 1.8 %collective-permute-start.8 = (bf16[2,4,4,16,128]{4,3,2,1,0:T(8,128)(2,1)S(1)}, bf16[2,4,4,16,128]{4,3,2,1,0:T(8,128)(2,1)S(1)}, u32[]{:S(2)}, u32[]{:S(2)}) collective-permute-start(bf16[2,4,4,16,128]{4,3,2,1,0:T(8,128)(2,1)S(1)} %get-tuple-element.32), channel_id=1, source_target_pairs={{0,2},{1,3},{2,0},{3,1},{4,6},{5,7},{6,4},{7,5},{8,10},{9,11},{10,... | collective-permute-start | bytes 393224 | tf_op jit(solution)/shard_map/ppermute | solution.py:470
  25.8 2.7 %collective-permute-start.9 = (bf16[2,4,4,16,128]{4,3,2,1,0:T(8,128)(2,1)S(1)}, bf16[2,4,4,16,128]{4,3,2,1,0:T(8,128)(2,1)S(1)}, u32[]{:S(2)}, u32[]{:S(2)}) collective-permute-start(bf16[2,4,4,16,128]{4,3,2,1,0:T(8,128)(2,1)S(1)} %get-tuple-element.33), channel_id=1, source_target_pairs={{0,4},{1,5},{2,6},{3,7},{4,0},{5,1},{6,2},{7,3},{8,12},{9,13},{10,... | collective-permute-start | bytes 393224 | tf_op jit(solution)/shard_map/ppermute | solution.py:470
  28.5 0.0 collective-permute-done.4.refs_1_
  28.5 0.0 collective-permute-start.10
  28.5 0.0 collective-permute-done.5.refs_2_
  28.6 1.7 %collective-permute-start.12 = (bf16[4,4,64,128]{3,2,1,0:T(8,128)(2,1)S(1)}, bf16[4,4,64,128]{3,2,1,0:T(8,128)(2,1)S(1)}, u32[]{:S(2)}, u32[]{:S(2)}) collective-permute-start(bf16[4,4,64,128]{3,2,1,0:T(8,128)(2,1)S(1)} %near.1.refs_2_.refs_0_), channel_id=1, source_target_pairs={{0,16},{8,24},{16,0},{24,8},{1,17},{9,25},{17,1},{25,9},{2,18},{10... | collective-permute-start | bytes 786440 | tf_op jit(solution)/shard_map/ppermute | solution.py:470
  30.2 0.7 %collective-permute-done.6.refs_3_ = bf16[4,4,16,128]{3,2,1,0:T(8,128)(2,1)S(1)} collective-permute-done((bf16[4,4,16,128]{3,2,1,0:T(8,128)(2,1)S(1)}, bf16[4,4,16,128]{3,2,1,0:T(8,128)(2,1)S(1)}, u32[]{:S(2)}, u32[]{:S(2)}) %collective-permute-start.6) | collective-permute-done | bytes 65568 | tf_op jit(solution)/shard_map/ppermute | solution.py:470
  30.9 1.6 %collective-permute-start.13 = (bf16[4,4,64,128]{3,2,1,0:T(8,128)(2,1)S(1)}, bf16[4,4,64,128]{3,2,1,0:T(8,128)(2,1)S(1)}, u32[]{:S(2)}, u32[]{:S(2)}) collective-permute-start(bf16[4,4,64,128]{3,2,1,0:T(8,128)(2,1)S(1)} %far.1.refs_1_), channel_id=1, source_target_pairs={{0,16},{8,24},{16,0},{24,8},{1,17},{9,25},{17,1},{25,9},{2,18},{10... | collective-permute-start | bytes 786440 | tf_op jit(solution)/shard_map/ppermute | solution.py:470
  32.5 0.0 collective-permute-done.8.refs_4_
  32.5 6.0 %collective-permute-done.9.refs_5_ = bf16[2,4,4,16,128]{4,3,2,1,0:T(8,128)(2,1)S(1)} collective-permute-done((bf16[2,4,4,16,128]{4,3,2,1,0:T(8,128)(2,1)S(1)}, bf16[2,4,4,16,128]{4,3,2,1,0:T(8,128)(2,1)S(1)}, u32[]{:S(2)}, u32[]{:S(2)}) %collective-permute-start.9) | collective-permute-done | bytes 131104 | tf_op jit(solution)/shard_map/ppermute | solution.py:470
  38.5 0.0 collective-permute-done.10.refs_6_
  38.5 0.1 other.1
  38.7 0.1 collective-permute-start.11
  38.7 0.0 collective-permute-done.12.refs_4_
  38.7 0.5 %collective-permute-start.14 = (bf16[4,4,64,128]{3,2,1,0:T(8,128)(2,1)S(1)}, bf16[4,4,64,128]{3,2,1,0:T(8,128)(2,1)S(1)}, u32[]{:S(2)}, u32[]{:S(2)}) collective-permute-start(bf16[4,4,64,128]{3,2,1,0:T(8,128)(2,1)S(1)} %collective-permute-done.12.refs_4_), channel_id=1, source_target_pairs={{0,8},{8,0},{16,24},{24,16},{1,9},{9,1},{17,25},{25,17},{2,10},{10... | collective-permute-start | bytes 786440 | tf_op jit(solution)/shard_map/ppermute | solution.py:470
  39.2 1.5 %collective-permute-done.13.refs_5_ = bf16[4,4,64,128]{3,2,1,0:T(8,128)(2,1)S(1)} collective-permute-done((bf16[4,4,64,128]{3,2,1,0:T(8,128)(2,1)S(1)}, bf16[4,4,64,128]{3,2,1,0:T(8,128)(2,1)S(1)}, u32[]{:S(2)}, u32[]{:S(2)}) %collective-permute-start.13) | collective-permute-done | bytes 262176 | tf_op jit(solution)/shard_map/ppermute | solution.py:470
  40.7 0.0 collective-permute-start.15
  40.7 0.3 collective-permute-done.14.refs_6_
  41.0 1.3 %collective-permute-done.15.refs_7_ = bf16[4,4,64,128]{3,2,1,0:T(8,128)(2,1)S(1)} collective-permute-done((bf16[4,4,64,128]{3,2,1,0:T(8,128)(2,1)S(1)}, bf16[4,4,64,128]{3,2,1,0:T(8,128)(2,1)S(1)}, u32[]{:S(2)}, u32[]{:S(2)}) %collective-permute-start.15) | collective-permute-done | bytes 262176 | tf_op jit(solution)/shard_map/ppermute | solution.py:470
  42.3 0.0 copy-done
  42.3 2.9 %correlate.1 = (f32[2,3,4,128,128]{4,3,2,1,0:T(8,128)}, f32[2,8,128,128]{3,2,1,0:T(8,128)}) custom-call(s32[3]{0:T(128)S(1)} %copy-done, bf16[4,4,64,128]{3,2,1,0:T(8,128)(2,1)S(1)} %near.1.refs_2_.refs_0_, bf16[4,4,64,128]{3,2,1,0:T(8,128)(2,1)S(1)} %far.1.refs_1_, bf16[4,4,64,128]{3,2,1,0:T(8,128)(2,1)S(1)} %get-tuple-element.35.refs_2_, ...), custom_call_target="tpu_custom_call" | custom-call | flops 1073741824 | bytes 4194304 | tf_op jit(solution)/shard_map/correlate/pallas_call | solution.py:446
  45.2 0.0 collective-permute-done.11.refs_4_
  45.2 1.9 %correlate_rest.1 = f32[2,3,4,128,128]{4,3,2,1,0:T(8,128)} custom-call(s32[3]{0:T(128)S(1)} %copy-done, bf16[4,4,64,128]{3,2,1,0:T(8,128)(2,1)S(1)} %near.1.refs_2_.refs_0_, bf16[4,4,64,128]{3,2,1,0:T(8,128)(2,1)S(1)} %far.1.refs_1_, bf16[4,4,64,128]{3,2,1,0:T(8,128)(2,1)S(1)} %get-tuple-element.35.refs_2_, ...), custom_call_target="tpu_custom_call", output_to_operand_aliasing={{}: (6, {})} | custom-call | flops 536870912 | bytes 4194304 | tf_op jit(solution)/shard_map/correlate_rest/pallas_call | solution.py:446
  (4 shorter events, 0.1 us)
Async XLA Ops:
  9.0 10.2 %collective-permute-start.3 = (bf16[4,4,4,16,128]{4,3,2,1,0:T(8,128)(2,1)S(1)}, bf16[4,4,4,16,128]{4,3,2,1,0:T(8,128)(2,1)S(1)}, u32[]{:S(2)}, u32[]{:S(2)}) collective-permute-start(bf16[4,4,4,16,128]{4,3,2,1,0:T(8,128)(2,1)S(1)} %get-tuple-element.25), channel_id=1, source_target_pairs={{0,1},{1,0},{2,3},{3,2},{4,5},{5,4},{6,7},{7,6},{8,9},{9,8},{10,11... | collective-permute-start | bytes 786440 | tf_op jit(solution)/shard_map/ppermute | solution.py:470
  12.0 12.0 %collective-permute-start.7 = (bf16[4,4,4,16,128]{4,3,2,1,0:T(8,128)(2,1)}, bf16[4,4,4,16,128]{4,3,2,1,0:T(8,128)(2,1)S(1)}, u32[]{:S(2)}, u32[]{:S(2)}) collective-permute-start(bf16[4,4,4,16,128]{4,3,2,1,0:T(8,128)(2,1)} %get-tuple-element.30), channel_id=1, source_target_pairs={{0,1},{1,0},{2,3},{3,2},{4,5},{5,4},{6,7},{7,6},{8,9},{9,8},{10,11... | collective-permute-start | bytes 786440 | tf_op jit(solution)/shard_map/ppermute | solution.py:470
  12.1 9.3 %collective-permute-start = (bf16[4,4,16,128]{3,2,1,0:T(8,128)(2,1)S(1)}, bf16[4,4,16,128]{3,2,1,0:T(8,128)(2,1)S(1)}, u32[]{:S(2)}, u32[]{:S(2)}) collective-permute-start(bf16[4,4,16,128]{3,2,1,0:T(8,128)(2,1)S(1)} %get-tuple-element.22), channel_id=1, source_target_pairs={{0,2},{1,3},{2,0},{3,1},{4,6},{5,7},{6,4},{7,5},{8,10},{9,11},{10,... | collective-permute-start | bytes 196616 | tf_op jit(solution)/shard_map/ppermute | solution.py:470
  14.1 9.8 %collective-permute-start.1 = (bf16[4,4,16,128]{3,2,1,0:T(8,128)(2,1)S(1)}, bf16[4,4,16,128]{3,2,1,0:T(8,128)(2,1)S(1)}, u32[]{:S(2)}, u32[]{:S(2)}) collective-permute-start(bf16[4,4,16,128]{3,2,1,0:T(8,128)(2,1)S(1)} %get-tuple-element.23), channel_id=1, source_target_pairs={{0,4},{1,5},{2,6},{3,7},{4,0},{5,1},{6,2},{7,3},{8,12},{9,13},{10,... | collective-permute-start | bytes 196616 | tf_op jit(solution)/shard_map/ppermute | solution.py:470
  16.7 7.3 %collective-permute-start.2 = (bf16[4,4,16,128]{3,2,1,0:T(8,128)(2,1)S(1)}, bf16[4,4,16,128]{3,2,1,0:T(8,128)(2,1)S(1)}, u32[]{:S(2)}, u32[]{:S(2)}) collective-permute-start(bf16[4,4,16,128]{3,2,1,0:T(8,128)(2,1)S(1)} %get-tuple-element.24), channel_id=1, source_target_pairs={{0,6},{1,7},{2,4},{3,5},{4,2},{5,3},{6,0},{7,1},{8,14},{9,15},{10,... | collective-permute-start | bytes 196616 | tf_op jit(solution)/shard_map/ppermute | solution.py:470
  19.2 9.3 %collective-permute-start.4 = (bf16[4,4,16,128]{3,2,1,0:T(8,128)(2,1)S(1)}, bf16[4,4,16,128]{3,2,1,0:T(8,128)(2,1)S(1)}, u32[]{:S(2)}, u32[]{:S(2)}) collective-permute-start(bf16[4,4,16,128]{3,2,1,0:T(8,128)(2,1)S(1)} %get-tuple-element.26), channel_id=1, source_target_pairs={{0,2},{1,3},{2,0},{3,1},{4,6},{5,7},{6,4},{7,5},{8,10},{9,11},{10,... | collective-permute-start | bytes 196616 | tf_op jit(solution)/shard_map/ppermute | solution.py:470
  21.4 7.2 %collective-permute-start.5 = (bf16[4,4,16,128]{3,2,1,0:T(8,128)(2,1)S(1)}, bf16[4,4,16,128]{3,2,1,0:T(8,128)(2,1)S(1)}, u32[]{:S(2)}, u32[]{:S(2)}) collective-permute-start(bf16[4,4,16,128]{3,2,1,0:T(8,128)(2,1)S(1)} %get-tuple-element.27), channel_id=1, source_target_pairs={{0,4},{1,5},{2,6},{3,7},{4,0},{5,1},{6,2},{7,3},{8,12},{9,13},{10,... | collective-permute-start | bytes 196616 | tf_op jit(solution)/shard_map/ppermute | solution.py:470
  24.0 6.9 %collective-permute-start.6 = (bf16[4,4,16,128]{3,2,1,0:T(8,128)(2,1)S(1)}, bf16[4,4,16,128]{3,2,1,0:T(8,128)(2,1)S(1)}, u32[]{:S(2)}, u32[]{:S(2)}) collective-permute-start(bf16[4,4,16,128]{3,2,1,0:T(8,128)(2,1)S(1)} %get-tuple-element.28), channel_id=1, source_target_pairs={{0,6},{1,7},{2,4},{3,5},{4,2},{5,3},{6,0},{7,1},{8,14},{9,15},{10,... | collective-permute-start | bytes 196616 | tf_op jit(solution)/shard_map/ppermute | solution.py:470
  24.0 18.3 %copy-start = (s32[3]{0:T(128)S(1)}, s32[3]{0:T(128)}, u32[]{:S(2)}) copy-start(s32[3]{0:T(128)} %pairing_ref.3) | copy-start | bytes 40
  24.1 8.4 %collective-permute-start.8 = (bf16[2,4,4,16,128]{4,3,2,1,0:T(8,128)(2,1)S(1)}, bf16[2,4,4,16,128]{4,3,2,1,0:T(8,128)(2,1)S(1)}, u32[]{:S(2)}, u32[]{:S(2)}) collective-permute-start(bf16[2,4,4,16,128]{4,3,2,1,0:T(8,128)(2,1)S(1)} %get-tuple-element.32), channel_id=1, source_target_pairs={{0,2},{1,3},{2,0},{3,1},{4,6},{5,7},{6,4},{7,5},{8,10},{9,11},{10,... | collective-permute-start | bytes 393224 | tf_op jit(solution)/shard_map/ppermute | solution.py:470
  25.8 12.7 %collective-permute-start.9 = (bf16[2,4,4,16,128]{4,3,2,1,0:T(8,128)(2,1)S(1)}, bf16[2,4,4,16,128]{4,3,2,1,0:T(8,128)(2,1)S(1)}, u32[]{:S(2)}, u32[]{:S(2)}) collective-permute-start(bf16[2,4,4,16,128]{4,3,2,1,0:T(8,128)(2,1)S(1)} %get-tuple-element.33), channel_id=1, source_target_pairs={{0,4},{1,5},{2,6},{3,7},{4,0},{5,1},{6,2},{7,3},{8,12},{9,13},{10,... | collective-permute-start | bytes 393224 | tf_op jit(solution)/shard_map/ppermute | solution.py:470
  28.5 10.0 %collective-permute-start.10 = (bf16[2,4,4,16,128]{4,3,2,1,0:T(8,128)(2,1)S(1)}, bf16[2,4,4,16,128]{4,3,2,1,0:T(8,128)(2,1)S(1)}, u32[]{:S(2)}, u32[]{:S(2)}) collective-permute-start(bf16[2,4,4,16,128]{4,3,2,1,0:T(8,128)(2,1)S(1)} %get-tuple-element.34), channel_id=1, source_target_pairs={{0,6},{1,7},{2,4},{3,5},{4,2},{5,3},{6,0},{7,1},{8,14},{9,15},{10,... | collective-permute-start | bytes 393224 | tf_op jit(solution)/shard_map/ppermute | solution.py:470
  28.6 10.2 %collective-permute-start.12 = (bf16[4,4,64,128]{3,2,1,0:T(8,128)(2,1)S(1)}, bf16[4,4,64,128]{3,2,1,0:T(8,128)(2,1)S(1)}, u32[]{:S(2)}, u32[]{:S(2)}) collective-permute-start(bf16[4,4,64,128]{3,2,1,0:T(8,128)(2,1)S(1)} %near.1.refs_2_.refs_0_), channel_id=1, source_target_pairs={{0,16},{8,24},{16,0},{24,8},{1,17},{9,25},{17,1},{25,9},{2,18},{10... | collective-permute-start | bytes 786440 | tf_op jit(solution)/shard_map/ppermute | solution.py:470
  30.9 9.8 %collective-permute-start.13 = (bf16[4,4,64,128]{3,2,1,0:T(8,128)(2,1)S(1)}, bf16[4,4,64,128]{3,2,1,0:T(8,128)(2,1)S(1)}, u32[]{:S(2)}, u32[]{:S(2)}) collective-permute-start(bf16[4,4,64,128]{3,2,1,0:T(8,128)(2,1)S(1)} %far.1.refs_1_), channel_id=1, source_target_pairs={{0,16},{8,24},{16,0},{24,8},{1,17},{9,25},{17,1},{25,9},{2,18},{10... | collective-permute-start | bytes 786440 | tf_op jit(solution)/shard_map/ppermute | solution.py:470
  38.7 6.5 %collective-permute-start.11 = (bf16[2,4,4,64,128]{4,3,2,1,0:T(8,128)(2,1)S(1)}, bf16[2,4,4,64,128]{4,3,2,1,0:T(8,128)(2,1)S(1)}, u32[]{:S(2)}, u32[]{:S(2)}) collective-permute-start(bf16[2,4,4,64,128]{4,3,2,1,0:T(8,128)(2,1)S(1)} %get-tuple-element.37), channel_id=1, source_target_pairs={{0,8},{8,0},{16,24},{24,16},{1,9},{9,1},{17,25},{25,17},{2,10},{10... | collective-permute-start | bytes 1572872 | tf_op jit(solution)/shard_map/ppermute | solution.py:470
  38.7 2.3 %collective-permute-start.14 = (bf16[4,4,64,128]{3,2,1,0:T(8,128)(2,1)S(1)}, bf16[4,4,64,128]{3,2,1,0:T(8,128)(2,1)S(1)}, u32[]{:S(2)}, u32[]{:S(2)}) collective-permute-start(bf16[4,4,64,128]{3,2,1,0:T(8,128)(2,1)S(1)} %collective-permute-done.12.refs_4_), channel_id=1, source_target_pairs={{0,8},{8,0},{16,24},{24,16},{1,9},{9,1},{17,25},{25,17},{2,10},{10... | collective-permute-start | bytes 786440 | tf_op jit(solution)/shard_map/ppermute | solution.py:470
  40.7 1.5 %collective-permute-start.15 = (bf16[4,4,64,128]{3,2,1,0:T(8,128)(2,1)S(1)}, bf16[4,4,64,128]{3,2,1,0:T(8,128)(2,1)S(1)}, u32[]{:S(2)}, u32[]{:S(2)}) collective-permute-start(bf16[4,4,64,128]{3,2,1,0:T(8,128)(2,1)S(1)} %collective-permute-done.13.refs_5_), channel_id=1, source_target_pairs={{0,8},{8,0},{16,24},{24,16},{1,9},{9,1},{17,25},{25,17},{2,10},{10... | collective-permute-start | bytes 786440 | tf_op jit(solution)/shard_map/ppermute | solution.py:470

commit v3 on v2

--- a/solution.py
+++ b/solution.py
@@ -80,6 +80,10 @@
 
 def top_bit(count):
     return count.bit_length() - 1
+
+
+def hops(count):
+    return [0] + sorted(range(2, count, 2), key=lambda hop: (-top_bit(hop), hop))
 
 
 def spectra_kernel(chan_count, spectra_count, volt_hbm, taps_hbm, table_hbm, *refs):
@@ -193,8 +197,8 @@
     own_moving, own_other, *direct, held, relay_moving, relay_other = outs
     own_moving[...] = pieces[own, moving]
     own_other[...] = pieces[own, other]
-    for index in range(chan_count // 2):
-        chan = jnp.bitwise_xor(own, 2 * index)
+    for index, hop in enumerate(hops(chan_count)):
+        chan = jnp.bitwise_xor(own, hop)
         if index:
             direct[index - 1][...] = pieces[chan, moving]
             held[index - 1] = pieces[chan, other]
@@ -240,7 +244,7 @@
     return outs[:2] + [outs[2:-3]] + outs[-3:]
 
 
-def vmem_call(name, kernel, out_shapes, operands, after=()):
+def vmem_call(name, kernel, out_shapes, operands, after=(), cost=None, aliases=None):
     count = len(operands)
     operands = list(operands) + list(after)
 
@@ -254,13 +258,15 @@
         + [pl.BlockSpec(memory_space=pl.ANY)] * len(after),
         out_specs=[pl.BlockSpec(memory_space=pltpu.VMEM)] * len(out_shapes),
         compiler_params=pltpu.CompilerParams(vmem_limit_bytes=8 * MIB),
+        cost_estimate=cost,
+        input_output_aliases=aliases or {},
         name=name,
     )(*operands)
 
 
 def split_kernel(relayed, *outs):
     for index, out in enumerate(outs):
-        out[...] = relayed[index + 1]
+        out[...] = relayed[index]
 
 
 def hand_on_kernel(held, relayed, *outs):
@@ -276,18 +282,14 @@
         return
     own = lax.axis_index("chan")
     rows = out.shape[2] // count
-    for k, piece in enumerate(pieces):
-        source = jnp.bitwise_xor(lax.div(own, 2), k)
+    for hop, piece in zip(hops(2 * count), pieces):
+        source = lax.div(jnp.bitwise_xor(own, hop), 2)
         span = pl.ds(pl.multiple_of(source * rows, rows), rows)
         out[:, :, span, :] = piece[...]
 
 
 def lay_kernel(*refs):
     lay(refs[-1], refs[:-1])
-
-
-def lay_relayed_kernel(relayed, *refs):
-    lay(refs[-1], [relayed.at[0], *refs[:-1]])
 
 
 def lay_rest_kernel(rest_count, near_moving, far_moving, own_other, relayed, *refs):
@@ -319,143 +321,199 @@
 
 
 def products(left, right):
-    slices = left.shape[0]
-    real_first = [left[i] for i in range(slices)]
-    turned = real_first[slices // 2 :] + [-value for value in real_first[: slices // 2]]
-    other = jnp.concatenate([right[i] for i in range(slices)], axis=1)
+    slices, rows, _ = left.shape
+
+    def operand(values):
+        part = slices // 2
+        real = jnp.concatenate([values[i] for i in range(part)], axis=1)
+        imag = jnp.concatenate([values[i] for i in range(part, slices)], axis=1)
+        return jnp.concatenate([real, imag], axis=0)
+
     contract = (((1,), (1,)), ((), ()))
+    all_parts = lax.dot_general(
+        operand(left), operand(right), contract, preferred_element_type=jnp.float32
+    )
     scale = 2.0 / (slices * LANES)
-    results = []
-    for side in (real_first, turned):
-        rows = jnp.concatenate(side, axis=1)
-        results.append(
-            lax.dot_general(rows, other, contract, preferred_element_type=jnp.float32) * scale
-        )
-    return results
+    real = all_parts[:rows, :rows] + all_parts[rows:, rows:]
+    imag = all_parts[rows:, :rows] - all_parts[:rows, rows:]
+    return real * scale, imag * scale
 
 
 def fill(target, parts, chan_count):
     if len(parts) == 1:
         target[...] = parts[0][...]
         return
+    for parity, part in enumerate(parts):
+        fill_parity(target, part, chan_count, parity)
+
+
+def fill_parity(target, part, chan_count, parity):
     own = lax.rem(lax.axis_index("chan"), 2)
+    first = own if parity == 0 else 1 - own
     rows = target.shape[2] // chan_count
-    for parity, part in enumerate(parts):
-        first = own if parity == 0 else 1 - own
-        for source in range(chan_count // 2):
-            span = pl.ds(pl.multiple_of((2 * source + first) * rows, rows), rows)
-            target[:, :, span, :] = part[:, :, pl.ds(source * rows, rows), :]
-
-
-def correlate_kernel(chan_count, block_bits, masks, layout, with_autos, pairing_ref, *refs):
-    inputs = []
-    at = 0
+    for source in range(chan_count // 2):
+        span = pl.ds(pl.multiple_of((2 * source + first) * rows, rows), rows)
+        target[:, :, span, :] = part[:, :, pl.ds(source * rows, rows), :]
+
+
+def autos_kernel(chan_count, block_bits, paired, *refs):
+    count = 2 if paired else 1
+    inputs = refs[: 2 * count]
+    block, autos_hbm, autos, sems = refs[-4:]
+    half = block.shape[1]
+    top = bit_of(lax.axis_index("inp"), block_bits - 1)
+    copies = []
+    for slot in range(2):
+        fill(block.at[slot], inputs[slot * count : (slot + 1) * count], chan_count)
+        for group in range(half):
+            rows = block[slot, group]
+            at = half * (slot * top + (1 - slot) * (1 - top)) + group
+            autos[0, slot, group], autos[1, slot, group] = products(rows, rows)
+            for part in range(2):
+                copy = pltpu.make_async_copy(
+                    autos.at[part, slot, group], autos_hbm.at[part, at], sems.at[part, slot, group]
+                )
+                copy.start()
+                copies.append(copy)
+    for copy in copies:
+        copy.wait()
+
+
+def autos_call(operands, chan_count, block_bits, after=()):
+    half, slices, rows = operands[0].shape[:3]
+    paired = len(operands) == 4
+    rows *= 2 if paired else 1
+    auto_shape = (2, 2, half, rows, rows)
+    block_shape = (2, half, slices, rows, LANES)
+    return pl.pallas_call(
+        functools.partial(autos_kernel, chan_count, block_bits, paired),
+        out_shape=[
+            jax.ShapeDtypeStruct(block_shape, jnp.bfloat16),
+            jax.ShapeDtypeStruct((2, 2 * half, rows, rows), jnp.float32),
+        ],
+        in_specs=[pl.BlockSpec(memory_space=pltpu.VMEM)] * len(operands)
+        + [pl.BlockSpec(memory_space=pl.ANY)] * len(after),
+        out_specs=[pl.BlockSpec(memory_space=pltpu.VMEM), pl.BlockSpec(memory_space=pltpu.HBM)],
+        scratch_shapes=[
+            pltpu.VMEM(auto_shape, jnp.float32),
+            pltpu.SemaphoreType.DMA(auto_shape[:3]),
+        ],
+        compiler_params=pltpu.CompilerParams(vmem_limit_bytes=8 * MIB),
+        cost_estimate=pl.CostEstimate(
+            flops=16 * half * rows * rows * slices * LANES,
+            bytes_accessed=4 << 20,
+            transcendentals=0,
+        ),
+        name="autos",
+    )(*operands, *after)
+
+
+def parts_of(layout, refs):
+    found, at = [], 0
     for kind in layout:
         if kind == "stack":
-            inputs.append([refs[at].at[0], refs[at].at[1]])
+            found.append([refs[at].at[0], refs[at].at[1]])
             at += 1
         else:
             count = 2 if kind == "pair" else 1
-            inputs.append(list(refs[at : at + count]))
+            found.append(list(refs[at : at + count]))
             at += count
-    if not with_autos:
-        at += 1
-    refs = refs[at:]
-    vis_hbm, refs = refs[0], refs[1:]
-    if with_autos:
-        autos_hbm, block, others, vis, vis_sems, autos, auto_sems = refs
-    else:
-        block, others, vis, vis_sems = refs
-    top = bit_of(lax.axis_index("inp"), block_bits - 1)
+    return found
+
+
+def fill_parity_kernel(chan_count, parity, *refs):
+    for index, part in enumerate(refs[: -1 - parity]):
+        fill_parity(refs[-1].at[index], part, chan_count, parity)
+
+
+def fill_kernel(*refs):
+    for index, part in enumerate(refs[:-1]):
+        refs[-1][index] = part[...]
+
+
+def cross_kernel(chan_count, block_bits, early, late, layout, pairing_hbm, block, filled, *refs):
+    inputs, refs = refs[: -len(SCRATCH)], refs[-len(SCRATCH) :]
+    vis_hbm, others, vis, pairing_ref, vis_sems, pairing_sem = refs
+    pairing_copy = pltpu.make_async_copy(pairing_hbm, pairing_ref, pairing_sem)
+    pairing_copy.start()
+    own = lax.axis_index("inp")
+    top = bit_of(own, block_bits - 1)
     half = block.shape[1]
-    for slot in range(2):
-        fill(block.at[slot], inputs[slot], chan_count)
-    for index in range(len(masks)):
-        fill(others.at[index], inputs[2 + index], chan_count)
-    places = []
-    for mask in masks:
-        at = jnp.int32(0)
+    for index, parts in enumerate(parts_of(layout, inputs)):
+        fill(others.at[index], parts, chan_count)
+    partners = [(mask, filled.at[at]) for at, mask in enumerate(early)]
+    partners += [(mask, others.at[at]) for at, mask in enumerate(late)]
+    copies = []
+    for index, (mask, other) in enumerate(partners):
+        bit = top_bit(mask)
+        slot = 1
+        if bit != block_bits - 1:
+            slot = (bit_of(own, bit) == top).astype(jnp.int32)
+        for group in range(half):
+            vis[0, index, group], vis[1, index, group] = products(block[slot, group], other[group])
+        if index == 0:
+            pairing_copy.wait()
+        place = jnp.int32(0)
         for turn_at in range(pairing_ref.shape[0]):
-            at = jnp.where(pairing_ref[turn_at] == mask, turn_at, at)
-        places.append(at)
-    copies = []
-
-    def store(source, target, sem):
-        copy = pltpu.make_async_copy(source, target, sem)
-        copy.start()
-        copies.append(copy)
-
-    for group in range(half):
-        for index, mask in enumerate(masks):
-            bit = top_bit(mask)
-            slot = 1
-            if bit != block_bits - 1:
-                slot = (bit_of(lax.axis_index("inp"), bit) == top).astype(jnp.int32)
-            left = block[slot, group]
-            vis[0, index, group], vis[1, index, group] = products(left, others[index, group])
-            for part in range(2):
-                store(
-                    vis.at[part, index, group],
-                    vis_hbm.at[part, places[index], group],
-                    vis_sems.at[part, index, group],
-                )
-        for slot in range(2 * with_autos):
-            left = block[slot, group]
-            at = half * (slot * top + (1 - slot) * (1 - top)) + group
-            autos[0, slot, group], autos[1, slot, group] = products(left, left)
-            for part in range(2):
-                store(
-                    autos.at[part, slot, group],
-                    autos_hbm.at[part, at],
-                    auto_sems.at[part, slot, group],
-                )
+            place = jnp.where(pairing_ref[turn_at] == mask, turn_at, place)
+        for part in range(2):
+            copy = pltpu.make_async_copy(
+                vis.at[part, index], vis_hbm.at[part, place], vis_sems.at[part, index]
+            )
+            copy.start()
+            copies.append(copy)
     for copy in copies:
         copy.wait()
 
 
-def correlate(pairing, entries, masks, chan_count, block_bits, before=None):
-    half, slices, rows = entries[0][1][0].shape[-4:-1]
-    operands, layout = [], []
-    for kind, values in entries:
-        layout.append(kind)
-        operands += values
-    if layout[0] != "whole":
-        rows *= 2
-    with_autos = before is None
-    round_count = pairing.shape[0]
-    vis_shape = (2, len(masks), half, rows, rows)
-    auto_shape = (2, 2, half, rows, rows)
-    outs = [jax.ShapeDtypeStruct((2, round_count, half, rows, rows), jnp.float32)]
-    scratch = [
-        pltpu.VMEM((2, half, slices, rows, LANES), jnp.bfloat16),
-        pltpu.VMEM((len(masks), half, slices, rows, LANES), jnp.bfloat16),
-        pltpu.VMEM(vis_shape, jnp.float32),
-        pltpu.SemaphoreType.DMA(vis_shape[:3]),
-    ]
-    specs = [pl.BlockSpec(memory_space=pltpu.SMEM)]
-    specs += [pl.BlockSpec(memory_space=pltpu.VMEM)] * len(operands)
-    aliases = {}
-    if with_autos:
-        outs.append(jax.ShapeDtypeStruct((2, 2 * half, rows, rows), jnp.float32))
-        scratch += [pltpu.VMEM(auto_shape, jnp.float32), pltpu.SemaphoreType.DMA(auto_shape[:3])]
+SCRATCH = ("vis_hbm", "others", "vis", "pairing_ref", "vis_sems", "pairing_sem")
+
+
+def cross_call(pairing, block, received, early, late, chan_count, block_bits):
+    _, half, slices, rows, _ = block.shape
+    filled_shape = (len(early),) + block.shape[1:]
+    cost = functools.partial(pl.CostEstimate, transcendentals=0)
+    if received[early[0]][0] == "pair":
+        filled = []
+        for parity in range(2):
+            filled = vmem_call(
+                "fill_far" if parity else "fill_near",
+                functools.partial(fill_parity_kernel, chan_count, parity),
+                [filled_shape],
+                [received[mask][1][parity] for mask in early] + list(filled),
+                cost=cost(flops=(1 << 29, 4 << 28)[parity], bytes_accessed=(1 << 10, 1 << 20)[parity]),
+                aliases={len(early): 0} if parity else None,
+            )
     else:
-        aliases = {len(specs): 0}
-        specs.append(pl.BlockSpec(memory_space=pltpu.HBM))
-        operands = operands + [before]
-    flops = 16 * len(masks) * half * rows * rows * slices * LANES
+        filled = vmem_call(
+            "fill", fill_kernel, [filled_shape], [received[mask][1][0] for mask in early]
+        )
+    (filled,) = filled
+    layout = tuple(received[mask][0] for mask in late)
+    operands = [value for mask in late for value in received[mask][1]]
+    count = len(early) + len(late)
+    vis_shape = (2, count, half, rows, rows)
     return pl.pallas_call(
-        functools.partial(
-            correlate_kernel, chan_count, block_bits, masks, tuple(layout), with_autos
+        functools.partial(cross_kernel, chan_count, block_bits, early, late, layout),
+        out_shape=jax.ShapeDtypeStruct(vis_shape, jnp.float32),
+        in_specs=[pl.BlockSpec(memory_space=pltpu.HBM)]
+        + [pl.BlockSpec(memory_space=pltpu.VMEM)] * (2 + len(operands)),
+        out_specs=pl.BlockSpec(memory_space=pltpu.HBM),
+        scratch_shapes=[
+            pltpu.VMEM((len(late), half, slices, rows, LANES), jnp.bfloat16),
+            pltpu.VMEM(vis_shape, jnp.float32),
+            pltpu.SMEM(pairing.shape, jnp.int32),
+            pltpu.SemaphoreType.DMA(vis_shape[:2]),
+            pltpu.SemaphoreType.DMA(()),
+        ],
+        compiler_params=pltpu.CompilerParams(vmem_limit_bytes=16 * MIB),
+        cost_estimate=pl.CostEstimate(
+            flops=16 * count * half * rows * rows * slices * LANES,
+            bytes_accessed=4 << 20,
+            transcendentals=0,
         ),
-        out_shape=outs,
-        in_specs=specs,
-        out_specs=[pl.BlockSpec(memory_space=pltpu.HBM)] * len(outs),
-        scratch_shapes=scratch,
-        input_output_aliases=aliases,
-        compiler_params=pltpu.CompilerParams(vmem_limit_bytes=24 * MIB),
-        cost_estimate=pl.CostEstimate(flops=flops, bytes_accessed=4 << 20, transcendentals=0),
-        name="correlate" if with_autos else "correlate_rest",
-    )(pairing, *operands)
+        name="cross",
+    )(pairing, block, filled, *operands)
 
 
 def on_device(voltages, filter_taps, pairing):
@@ -469,34 +527,40 @@
         count = lax.axis_size(axis)
         return lax.ppermute(value, axis, [(i, i ^ mask) for i in range(count)])
 
-    evens = list(range(2, chan_count, 2))
+    evens = hops(chan_count)[1:]
+
+    def along(values):
+        return [exchange(value, "chan", k) for value, k in zip(values, evens)]
+
     own_moving, own_other, direct, held, relay_moving, relay_other = spectra_pieces(
         voltages, filter_taps, chan_count
     )
     part = own_moving.shape
     half = part[0]
     relay_moving = exchange(relay_moving, "chan", 1)
-    direct = [exchange(value, "chan", k) for value, k in zip(direct, evens)]
+    direct = along(direct)
     relay_other = exchange(relay_other, "chan", 1)
-    onward = vmem_call(
-        "split", split_kernel, [part] * len(evens), [relay_moving], []
+    far_own, *onward = vmem_call(
+        "split", split_kernel, [part] * (chan_count // 2), [relay_moving], []
     )
-    onward = [exchange(value, "chan", k) for value, k in zip(onward, evens)]
-    near, far = [own_moving] + direct, [relay_moving[0]] + onward
+    onward = along(onward)
+    near, far = [own_moving] + direct, [far_own] + onward
     laid = part[:2] + (chan_count // 2 * signals, LANES)
     whole_tiles = signals % ROWS == 0
-    if whole_tiles:
-        (near,) = vmem_call("near", lay_kernel, [laid], near, [])
-        (far,) = vmem_call("far", lay_relayed_kernel, [laid], [relay_moving] + onward, [])
-    else:
+    top_mask = inp_count // 2
+    if not whole_tiles:
+        ordered = np.argsort(hops(chan_count))
         sources = jnp.bitwise_xor(own_chan // 2, jnp.arange(chan_count // 2))
 
         def merge(parts):
+            parts = [parts[at] for at in ordered]
             return jnp.take(jnp.stack(parts, axis=2), sources, axis=2).reshape(laid)
 
-        near, far = merge(near), merge(far)
-    top_mask = inp_count // 2
-    crossed = [exchange(value, "inp", top_mask) for value in (near, far)]
+        near, far = [merge(near)], [merge(far)]
+    (near,) = vmem_call("near", lay_kernel, [laid], near, [])
+    crossed = [exchange(near, "inp", top_mask)]
+    (far,) = vmem_call("far", lay_kernel, [laid], far, [])
+    crossed.append(exchange(far, "inp", top_mask))
     rest = vmem_call(
         "hand_on",
         hand_on_kernel,
@@ -504,7 +568,7 @@
         [held, relay_other],
         [near],
     )
-    rest = [exchange(value, "chan", k) for value, k in zip(rest, evens)]
+    rest = along(rest)
     if whole_tiles:
         other_kernel = functools.partial(lay_rest_kernel, len(evens))
         others = [own_other, relay_other] + rest
@@ -551,17 +615,10 @@
         received = {mask: interleave(entry) for mask, entry in received.items()}
     early = [mask for mask in masks if top_bit(mask) == block_bits - 1]
     late = [mask for mask in masks if top_bit(mask) != block_bits - 1]
-    visibilities, autos = correlate(
-        pairing, block + [received[mask] for mask in early], early, chan_count, block_bits
+    rows, autos = autos_call(
+        [value for _, values in block for value in values], chan_count, block_bits, []
     )
-    (visibilities,) = correlate(
-        pairing,
-        block + [received[mask] for mask in late],
-        late,
-        chan_count,
-        block_bits,
-        visibilities,
-    )
+    visibilities = cross_call(pairing, rows, received, early, late, chan_count, block_bits)
     return (visibilities, autos)
 
 

time: 47.2 us -> 42.6 us (0.903)
  waiting for transfers between devices: 12.2 us -> 8.11 us
  Pallas kernels: 13.4 us -> 12.1 us
  starting transfers between devices: 20.8 us -> 21.5 us
    ppermute x16, waiting for transfers between devices: 12.2 us -> 8.11 us  [exchange(): return lax.ppermute(value, axis, [(i, i ^ mask) for i in range(count)])]
    pallas_call x2, Pallas kernels: 4.8 us -> 3.42 us  [the longest x1 1.92 us: cross_call(): pl.pallas_call(functools.partial(cross_kernel, chan_count, block_bits, ea...]
    ppermute x16, starting transfers between devices: 20.8 us -> 21.5 us  [exchange(): return lax.ppermute(value, axis, [(i, i ^ mask) for i in range(count)])]
  transfers between devices with their start and end apart: 16 -> 16, of which waited for: 6 -> 5; matrix products, arithmetic and copies ran while one was open for 0% -> 0% of each run, Pallas kernels for 7% -> 4%
where the time goes in v3:
time: 42.6 us; the launch traced here: 42.5 us
  starting transfers between devices  21.5 us (50%)
  Pallas kernels  12.1 us (28%)
  waiting for transfers between devices  8.11 us (19%)
  between operations  0.75 us (2%)
    ppermute x16, starting transfers between devices, exchange(): return lax.ppermute(value, axis, [(i, i ^ mask) for i in range(count)])  21.5 us
    pallas_call x1, Pallas kernels, spectra_pieces(): pl.pallas_call(functools.partial(spectra_kernel, chan_count, spectra_coun...  8.36 us
    ppermute x16, waiting for transfers between devices, exchange(): return lax.ppermute(value, axis, [(i, i ^ mask) for i in range(count)])  8.11 us
    pallas_call x1, Pallas kernels, cross_call(): pl.pallas_call(functools.partial(cross_kernel, chan_count, block_bits, ea...  1.92 us
    pallas_call x1, Pallas kernels, autos_call(): pl.pallas_call(functools.partial(autos_kernel, chan_count, block_bits, pa...  1.5 us
  transfers between devices with their start and end apart: 16, of which 5 were waited for; matrix products, arithmetic and copies ran while one was open for 0% of the time, Pallas kernels for 4%

profile of v3, /device:TPU:0, one launch (start us, length us, event | category | flops | bytes accessed | tf_op | source)
XLA Modules:
  0.0 42.5 jit_solution(17449474092063728594)
XLA Ops:
  0.6 8.4 %spectra.1 = (bf16[4,4,16,128]{3,2,1,0:T(8,128)(2,1)S(1)}, bf16[4,4,16,128]{3,2,1,0:T(8,128)(2,1)S(1)}, bf16[4,4,16,128]{3,2,1,0:T(8,128)(2,1)S(1)}, bf16[4,4,16...) custom-call(bf16[2,16,77824]{2,1,0:T(8,128)(2,1)} %volt_hbm.1, ...), custom_call_target="tpu_custom_call" | custom-call | tf_op jit(solution)/shard_map/spectra/pallas_call | solution.py:223
  9.0 3.0 %collective-permute-start.3 = (bf16[4,4,4,16,128]{4,3,2,1,0:T(8,128)(2,1)S(1)}, bf16[4,4,4,16,128]{4,3,2,1,0:T(8,128)(2,1)S(1)}, u32[]{:S(2)}, u32[]{:S(2)}) collective-permute-start(bf16[4,4,4,16,128]{4,3,2,1,0:T(8,128)(2,1)S(1)} %get-tuple-element.26), channel_id=1, source_target_pairs={{0,1},{1,0},{2,3},{3,2},{4,5},{5,4},{6,7},{7,6},{8,9},{9,8},{10,11... | collective-permute-start | bytes 786440 | tf_op jit(solution)/shard_map/ppermute | solution.py:528
  12.0 0.1 collective-permute-start.7
  12.1 3.0 %collective-permute-start = (bf16[4,4,16,128]{3,2,1,0:T(8,128)(2,1)S(1)}, bf16[4,4,16,128]{3,2,1,0:T(8,128)(2,1)S(1)}, u32[]{:S(2)}, u32[]{:S(2)}) collective-permute-start(bf16[4,4,16,128]{3,2,1,0:T(8,128)(2,1)S(1)} %get-tuple-element.23), channel_id=1, source_target_pairs={{0,4},{1,5},{2,6},{3,7},{4,0},{5,1},{6,2},{7,3},{8,12},{9,13},{10,... | collective-permute-start | bytes 196616 | tf_op jit(solution)/shard_map/ppermute | solution.py:528
  15.1 1.3 %collective-permute-start.1 = (bf16[4,4,16,128]{3,2,1,0:T(8,128)(2,1)S(1)}, bf16[4,4,16,128]{3,2,1,0:T(8,128)(2,1)S(1)}, u32[]{:S(2)}, u32[]{:S(2)}) collective-permute-start(bf16[4,4,16,128]{3,2,1,0:T(8,128)(2,1)S(1)} %get-tuple-element.24), channel_id=1, source_target_pairs={{0,6},{1,7},{2,4},{3,5},{4,2},{5,3},{6,0},{7,1},{8,14},{9,15},{10,... | collective-permute-start | bytes 196616 | tf_op jit(solution)/shard_map/ppermute | solution.py:528
  16.5 0.2 collective-permute-start.2
  16.7 2.5 %collective-permute-done.3.refs_0_ = bf16[4,4,4,16,128]{4,3,2,1,0:T(8,128)(2,1)S(1)} collective-permute-done((bf16[4,4,4,16,128]{4,3,2,1,0:T(8,128)(2,1)S(1)}, bf16[4,4,4,16,128]{4,3,2,1,0:T(8,128)(2,1)S(1)}, u32[]{:S(2)}, u32[]{:S(2)}) %collective-permute-start.3) | collective-permute-done | bytes 262176 | tf_op jit(solution)/shard_map/ppermute | solution.py:528
  19.2 3.2 %collective-permute-start.4 = (bf16[4,4,16,128]{3,2,1,0:T(8,128)(2,1)S(1)}, bf16[4,4,16,128]{3,2,1,0:T(8,128)(2,1)S(1)}, u32[]{:S(2)}, u32[]{:S(2)}) collective-permute-start(bf16[4,4,16,128]{3,2,1,0:T(8,128)(2,1)S(1)} %get-tuple-element.28), channel_id=1, source_target_pairs={{0,4},{1,5},{2,6},{3,7},{4,0},{5,1},{6,2},{7,3},{8,12},{9,13},{10,... | collective-permute-start | bytes 196616 | tf_op jit(solution)/shard_map/ppermute | solution.py:528
  22.4 0.0 collective-permute-done.refs_1_
  22.4 1.3 %collective-permute-start.5 = (bf16[4,4,16,128]{3,2,1,0:T(8,128)(2,1)S(1)}, bf16[4,4,16,128]{3,2,1,0:T(8,128)(2,1)S(1)}, u32[]{:S(2)}, u32[]{:S(2)}) collective-permute-start(bf16[4,4,16,128]{3,2,1,0:T(8,128)(2,1)S(1)} %get-tuple-element.29), channel_id=1, source_target_pairs={{0,6},{1,7},{2,4},{3,5},{4,2},{5,3},{6,0},{7,1},{8,14},{9,15},{10,... | collective-permute-start | bytes 196616 | tf_op jit(solution)/shard_map/ppermute | solution.py:528
  23.7 0.0 collective-permute-done.1.refs_2_
  23.7 0.3 collective-permute-start.6
  24.0 0.0 collective-permute-done.2.refs_3_
  24.1 1.6 %collective-permute-start.13 = (bf16[4,4,64,128]{3,2,1,0:T(8,128)(2,1)S(1)}, bf16[4,4,64,128]{3,2,1,0:T(8,128)(2,1)S(1)}, u32[]{:S(2)}, u32[]{:S(2)}) collective-permute-start(bf16[4,4,64,128]{3,2,1,0:T(8,128)(2,1)S(1)} %near.1.refs_2_.refs_0_), channel_id=1, source_target_pairs={{0,16},{8,24},{16,0},{24,8},{1,17},{9,25},{17,1},{25,9},{2,18},{10... | collective-permute-start | bytes 786440 | tf_op jit(solution)/shard_map/ppermute | solution.py:528
  25.6 0.0 collective-permute-done.7.refs_1_.refs_3_
  25.7 0.0 copy-start
  25.7 2.8 %collective-permute-start.8 = (bf16[2,4,4,16,128]{4,3,2,1,0:T(8,128)(2,1)S(1)}, bf16[2,4,4,16,128]{4,3,2,1,0:T(8,128)(2,1)S(1)}, u32[]{:S(2)}, u32[]{:S(2)}) collective-permute-start(bf16[2,4,4,16,128]{4,3,2,1,0:T(8,128)(2,1)S(1)} %get-tuple-element.34), channel_id=1, source_target_pairs={{0,4},{1,5},{2,6},{3,7},{4,0},{5,1},{6,2},{7,3},{8,12},{9,13},{10,... | collective-permute-start | bytes 393224 | tf_op jit(solution)/shard_map/ppermute | solution.py:528
  28.5 0.0 collective-permute-done.4.refs_1_
  28.5 1.4 %collective-permute-start.9 = (bf16[2,4,4,16,128]{4,3,2,1,0:T(8,128)(2,1)S(1)}, bf16[2,4,4,16,128]{4,3,2,1,0:T(8,128)(2,1)S(1)}, u32[]{:S(2)}, u32[]{:S(2)}) collective-permute-start(bf16[2,4,4,16,128]{4,3,2,1,0:T(8,128)(2,1)S(1)} %get-tuple-element.35), channel_id=1, source_target_pairs={{0,6},{1,7},{2,4},{3,5},{4,2},{5,3},{6,0},{7,1},{8,14},{9,15},{10,... | collective-permute-start | bytes 393224 | tf_op jit(solution)/shard_map/ppermute | solution.py:528
  29.8 0.0 collective-permute-done.5.refs_2_
  29.8 1.0 %collective-permute-start.10 = (bf16[2,4,4,16,128]{4,3,2,1,0:T(8,128)(2,1)S(1)}, bf16[2,4,4,16,128]{4,3,2,1,0:T(8,128)(2,1)S(1)}, u32[]{:S(2)}, u32[]{:S(2)}) collective-permute-start(bf16[2,4,4,16,128]{4,3,2,1,0:T(8,128)(2,1)S(1)} %get-tuple-element.36), channel_id=1, source_target_pairs={{0,2},{1,3},{2,0},{3,1},{4,6},{5,7},{6,4},{7,5},{8,10},{9,11},{10,... | collective-permute-start | bytes 393224 | tf_op jit(solution)/shard_map/ppermute | solution.py:528
  30.8 0.0 collective-permute-done.6.refs_3_
  30.9 1.6 %collective-permute-start.11 = (bf16[4,4,64,128]{3,2,1,0:T(8,128)(2,1)S(1)}, bf16[4,4,64,128]{3,2,1,0:T(8,128)(2,1)S(1)}, u32[]{:S(2)}, u32[]{:S(2)}) collective-permute-start(bf16[4,4,64,128]{3,2,1,0:T(8,128)(2,1)S(1)} %far.1.refs_1_), channel_id=1, source_target_pairs={{0,16},{8,24},{16,0},{24,8},{1,17},{9,25},{17,1},{25,9},{2,18},{10... | collective-permute-start | bytes 786440 | tf_op jit(solution)/shard_map/ppermute | solution.py:528
  32.5 5.0 %collective-permute-done.8.refs_4_ = bf16[2,4,4,16,128]{4,3,2,1,0:T(8,128)(2,1)S(1)} collective-permute-done((bf16[2,4,4,16,128]{4,3,2,1,0:T(8,128)(2,1)S(1)}, bf16[2,4,4,16,128]{4,3,2,1,0:T(8,128)(2,1)S(1)}, u32[]{:S(2)}, u32[]{:S(2)}) %collective-permute-start.8) | collective-permute-done | bytes 131104 | tf_op jit(solution)/shard_map/ppermute | solution.py:528
  37.5 0.0 collective-permute-done.9.refs_5_
  37.5 0.1 collective-permute-done.10.refs_6_
  37.6 0.1 other.1
  37.7 0.1 collective-permute-start.15
  37.8 0.0 collective-permute-done.13.refs_0_
  37.8 0.5 %collective-permute-start.14 = (bf16[4,4,64,128]{3,2,1,0:T(8,128)(2,1)S(1)}, bf16[4,4,64,128]{3,2,1,0:T(8,128)(2,1)S(1)}, u32[]{:S(2)}, u32[]{:S(2)}) collective-permute-start(bf16[4,4,64,128]{3,2,1,0:T(8,128)(2,1)S(1)} %collective-permute-done.13.refs_0_), channel_id=1, source_target_pairs={{0,8},{8,0},{16,24},{24,16},{1,9},{9,1},{17,25},{25,17},{2,10},{10... | collective-permute-start | bytes 786440 | tf_op jit(solution)/shard_map/ppermute | solution.py:528
  38.3 0.0 collective-permute-done.11.refs_0_
  38.3 0.1 collective-permute-start.12
  38.4 1.5 %autos.1 = (bf16[2,4,4,128,128]{4,3,2,1,0:T(8,128)(2,1)S(1)}, f32[2,8,128,128]{3,2,1,0:T(8,128)}) custom-call(bf16[4,4,64,128]{3,2,1,0:T(8,128)(2,1)S(1)} %near.1.refs_2_.refs_0_, bf16[4,4,64,128]{3,2,1,0:T(8,128)(2,1)S(1)} %far.1.refs_1_, bf16[4,4,64,128]{3,2,1,0:T(8,128)(2,1)S(1)} %get-tuple-element.37.refs_2_, ...), custom_call_target="tpu_custom_call" | custom-call | flops 536870912 | bytes 4194304 | tf_op jit(solution)/shard_map/autos/pallas_call | solution.py:388
  39.9 0.2 collective-permute-done.14.refs_1_
  40.1 0.1 fill_near.1.refs_2_
  40.2 0.3 collective-permute-done.12.refs_1_
  40.5 0.1 fill_far.1.filled
  40.5 0.0 collective-permute-done.15.refs_0_
  40.6 0.0 copy-done
  40.6 1.9 %cross.1 = f32[2,3,4,128,128]{4,3,2,1,0:T(8,128)} custom-call(s32[3]{0:T(128)S(1)} %copy-done, bf16[2,4,4,128,128]{4,3,2,1,0:T(8,128)(2,1)S(1)} %get-tuple-element.39.block, bf16[2,4,4,128,128]{4,3,2,1,0:T(8,128)(2,1)S(1)} %fill_far.1.filled, bf16[2,4,4,64,128]{4,3,2,1,0:T(8,128)(2,1)S(1)} %collective-permute-done.15.refs_0_), custom_call_target="tpu_custom_call" | custom-call | flops 1610612736 | bytes 4194304 | tf_op jit(solution)/shard_map/cross/pallas_call | solution.py:496
  (4 shorter events, 0.1 us)
Async XLA Ops:
  9.0 10.2 %collective-permute-start.3 = (bf16[4,4,4,16,128]{4,3,2,1,0:T(8,128)(2,1)S(1)}, bf16[4,4,4,16,128]{4,3,2,1,0:T(8,128)(2,1)S(1)}, u32[]{:S(2)}, u32[]{:S(2)}) collective-permute-start(bf16[4,4,4,16,128]{4,3,2,1,0:T(8,128)(2,1)S(1)} %get-tuple-element.26), channel_id=1, source_target_pairs={{0,1},{1,0},{2,3},{3,2},{4,5},{5,4},{6,7},{7,6},{8,9},{9,8},{10,11... | collective-permute-start | bytes 786440 | tf_op jit(solution)/shard_map/ppermute | solution.py:528
  12.0 13.6 %collective-permute-start.7 = (bf16[4,4,4,16,128]{4,3,2,1,0:T(8,128)(2,1)}, bf16[4,4,4,16,128]{4,3,2,1,0:T(8,128)(2,1)S(1)}, u32[]{:S(2)}, u32[]{:S(2)}) collective-permute-start(bf16[4,4,4,16,128]{4,3,2,1,0:T(8,128)(2,1)} %get-tuple-element.32), channel_id=1, source_target_pairs={{0,1},{1,0},{2,3},{3,2},{4,5},{5,4},{6,7},{7,6},{8,9},{9,8},{10,11... | collective-permute-start | bytes 786440 | tf_op jit(solution)/shard_map/ppermute | solution.py:528
  12.1 10.3 %collective-permute-start = (bf16[4,4,16,128]{3,2,1,0:T(8,128)(2,1)S(1)}, bf16[4,4,16,128]{3,2,1,0:T(8,128)(2,1)S(1)}, u32[]{:S(2)}, u32[]{:S(2)}) collective-permute-start(bf16[4,4,16,128]{3,2,1,0:T(8,128)(2,1)S(1)} %get-tuple-element.23), channel_id=1, source_target_pairs={{0,4},{1,5},{2,6},{3,7},{4,0},{5,1},{6,2},{7,3},{8,12},{9,13},{10,... | collective-permute-start | bytes 196616 | tf_op jit(solution)/shard_map/ppermute | solution.py:528
  15.1 8.6 %collective-permute-start.1 = (bf16[4,4,16,128]{3,2,1,0:T(8,128)(2,1)S(1)}, bf16[4,4,16,128]{3,2,1,0:T(8,128)(2,1)S(1)}, u32[]{:S(2)}, u32[]{:S(2)}) collective-permute-start(bf16[4,4,16,128]{3,2,1,0:T(8,128)(2,1)S(1)} %get-tuple-element.24), channel_id=1, source_target_pairs={{0,6},{1,7},{2,4},{3,5},{4,2},{5,3},{6,0},{7,1},{8,14},{9,15},{10,... | collective-permute-start | bytes 196616 | tf_op jit(solution)/shard_map/ppermute | solution.py:528
  16.5 7.6 %collective-permute-start.2 = (bf16[4,4,16,128]{3,2,1,0:T(8,128)(2,1)S(1)}, bf16[4,4,16,128]{3,2,1,0:T(8,128)(2,1)S(1)}, u32[]{:S(2)}, u32[]{:S(2)}) collective-permute-start(bf16[4,4,16,128]{3,2,1,0:T(8,128)(2,1)S(1)} %get-tuple-element.25), channel_id=1, source_target_pairs={{0,2},{1,3},{2,0},{3,1},{4,6},{5,7},{6,4},{7,5},{8,10},{9,11},{10,... | collective-permute-start | bytes 196616 | tf_op jit(solution)/shard_map/ppermute | solution.py:528
  19.2 9.3 %collective-permute-start.4 = (bf16[4,4,16,128]{3,2,1,0:T(8,128)(2,1)S(1)}, bf16[4,4,16,128]{3,2,1,0:T(8,128)(2,1)S(1)}, u32[]{:S(2)}, u32[]{:S(2)}) collective-permute-start(bf16[4,4,16,128]{3,2,1,0:T(8,128)(2,1)S(1)} %get-tuple-element.28), channel_id=1, source_target_pairs={{0,4},{1,5},{2,6},{3,7},{4,0},{5,1},{6,2},{7,3},{8,12},{9,13},{10,... | collective-permute-start | bytes 196616 | tf_op jit(solution)/shard_map/ppermute | solution.py:528
  22.4 7.5 %collective-permute-start.5 = (bf16[4,4,16,128]{3,2,1,0:T(8,128)(2,1)S(1)}, bf16[4,4,16,128]{3,2,1,0:T(8,128)(2,1)S(1)}, u32[]{:S(2)}, u32[]{:S(2)}) collective-permute-start(bf16[4,4,16,128]{3,2,1,0:T(8,128)(2,1)S(1)} %get-tuple-element.29), channel_id=1, source_target_pairs={{0,6},{1,7},{2,4},{3,5},{4,2},{5,3},{6,0},{7,1},{8,14},{9,15},{10,... | collective-permute-start | bytes 196616 | tf_op jit(solution)/shard_map/ppermute | solution.py:528
  23.7 7.1 %collective-permute-start.6 = (bf16[4,4,16,128]{3,2,1,0:T(8,128)(2,1)S(1)}, bf16[4,4,16,128]{3,2,1,0:T(8,128)(2,1)S(1)}, u32[]{:S(2)}, u32[]{:S(2)}) collective-permute-start(bf16[4,4,16,128]{3,2,1,0:T(8,128)(2,1)S(1)} %get-tuple-element.30), channel_id=1, source_target_pairs={{0,2},{1,3},{2,0},{3,1},{4,6},{5,7},{6,4},{7,5},{8,10},{9,11},{10,... | collective-permute-start | bytes 196616 | tf_op jit(solution)/shard_map/ppermute | solution.py:528
  24.1 13.8 %collective-permute-start.13 = (bf16[4,4,64,128]{3,2,1,0:T(8,128)(2,1)S(1)}, bf16[4,4,64,128]{3,2,1,0:T(8,128)(2,1)S(1)}, u32[]{:S(2)}, u32[]{:S(2)}) collective-permute-start(bf16[4,4,64,128]{3,2,1,0:T(8,128)(2,1)S(1)} %near.1.refs_2_.refs_0_), channel_id=1, source_target_pairs={{0,16},{8,24},{16,0},{24,8},{1,17},{9,25},{17,1},{25,9},{2,18},{10... | collective-permute-start | bytes 786440 | tf_op jit(solution)/shard_map/ppermute | solution.py:528
  25.7 14.9 %copy-start = (s32[3]{0:T(128)S(1)}, s32[3]{0:T(128)}, u32[]{:S(2)}) copy-start(s32[3]{0:T(128)} %pairing_hbm.1) | copy-start | bytes 40
  25.7 11.8 %collective-permute-start.8 = (bf16[2,4,4,16,128]{4,3,2,1,0:T(8,128)(2,1)S(1)}, bf16[2,4,4,16,128]{4,3,2,1,0:T(8,128)(2,1)S(1)}, u32[]{:S(2)}, u32[]{:S(2)}) collective-permute-start(bf16[2,4,4,16,128]{4,3,2,1,0:T(8,128)(2,1)S(1)} %get-tuple-element.34), channel_id=1, source_target_pairs={{0,4},{1,5},{2,6},{3,7},{4,0},{5,1},{6,2},{7,3},{8,12},{9,13},{10,... | collective-permute-start | bytes 393224 | tf_op jit(solution)/shard_map/ppermute | solution.py:528
  28.5 9.0 %collective-permute-start.9 = (bf16[2,4,4,16,128]{4,3,2,1,0:T(8,128)(2,1)S(1)}, bf16[2,4,4,16,128]{4,3,2,1,0:T(8,128)(2,1)S(1)}, u32[]{:S(2)}, u32[]{:S(2)}) collective-permute-start(bf16[2,4,4,16,128]{4,3,2,1,0:T(8,128)(2,1)S(1)} %get-tuple-element.35), channel_id=1, source_target_pairs={{0,6},{1,7},{2,4},{3,5},{4,2},{5,3},{6,0},{7,1},{8,14},{9,15},{10,... | collective-permute-start | bytes 393224 | tf_op jit(solution)/shard_map/ppermute | solution.py:528
  29.8 7.8 %collective-permute-start.10 = (bf16[2,4,4,16,128]{4,3,2,1,0:T(8,128)(2,1)S(1)}, bf16[2,4,4,16,128]{4,3,2,1,0:T(8,128)(2,1)S(1)}, u32[]{:S(2)}, u32[]{:S(2)}) collective-permute-start(bf16[2,4,4,16,128]{4,3,2,1,0:T(8,128)(2,1)S(1)} %get-tuple-element.36), channel_id=1, source_target_pairs={{0,2},{1,3},{2,0},{3,1},{4,6},{5,7},{6,4},{7,5},{8,10},{9,11},{10,... | collective-permute-start | bytes 393224 | tf_op jit(solution)/shard_map/ppermute | solution.py:528
  30.9 7.5 %collective-permute-start.11 = (bf16[4,4,64,128]{3,2,1,0:T(8,128)(2,1)S(1)}, bf16[4,4,64,128]{3,2,1,0:T(8,128)(2,1)S(1)}, u32[]{:S(2)}, u32[]{:S(2)}) collective-permute-start(bf16[4,4,64,128]{3,2,1,0:T(8,128)(2,1)S(1)} %far.1.refs_1_), channel_id=1, source_target_pairs={{0,16},{8,24},{16,0},{24,8},{1,17},{9,25},{17,1},{25,9},{2,18},{10... | collective-permute-start | bytes 786440 | tf_op jit(solution)/shard_map/ppermute | solution.py:528
  37.7 2.8 %collective-permute-start.15 = (bf16[2,4,4,64,128]{4,3,2,1,0:T(8,128)(2,1)S(1)}, bf16[2,4,4,64,128]{4,3,2,1,0:T(8,128)(2,1)S(1)}, u32[]{:S(2)}, u32[]{:S(2)}) collective-permute-start(bf16[2,4,4,64,128]{4,3,2,1,0:T(8,128)(2,1)S(1)} %get-tuple-element.40), channel_id=1, source_target_pairs={{0,8},{8,0},{16,24},{24,16},{1,9},{9,1},{17,25},{25,17},{2,10},{10... | collective-permute-start | bytes 1572872 | tf_op jit(solution)/shard_map/ppermute | solution.py:528
  37.8 2.3 %collective-permute-start.14 = (bf16[4,4,64,128]{3,2,1,0:T(8,128)(2,1)S(1)}, bf16[4,4,64,128]{3,2,1,0:T(8,128)(2,1)S(1)}, u32[]{:S(2)}, u32[]{:S(2)}) collective-permute-start(bf16[4,4,64,128]{3,2,1,0:T(8,128)(2,1)S(1)} %collective-permute-done.13.refs_0_), channel_id=1, source_target_pairs={{0,8},{8,0},{16,24},{24,16},{1,9},{9,1},{17,25},{25,17},{2,10},{10... | collective-permute-start | bytes 786440 | tf_op jit(solution)/shard_map/ppermute | solution.py:528
  38.3 2.1 %collective-permute-start.12 = (bf16[4,4,64,128]{3,2,1,0:T(8,128)(2,1)S(1)}, bf16[4,4,64,128]{3,2,1,0:T(8,128)(2,1)S(1)}, u32[]{:S(2)}, u32[]{:S(2)}) collective-permute-start(bf16[4,4,64,128]{3,2,1,0:T(8,128)(2,1)S(1)} %collective-permute-done.11.refs_0_), channel_id=1, source_target_pairs={{0,8},{8,0},{16,24},{24,16},{1,9},{9,1},{17,25},{25,17},{2,10},{10... | collective-permute-start | bytes 786440 | tf_op jit(solution)/shard_map/ppermute | solution.py:528

commit v4 on v3

--- a/solution.py
+++ b/solution.py
@@ -86,47 +86,63 @@
     return [0] + sorted(range(2, count, 2), key=lambda hop: (-top_bit(hop), hop))
 
 
+def frame_loads(frame_count):
+    bounds = [0] + list(range(5, frame_count, 7)) + [frame_count]
+    return list(zip(bounds[:-1], bounds[1:]))
+
+
 def spectra_kernel(chan_count, spectra_count, volt_hbm, taps_hbm, table_hbm, *refs):
     outs, scratch = refs[:-10], refs[-10:]
     volt_ref, taps_ref, table_ref, matrix_ref = scratch[:4]
     filtered, first, last, pieces, volt_sems, table_sems = scratch[4:]
     tap_count, fine = taps_ref.shape
     frame_count = spectra_count + tap_count - 1
-    volt_copies = [
-        pltpu.make_async_copy(volt_hbm.at[part], volt_ref.at[part], volt_sems.at[part])
-        for part in range(2)
-    ]
+    loads = frame_loads(frame_count)
+    volt_copies = []
+    for at, (begin, end) in enumerate(loads):
+        span = pl.ds(begin * fine, (end - begin) * fine)
+        volt_copies.append(
+            pltpu.make_async_copy(
+                volt_hbm.at[:, :, span], volt_ref.at[:, :, span], volt_sems.at[at]
+            )
+        )
     table_copies = [
         pltpu.make_async_copy(source, target, table_sems.at[at])
         for at, (source, target) in enumerate(
             [(taps_hbm, taps_ref), (table_hbm, table_ref)]
         )
     ]
+    volt_copies[0].start()
     table_copies[0].start()
-    volt_copies[0].start()
-    volt_copies[1].start()
+    for copy in volt_copies[1:]:
+        copy.start()
     table_copies[1].start()
-    table_copies[0].wait()
-    for part in range(2):
-        volt_copies[part].wait()
-
-        def filter_column(p, carry, part=part):
+    for at, (begin, end) in enumerate(loads):
+        if at == 0:
+            table_copies[0].wait()
+        volt_copies[at].wait()
+
+        def filter_column(p, carry, begin=begin, end=end):
             column = pl.multiple_of(p * LANES, LANES)
-            taps = [taps_ref[pl.ds(t, 1), pl.ds(column, LANES)] for t in range(tap_count)]
-            sums = [None] * spectra_count
-            for frame in range(frame_count):
-                at = pl.multiple_of(frame * fine + column, LANES)
-                values = volt_ref[part, :, pl.ds(at, LANES)].astype(jnp.float32)
-                for s in range(spectra_count):
-                    t = frame - s
-                    if 0 <= t < tap_count:
-                        term = taps[t] * values
-                        sums[s] = term if sums[s] is None else sums[s] + term
-            for s in range(spectra_count):
-                filtered[s, part, p] = sums[s]
+            taps = {}
+            for t in range(max(0, begin - spectra_count + 1), min(tap_count, end)):
+                taps[t] = taps_ref[pl.ds(t, 1), pl.ds(column, LANES)]
+            for part in range(2):
+                sums = {}
+                for frame in range(begin, end):
+                    lane = pl.multiple_of(frame * fine + column, LANES)
+                    values = volt_ref[part, :, pl.ds(lane, LANES)].astype(jnp.float32)
+                    for s in range(spectra_count):
+                        if 0 <= frame - s < tap_count:
+                            term = taps[frame - s] * values
+                            if s not in sums and frame > s:
+                                sums[s] = filtered[s, part, p]
+                            sums[s] = sums[s] + term if s in sums else term
+                for s, total in sums.items():
+                    filtered[s, part, p] = total
             return carry
 
-        lax.fori_loop(0, OUTER, filter_column, 0)
+        lax.fori_loop(0, OUTER, filter_column, 0, unroll=4)
     table_copies[1].wait()
     table = table_ref[pl.ds(0, 2 * LANES), :]
     matrix_ref[0] = table.astype(jnp.bfloat16)
@@ -139,7 +155,7 @@
                 real, imag = turn(values[r], a * r, OUTER)
                 first[0, r, a] = real
                 first[1, r, a] = imag
-        odd = lax.rem(s, 2)
+        odd = s % 2
         for r in range(4):
             values = eight([(first[0, r, a], first[1, r, a]) for a in range(8)])
             highs, lows = [], []
@@ -163,33 +179,35 @@
                 last[s, 1, r + 4 * t] = rows[:, LANES:]
         return carry
 
-    lax.fori_loop(0, spectra_count, transform, 0)
 
     lane = lax.broadcasted_iota(jnp.int32, (ROWS, LANES), 1)
     bits = [(lane >> bit) & 1 == 1 for bit in range(7)]
     group_count = pieces.shape[1]
 
-    def regroup(part, carry):
-        for pair in range(spectra_count // 2):
-            even = [last[2 * pair, part, k1] for k1 in range(OUTER)]
-            odd = [last[2 * pair + 1, part, k1] for k1 in range(OUTER)]
-            mixed = [
-                [jnp.where(bits[1], odd[v], even[v]) for v in range(OUTER)],
-                [jnp.where(bits[1], even[v], odd[v - 1]) for v in range(OUTER)],
-            ]
-            for which in range(2):
-                tiles = [mixed[which][-v % OUTER] for v in range(OUTER)]
-                for bit in range(5):
-                    tiles = [
-                        jnp.where(bits[2 + bit], tiles[v - (1 << bit)], tiles[v])
-                        for v in range(OUTER)
-                    ]
-                for u in range(OUTER):
-                    chan, group = divmod(2 * u + which, group_count)
-                    pieces[chan, group, part * (spectra_count // 2) + pair] = tiles[u]
-        return carry
-
-    lax.fori_loop(0, 2, regroup, 0)
+    def regroup(part, pair):
+        even = [last[2 * pair, part, k1] for k1 in range(OUTER)]
+        odd = [last[2 * pair + 1, part, k1] for k1 in range(OUTER)]
+        mixed = [
+            [jnp.where(bits[1], odd[v], even[v]) for v in range(OUTER)],
+            [jnp.where(bits[1], even[v], odd[v - 1]) for v in range(OUTER)],
+        ]
+        for which in range(2):
+            tiles = [mixed[which][-v % OUTER] for v in range(OUTER)]
+            for bit in range(5):
+                tiles = [
+                    jnp.where(bits[2 + bit], tiles[v - (1 << bit)], tiles[v])
+                    for v in range(OUTER)
+                ]
+            for u in range(OUTER):
+                chan, group = divmod(2 * u + which, group_count)
+                pieces[chan, group, part * (spectra_count // 2) + pair] = tiles[u]
+
+    for s in range(spectra_count):
+        transform(s, 0)
+        if s % 2:
+            regroup(0, s // 2)
+            regroup(1, s // 2)
+
     own = lax.axis_index("chan")
     top = bit_of(lax.axis_index("inp"), top_bit(lax.axis_size("inp")) - 1)
     half = group_count // 2
@@ -234,7 +252,7 @@
             pltpu.VMEM((2, 4, 8, ROWS, LANES), jnp.float32),
             pltpu.VMEM((spectra_count, 2, OUTER, ROWS, LANES), jnp.bfloat16),
             pltpu.VMEM((chan_count,) + piece, jnp.bfloat16),
-            pltpu.SemaphoreType.DMA((2,)),
+            pltpu.SemaphoreType.DMA((len(frame_loads(spectra_count + tap_count - 1)),)),
             pltpu.SemaphoreType.DMA((2,)),
         ],
         compiler_params=pltpu.CompilerParams(vmem_limit_bytes=53 * MIB),

time: 42.6 us -> 41.2 us (0.967)
  Pallas kernels: 12.1 us -> 10.7 us
    pallas_call x1, Pallas kernels: 8.36 us -> 6.93 us  [spectra_pieces(): pl.pallas_call(functools.partial(spectra_kernel, chan_count, spectra_coun...]
where the time goes in v4:
time: 41.2 us; the launch traced here: 41.1 us
  starting transfers between devices  21.5 us (52%)
  Pallas kernels  10.7 us (26%)
  waiting for transfers between devices  8.11 us (20%)
  between operations  0.75 us (2%)
    ppermute x16, starting transfers between devices, exchange(): return lax.ppermute(value, axis, [(i, i ^ mask) for i in range(count)])  21.5 us
    ppermute x16, waiting for transfers between devices, exchange(): return lax.ppermute(value, axis, [(i, i ^ mask) for i in range(count)])  8.11 us
    pallas_call x1, Pallas kernels, spectra_pieces(): pl.pallas_call(functools.partial(spectra_kernel, chan_count, spectra_coun...  6.93 us
    pallas_call x1, Pallas kernels, cross_call(): pl.pallas_call(functools.partial(cross_kernel, chan_count, block_bits, ea...  1.92 us
    pallas_call x1, Pallas kernels, autos_call(): pl.pallas_call(functools.partial(autos_kernel, chan_count, block_bits, pa...  1.5 us
  transfers between devices with their start and end apart: 16, of which 5 were waited for; matrix products, arithmetic and copies ran while one was open for 0% of the time, Pallas kernels for 4%

profile of v4, /device:TPU:0, one launch (start us, length us, event | category | flops | bytes accessed | tf_op | source)
XLA Modules:
  0.0 41.1 jit_solution(13957234482093538448)
XLA Ops:
  0.6 6.9 %spectra.1 = (bf16[4,4,16,128]{3,2,1,0:T(8,128)(2,1)S(1)}, bf16[4,4,16,128]{3,2,1,0:T(8,128)(2,1)S(1)}, bf16[4,4,16,128]{3,2,1,0:T(8,128)(2,1)S(1)}, bf16[4,4,16...) custom-call(bf16[2,16,77824]{2,1,0:T(8,128)(2,1)} %volt_hbm.1, ...), custom_call_target="tpu_custom_call" | custom-call | tf_op jit(solution)/shard_map/spectra/pallas_call | solution.py:241
  7.6 3.0 %collective-permute-start.3 = (bf16[4,4,4,16,128]{4,3,2,1,0:T(8,128)(2,1)S(1)}, bf16[4,4,4,16,128]{4,3,2,1,0:T(8,128)(2,1)S(1)}, u32[]{:S(2)}, u32[]{:S(2)}) collective-permute-start(bf16[4,4,4,16,128]{4,3,2,1,0:T(8,128)(2,1)S(1)} %get-tuple-element.26), channel_id=1, source_target_pairs={{0,1},{1,0},{2,3},{3,2},{4,5},{5,4},{6,7},{7,6},{8,9},{9,8},{10,11... | collective-permute-start | bytes 786440 | tf_op jit(solution)/shard_map/ppermute | solution.py:546
  10.6 0.1 collective-permute-start.7
  10.7 3.0 %collective-permute-start = (bf16[4,4,16,128]{3,2,1,0:T(8,128)(2,1)S(1)}, bf16[4,4,16,128]{3,2,1,0:T(8,128)(2,1)S(1)}, u32[]{:S(2)}, u32[]{:S(2)}) collective-permute-start(bf16[4,4,16,128]{3,2,1,0:T(8,128)(2,1)S(1)} %get-tuple-element.23), channel_id=1, source_target_pairs={{0,4},{1,5},{2,6},{3,7},{4,0},{5,1},{6,2},{7,3},{8,12},{9,13},{10,... | collective-permute-start | bytes 196616 | tf_op jit(solution)/shard_map/ppermute | solution.py:546
  13.7 1.3 %collective-permute-start.1 = (bf16[4,4,16,128]{3,2,1,0:T(8,128)(2,1)S(1)}, bf16[4,4,16,128]{3,2,1,0:T(8,128)(2,1)S(1)}, u32[]{:S(2)}, u32[]{:S(2)}) collective-permute-start(bf16[4,4,16,128]{3,2,1,0:T(8,128)(2,1)S(1)} %get-tuple-element.24), channel_id=1, source_target_pairs={{0,6},{1,7},{2,4},{3,5},{4,2},{5,3},{6,0},{7,1},{8,14},{9,15},{10,... | collective-permute-start | bytes 196616 | tf_op jit(solution)/shard_map/ppermute | solution.py:546
  15.0 0.2 collective-permute-start.2
  15.3 2.5 %collective-permute-done.3.refs_0_ = bf16[4,4,4,16,128]{4,3,2,1,0:T(8,128)(2,1)S(1)} collective-permute-done((bf16[4,4,4,16,128]{4,3,2,1,0:T(8,128)(2,1)S(1)}, bf16[4,4,4,16,128]{4,3,2,1,0:T(8,128)(2,1)S(1)}, u32[]{:S(2)}, u32[]{:S(2)}) %collective-permute-start.3) | collective-permute-done | bytes 262176 | tf_op jit(solution)/shard_map/ppermute | solution.py:546
  17.8 3.2 %collective-permute-start.4 = (bf16[4,4,16,128]{3,2,1,0:T(8,128)(2,1)S(1)}, bf16[4,4,16,128]{3,2,1,0:T(8,128)(2,1)S(1)}, u32[]{:S(2)}, u32[]{:S(2)}) collective-permute-start(bf16[4,4,16,128]{3,2,1,0:T(8,128)(2,1)S(1)} %get-tuple-element.28), channel_id=1, source_target_pairs={{0,4},{1,5},{2,6},{3,7},{4,0},{5,1},{6,2},{7,3},{8,12},{9,13},{10,... | collective-permute-start | bytes 196616 | tf_op jit(solution)/shard_map/ppermute | solution.py:546
  21.0 0.0 collective-permute-done.refs_1_
  21.0 1.4 %collective-permute-start.5 = (bf16[4,4,16,128]{3,2,1,0:T(8,128)(2,1)S(1)}, bf16[4,4,16,128]{3,2,1,0:T(8,128)(2,1)S(1)}, u32[]{:S(2)}, u32[]{:S(2)}) collective-permute-start(bf16[4,4,16,128]{3,2,1,0:T(8,128)(2,1)S(1)} %get-tuple-element.29), channel_id=1, source_target_pairs={{0,6},{1,7},{2,4},{3,5},{4,2},{5,3},{6,0},{7,1},{8,14},{9,15},{10,... | collective-permute-start | bytes 196616 | tf_op jit(solution)/shard_map/ppermute | solution.py:546
  22.3 0.0 collective-permute-done.1.refs_2_
  22.3 0.3 collective-permute-start.6
  22.6 0.0 collective-permute-done.2.refs_3_
  22.6 1.6 %collective-permute-start.13 = (bf16[4,4,64,128]{3,2,1,0:T(8,128)(2,1)S(1)}, bf16[4,4,64,128]{3,2,1,0:T(8,128)(2,1)S(1)}, u32[]{:S(2)}, u32[]{:S(2)}) collective-permute-start(bf16[4,4,64,128]{3,2,1,0:T(8,128)(2,1)S(1)} %near.1.refs_2_.refs_0_), channel_id=1, source_target_pairs={{0,16},{8,24},{16,0},{24,8},{1,17},{9,25},{17,1},{25,9},{2,18},{10... | collective-permute-start | bytes 786440 | tf_op jit(solution)/shard_map/ppermute | solution.py:546
  24.2 0.0 collective-permute-done.7.refs_1_.refs_3_
  24.2 0.0 copy-start
  24.3 2.8 %collective-permute-start.8 = (bf16[2,4,4,16,128]{4,3,2,1,0:T(8,128)(2,1)S(1)}, bf16[2,4,4,16,128]{4,3,2,1,0:T(8,128)(2,1)S(1)}, u32[]{:S(2)}, u32[]{:S(2)}) collective-permute-start(bf16[2,4,4,16,128]{4,3,2,1,0:T(8,128)(2,1)S(1)} %get-tuple-element.34), channel_id=1, source_target_pairs={{0,4},{1,5},{2,6},{3,7},{4,0},{5,1},{6,2},{7,3},{8,12},{9,13},{10,... | collective-permute-start | bytes 393224 | tf_op jit(solution)/shard_map/ppermute | solution.py:546
  27.1 0.0 collective-permute-done.4.refs_1_
  27.1 1.3 %collective-permute-start.9 = (bf16[2,4,4,16,128]{4,3,2,1,0:T(8,128)(2,1)S(1)}, bf16[2,4,4,16,128]{4,3,2,1,0:T(8,128)(2,1)S(1)}, u32[]{:S(2)}, u32[]{:S(2)}) collective-permute-start(bf16[2,4,4,16,128]{4,3,2,1,0:T(8,128)(2,1)S(1)} %get-tuple-element.35), channel_id=1, source_target_pairs={{0,6},{1,7},{2,4},{3,5},{4,2},{5,3},{6,0},{7,1},{8,14},{9,15},{10,... | collective-permute-start | bytes 393224 | tf_op jit(solution)/shard_map/ppermute | solution.py:546
  28.4 0.0 collective-permute-done.5.refs_2_
  28.4 1.0 %collective-permute-start.10 = (bf16[2,4,4,16,128]{4,3,2,1,0:T(8,128)(2,1)S(1)}, bf16[2,4,4,16,128]{4,3,2,1,0:T(8,128)(2,1)S(1)}, u32[]{:S(2)}, u32[]{:S(2)}) collective-permute-start(bf16[2,4,4,16,128]{4,3,2,1,0:T(8,128)(2,1)S(1)} %get-tuple-element.36), channel_id=1, source_target_pairs={{0,2},{1,3},{2,0},{3,1},{4,6},{5,7},{6,4},{7,5},{8,10},{9,11},{10,... | collective-permute-start | bytes 393224 | tf_op jit(solution)/shard_map/ppermute | solution.py:546
  29.4 0.0 collective-permute-done.6.refs_3_
  29.5 1.6 %collective-permute-start.11 = (bf16[4,4,64,128]{3,2,1,0:T(8,128)(2,1)S(1)}, bf16[4,4,64,128]{3,2,1,0:T(8,128)(2,1)S(1)}, u32[]{:S(2)}, u32[]{:S(2)}) collective-permute-start(bf16[4,4,64,128]{3,2,1,0:T(8,128)(2,1)S(1)} %far.1.refs_1_), channel_id=1, source_target_pairs={{0,16},{8,24},{16,0},{24,8},{1,17},{9,25},{17,1},{25,9},{2,18},{10... | collective-permute-start | bytes 786440 | tf_op jit(solution)/shard_map/ppermute | solution.py:546
  31.1 5.0 %collective-permute-done.8.refs_4_ = bf16[2,4,4,16,128]{4,3,2,1,0:T(8,128)(2,1)S(1)} collective-permute-done((bf16[2,4,4,16,128]{4,3,2,1,0:T(8,128)(2,1)S(1)}, bf16[2,4,4,16,128]{4,3,2,1,0:T(8,128)(2,1)S(1)}, u32[]{:S(2)}, u32[]{:S(2)}) %collective-permute-start.8) | collective-permute-done | bytes 131104 | tf_op jit(solution)/shard_map/ppermute | solution.py:546
  36.1 0.0 collective-permute-done.9.refs_5_
  36.1 0.1 collective-permute-done.10.refs_6_
  36.2 0.1 other.1
  36.3 0.1 collective-permute-start.15
  36.4 0.0 collective-permute-done.13.refs_0_
  36.4 0.5 %collective-permute-start.14 = (bf16[4,4,64,128]{3,2,1,0:T(8,128)(2,1)S(1)}, bf16[4,4,64,128]{3,2,1,0:T(8,128)(2,1)S(1)}, u32[]{:S(2)}, u32[]{:S(2)}) collective-permute-start(bf16[4,4,64,128]{3,2,1,0:T(8,128)(2,1)S(1)} %collective-permute-done.13.refs_0_), channel_id=1, source_target_pairs={{0,8},{8,0},{16,24},{24,16},{1,9},{9,1},{17,25},{25,17},{2,10},{10... | collective-permute-start | bytes 786440 | tf_op jit(solution)/shard_map/ppermute | solution.py:546
  36.9 0.0 collective-permute-done.11.refs_0_
  36.9 0.1 collective-permute-start.12
  37.0 1.5 %autos.1 = (bf16[2,4,4,128,128]{4,3,2,1,0:T(8,128)(2,1)S(1)}, f32[2,8,128,128]{3,2,1,0:T(8,128)}) custom-call(bf16[4,4,64,128]{3,2,1,0:T(8,128)(2,1)S(1)} %near.1.refs_2_.refs_0_, bf16[4,4,64,128]{3,2,1,0:T(8,128)(2,1)S(1)} %far.1.refs_1_, bf16[4,4,64,128]{3,2,1,0:T(8,128)(2,1)S(1)} %get-tuple-element.37.refs_2_, ...), custom_call_target="tpu_custom_call" | custom-call | flops 536870912 | bytes 4194304 | tf_op jit(solution)/shard_map/autos/pallas_call | solution.py:406
  38.5 0.2 collective-permute-done.14.refs_1_
  38.7 0.1 fill_near.1.refs_2_
  38.8 0.3 collective-permute-done.12.refs_1_
  39.1 0.1 fill_far.1.filled
  39.1 0.0 collective-permute-done.15.refs_0_
  39.1 0.0 copy-done
  39.1 1.9 %cross.1 = f32[2,3,4,128,128]{4,3,2,1,0:T(8,128)} custom-call(s32[3]{0:T(128)S(1)} %copy-done, bf16[2,4,4,128,128]{4,3,2,1,0:T(8,128)(2,1)S(1)} %get-tuple-element.39.block, bf16[2,4,4,128,128]{4,3,2,1,0:T(8,128)(2,1)S(1)} %fill_far.1.filled, bf16[2,4,4,64,128]{4,3,2,1,0:T(8,128)(2,1)S(1)} %collective-permute-done.15.refs_0_), custom_call_target="tpu_custom_call" | custom-call | flops 1610612736 | bytes 4194304 | tf_op jit(solution)/shard_map/cross/pallas_call | solution.py:514
  (4 shorter events, 0.1 us)
Async XLA Ops:
  7.6 10.2 %collective-permute-start.3 = (bf16[4,4,4,16,128]{4,3,2,1,0:T(8,128)(2,1)S(1)}, bf16[4,4,4,16,128]{4,3,2,1,0:T(8,128)(2,1)S(1)}, u32[]{:S(2)}, u32[]{:S(2)}) collective-permute-start(bf16[4,4,4,16,128]{4,3,2,1,0:T(8,128)(2,1)S(1)} %get-tuple-element.26), channel_id=1, source_target_pairs={{0,1},{1,0},{2,3},{3,2},{4,5},{5,4},{6,7},{7,6},{8,9},{9,8},{10,11... | collective-permute-start | bytes 786440 | tf_op jit(solution)/shard_map/ppermute | solution.py:546
  10.6 13.6 %collective-permute-start.7 = (bf16[4,4,4,16,128]{4,3,2,1,0:T(8,128)(2,1)}, bf16[4,4,4,16,128]{4,3,2,1,0:T(8,128)(2,1)S(1)}, u32[]{:S(2)}, u32[]{:S(2)}) collective-permute-start(bf16[4,4,4,16,128]{4,3,2,1,0:T(8,128)(2,1)} %get-tuple-element.32), channel_id=1, source_target_pairs={{0,1},{1,0},{2,3},{3,2},{4,5},{5,4},{6,7},{7,6},{8,9},{9,8},{10,11... | collective-permute-start | bytes 786440 | tf_op jit(solution)/shard_map/ppermute | solution.py:546
  10.7 10.3 %collective-permute-start = (bf16[4,4,16,128]{3,2,1,0:T(8,128)(2,1)S(1)}, bf16[4,4,16,128]{3,2,1,0:T(8,128)(2,1)S(1)}, u32[]{:S(2)}, u32[]{:S(2)}) collective-permute-start(bf16[4,4,16,128]{3,2,1,0:T(8,128)(2,1)S(1)} %get-tuple-element.23), channel_id=1, source_target_pairs={{0,4},{1,5},{2,6},{3,7},{4,0},{5,1},{6,2},{7,3},{8,12},{9,13},{10,... | collective-permute-start | bytes 196616 | tf_op jit(solution)/shard_map/ppermute | solution.py:546
  13.7 8.6 %collective-permute-start.1 = (bf16[4,4,16,128]{3,2,1,0:T(8,128)(2,1)S(1)}, bf16[4,4,16,128]{3,2,1,0:T(8,128)(2,1)S(1)}, u32[]{:S(2)}, u32[]{:S(2)}) collective-permute-start(bf16[4,4,16,128]{3,2,1,0:T(8,128)(2,1)S(1)} %get-tuple-element.24), channel_id=1, source_target_pairs={{0,6},{1,7},{2,4},{3,5},{4,2},{5,3},{6,0},{7,1},{8,14},{9,15},{10,... | collective-permute-start | bytes 196616 | tf_op jit(solution)/shard_map/ppermute | solution.py:546
  15.0 7.6 %collective-permute-start.2 = (bf16[4,4,16,128]{3,2,1,0:T(8,128)(2,1)S(1)}, bf16[4,4,16,128]{3,2,1,0:T(8,128)(2,1)S(1)}, u32[]{:S(2)}, u32[]{:S(2)}) collective-permute-start(bf16[4,4,16,128]{3,2,1,0:T(8,128)(2,1)S(1)} %get-tuple-element.25), channel_id=1, source_target_pairs={{0,2},{1,3},{2,0},{3,1},{4,6},{5,7},{6,4},{7,5},{8,10},{9,11},{10,... | collective-permute-start | bytes 196616 | tf_op jit(solution)/shard_map/ppermute | solution.py:546
  17.8 9.3 %collective-permute-start.4 = (bf16[4,4,16,128]{3,2,1,0:T(8,128)(2,1)S(1)}, bf16[4,4,16,128]{3,2,1,0:T(8,128)(2,1)S(1)}, u32[]{:S(2)}, u32[]{:S(2)}) collective-permute-start(bf16[4,4,16,128]{3,2,1,0:T(8,128)(2,1)S(1)} %get-tuple-element.28), channel_id=1, source_target_pairs={{0,4},{1,5},{2,6},{3,7},{4,0},{5,1},{6,2},{7,3},{8,12},{9,13},{10,... | collective-permute-start | bytes 196616 | tf_op jit(solution)/shard_map/ppermute | solution.py:546
  21.0 7.5 %collective-permute-start.5 = (bf16[4,4,16,128]{3,2,1,0:T(8,128)(2,1)S(1)}, bf16[4,4,16,128]{3,2,1,0:T(8,128)(2,1)S(1)}, u32[]{:S(2)}, u32[]{:S(2)}) collective-permute-start(bf16[4,4,16,128]{3,2,1,0:T(8,128)(2,1)S(1)} %get-tuple-element.29), channel_id=1, source_target_pairs={{0,6},{1,7},{2,4},{3,5},{4,2},{5,3},{6,0},{7,1},{8,14},{9,15},{10,... | collective-permute-start | bytes 196616 | tf_op jit(solution)/shard_map/ppermute | solution.py:546
  22.3 7.1 %collective-permute-start.6 = (bf16[4,4,16,128]{3,2,1,0:T(8,128)(2,1)S(1)}, bf16[4,4,16,128]{3,2,1,0:T(8,128)(2,1)S(1)}, u32[]{:S(2)}, u32[]{:S(2)}) collective-permute-start(bf16[4,4,16,128]{3,2,1,0:T(8,128)(2,1)S(1)} %get-tuple-element.30), channel_id=1, source_target_pairs={{0,2},{1,3},{2,0},{3,1},{4,6},{5,7},{6,4},{7,5},{8,10},{9,11},{10,... | collective-permute-start | bytes 196616 | tf_op jit(solution)/shard_map/ppermute | solution.py:546
  22.6 13.8 %collective-permute-start.13 = (bf16[4,4,64,128]{3,2,1,0:T(8,128)(2,1)S(1)}, bf16[4,4,64,128]{3,2,1,0:T(8,128)(2,1)S(1)}, u32[]{:S(2)}, u32[]{:S(2)}) collective-permute-start(bf16[4,4,64,128]{3,2,1,0:T(8,128)(2,1)S(1)} %near.1.refs_2_.refs_0_), channel_id=1, source_target_pairs={{0,16},{8,24},{16,0},{24,8},{1,17},{9,25},{17,1},{25,9},{2,18},{10... | collective-permute-start | bytes 786440 | tf_op jit(solution)/shard_map/ppermute | solution.py:546
  24.2 14.9 %copy-start = (s32[3]{0:T(128)S(1)}, s32[3]{0:T(128)}, u32[]{:S(2)}) copy-start(s32[3]{0:T(128)} %pairing_hbm.1) | copy-start | bytes 40
  24.3 11.8 %collective-permute-start.8 = (bf16[2,4,4,16,128]{4,3,2,1,0:T(8,128)(2,1)S(1)}, bf16[2,4,4,16,128]{4,3,2,1,0:T(8,128)(2,1)S(1)}, u32[]{:S(2)}, u32[]{:S(2)}) collective-permute-start(bf16[2,4,4,16,128]{4,3,2,1,0:T(8,128)(2,1)S(1)} %get-tuple-element.34), channel_id=1, source_target_pairs={{0,4},{1,5},{2,6},{3,7},{4,0},{5,1},{6,2},{7,3},{8,12},{9,13},{10,... | collective-permute-start | bytes 393224 | tf_op jit(solution)/shard_map/ppermute | solution.py:546
  27.1 9.0 %collective-permute-start.9 = (bf16[2,4,4,16,128]{4,3,2,1,0:T(8,128)(2,1)S(1)}, bf16[2,4,4,16,128]{4,3,2,1,0:T(8,128)(2,1)S(1)}, u32[]{:S(2)}, u32[]{:S(2)}) collective-permute-start(bf16[2,4,4,16,128]{4,3,2,1,0:T(8,128)(2,1)S(1)} %get-tuple-element.35), channel_id=1, source_target_pairs={{0,6},{1,7},{2,4},{3,5},{4,2},{5,3},{6,0},{7,1},{8,14},{9,15},{10,... | collective-permute-start | bytes 393224 | tf_op jit(solution)/shard_map/ppermute | solution.py:546
  28.4 7.8 %collective-permute-start.10 = (bf16[2,4,4,16,128]{4,3,2,1,0:T(8,128)(2,1)S(1)}, bf16[2,4,4,16,128]{4,3,2,1,0:T(8,128)(2,1)S(1)}, u32[]{:S(2)}, u32[]{:S(2)}) collective-permute-start(bf16[2,4,4,16,128]{4,3,2,1,0:T(8,128)(2,1)S(1)} %get-tuple-element.36), channel_id=1, source_target_pairs={{0,2},{1,3},{2,0},{3,1},{4,6},{5,7},{6,4},{7,5},{8,10},{9,11},{10,... | collective-permute-start | bytes 393224 | tf_op jit(solution)/shard_map/ppermute | solution.py:546
  29.5 7.5 %collective-permute-start.11 = (bf16[4,4,64,128]{3,2,1,0:T(8,128)(2,1)S(1)}, bf16[4,4,64,128]{3,2,1,0:T(8,128)(2,1)S(1)}, u32[]{:S(2)}, u32[]{:S(2)}) collective-permute-start(bf16[4,4,64,128]{3,2,1,0:T(8,128)(2,1)S(1)} %far.1.refs_1_), channel_id=1, source_target_pairs={{0,16},{8,24},{16,0},{24,8},{1,17},{9,25},{17,1},{25,9},{2,18},{10... | collective-permute-start | bytes 786440 | tf_op jit(solution)/shard_map/ppermute | solution.py:546
  36.3 2.8 %collective-permute-start.15 = (bf16[2,4,4,64,128]{4,3,2,1,0:T(8,128)(2,1)S(1)}, bf16[2,4,4,64,128]{4,3,2,1,0:T(8,128)(2,1)S(1)}, u32[]{:S(2)}, u32[]{:S(2)}) collective-permute-start(bf16[2,4,4,64,128]{4,3,2,1,0:T(8,128)(2,1)S(1)} %get-tuple-element.40), channel_id=1, source_target_pairs={{0,8},{8,0},{16,24},{24,16},{1,9},{9,1},{17,25},{25,17},{2,10},{10... | collective-permute-start | bytes 1572872 | tf_op jit(solution)/shard_map/ppermute | solution.py:546
  36.4 2.3 %collective-permute-start.14 = (bf16[4,4,64,128]{3,2,1,0:T(8,128)(2,1)S(1)}, bf16[4,4,64,128]{3,2,1,0:T(8,128)(2,1)S(1)}, u32[]{:S(2)}, u32[]{:S(2)}) collective-permute-start(bf16[4,4,64,128]{3,2,1,0:T(8,128)(2,1)S(1)} %collective-permute-done.13.refs_0_), channel_id=1, source_target_pairs={{0,8},{8,0},{16,24},{24,16},{1,9},{9,1},{17,25},{25,17},{2,10},{10... | collective-permute-start | bytes 786440 | tf_op jit(solution)/shard_map/ppermute | solution.py:546
  36.9 2.1 %collective-permute-start.12 = (bf16[4,4,64,128]{3,2,1,0:T(8,128)(2,1)S(1)}, bf16[4,4,64,128]{3,2,1,0:T(8,128)(2,1)S(1)}, u32[]{:S(2)}, u32[]{:S(2)}) collective-permute-start(bf16[4,4,64,128]{3,2,1,0:T(8,128)(2,1)S(1)} %collective-permute-done.11.refs_0_), channel_id=1, source_target_pairs={{0,8},{8,0},{16,24},{24,16},{1,9},{9,1},{17,25},{25,17},{2,10},{10... | collective-permute-start | bytes 786440 | tf_op jit(solution)/shard_map/ppermute | solution.py:546

commit v5 on v4

--- a/solution.py
+++ b/solution.py
@@ -14,6 +14,7 @@
 OUTER = 32
 ROWS = 16
 MIB = 1024 * 1024
+FILL_FLOPS = (9 << 26, 9 << 27)
 
 
 def twiddle_table():
@@ -374,56 +375,68 @@
         target[:, :, span, :] = part[:, :, pl.ds(source * rows, rows), :]
 
 
-def autos_kernel(chan_count, block_bits, paired, *refs):
-    count = 2 if paired else 1
-    inputs = refs[: 2 * count]
-    block, autos_hbm, autos, sems = refs[-4:]
+def round_of(pairing_ref, mask):
+    rounds = lax.broadcasted_iota(jnp.int32, pairing_ref.shape, 1)
+    return jnp.max(jnp.where(pairing_ref[...] == mask, rounds, 0))
+
+
+def first_kernel(chan_count, block_bits, count, mask, pairing_ref, *refs):
+    inputs = [refs[at * count : (at + 1) * count] for at in range(3)]
+    block, autos_hbm, vis_hbm, partner, autos, vis, sems, vis_sems = refs[3 * count :]
     half = block.shape[1]
     top = bit_of(lax.axis_index("inp"), block_bits - 1)
     copies = []
+
+    def store(source, target, sem):
+        copy = pltpu.make_async_copy(source, target, sem)
+        copy.start()
+        copies.append(copy)
+
     for slot in range(2):
-        fill(block.at[slot], inputs[slot * count : (slot + 1) * count], chan_count)
+        fill(block.at[slot], inputs[slot], chan_count)
         for group in range(half):
             rows = block[slot, group]
-            at = half * (slot * top + (1 - slot) * (1 - top)) + group
             autos[0, slot, group], autos[1, slot, group] = products(rows, rows)
-            for part in range(2):
-                copy = pltpu.make_async_copy(
-                    autos.at[part, slot, group], autos_hbm.at[part, at], sems.at[part, slot, group]
-                )
-                copy.start()
-                copies.append(copy)
+        place = pl.ds(half * (slot * top + (1 - slot) * (1 - top)), half)
+        for part in range(2):
+            store(autos.at[part, slot], autos_hbm.at[part, place], sems.at[part, slot])
+    fill(partner, inputs[2], chan_count)
+    for group in range(half):
+        vis[0, group], vis[1, group] = products(block[1, group], partner[group])
+    place = round_of(pairing_ref, mask)
+    for part in range(2):
+        store(vis.at[part], vis_hbm.at[part, place], vis_sems.at[part])
     for copy in copies:
         copy.wait()
 
 
-def autos_call(operands, chan_count, block_bits, after=()):
+def first_call(pairing, operands, mask, chan_count, block_bits):
     half, slices, rows = operands[0].shape[:3]
-    paired = len(operands) == 4
-    rows *= 2 if paired else 1
+    count = len(operands) // 3
+    rows *= count
     auto_shape = (2, 2, half, rows, rows)
     block_shape = (2, half, slices, rows, LANES)
     return pl.pallas_call(
-        functools.partial(autos_kernel, chan_count, block_bits, paired),
+        functools.partial(first_kernel, chan_count, block_bits, count, mask),
         out_shape=[
             jax.ShapeDtypeStruct(block_shape, jnp.bfloat16),
             jax.ShapeDtypeStruct((2, 2 * half, rows, rows), jnp.float32),
+            jax.ShapeDtypeStruct((2, pairing.shape[1], half, rows, rows), jnp.float32),
         ],
-        in_specs=[pl.BlockSpec(memory_space=pltpu.VMEM)] * len(operands)
-        + [pl.BlockSpec(memory_space=pl.ANY)] * len(after),
-        out_specs=[pl.BlockSpec(memory_space=pltpu.VMEM), pl.BlockSpec(memory_space=pltpu.HBM)],
+        in_specs=[pl.BlockSpec(memory_space=pltpu.VMEM)] * (1 + len(operands)),
+        out_specs=[pl.BlockSpec(memory_space=pltpu.VMEM)]
+        + [pl.BlockSpec(memory_space=pltpu.HBM)] * 2,
         scratch_shapes=[
+            pltpu.VMEM(block_shape[1:], jnp.bfloat16),
             pltpu.VMEM(auto_shape, jnp.float32),
-            pltpu.SemaphoreType.DMA(auto_shape[:3]),
+            pltpu.VMEM((2, half, rows, rows), jnp.float32),
+            pltpu.SemaphoreType.DMA((2, 2)),
+            pltpu.SemaphoreType.DMA((2,)),
         ],
-        compiler_params=pltpu.CompilerParams(vmem_limit_bytes=8 * MIB),
-        cost_estimate=pl.CostEstimate(
-            flops=16 * half * rows * rows * slices * LANES,
-            bytes_accessed=4 << 20,
-            transcendentals=0,
-        ),
-        name="autos",
-    )(*operands, *after)
+        compiler_params=pltpu.CompilerParams(vmem_limit_bytes=12 * MIB),
+        cost_estimate=pl.CostEstimate(flops=1 << 20, bytes_accessed=4 << 20, transcendentals=0),
+        name="correlate_first",
+    )(pairing, *operands)
 
 
 def parts_of(layout, refs):
@@ -449,11 +462,9 @@
         refs[-1][index] = part[...]
 
 
-def cross_kernel(chan_count, block_bits, early, late, layout, pairing_hbm, block, filled, *refs):
-    inputs, refs = refs[: -len(SCRATCH)], refs[-len(SCRATCH) :]
-    vis_hbm, others, vis, pairing_ref, vis_sems, pairing_sem = refs
-    pairing_copy = pltpu.make_async_copy(pairing_hbm, pairing_ref, pairing_sem)
-    pairing_copy.start()
+def cross_kernel(chan_count, block_bits, early, late, layout, pairing_ref, block, filled, *refs):
+    inputs, refs = refs[: -len(SCRATCH) - 1], refs[-len(SCRATCH) :]
+    vis_hbm, others, vis, vis_sems = refs
     own = lax.axis_index("inp")
     top = bit_of(own, block_bits - 1)
     half = block.shape[1]
@@ -469,11 +480,7 @@
             slot = (bit_of(own, bit) == top).astype(jnp.int32)
         for group in range(half):
             vis[0, index, group], vis[1, index, group] = products(block[slot, group], other[group])
-        if index == 0:
-            pairing_copy.wait()
-        place = jnp.int32(0)
-        for turn_at in range(pairing_ref.shape[0]):
-            place = jnp.where(pairing_ref[turn_at] == mask, turn_at, place)
+        place = round_of(pairing_ref, mask)
         for part in range(2):
             copy = pltpu.make_async_copy(
                 vis.at[part, index], vis_hbm.at[part, place], vis_sems.at[part, index]
@@ -484,10 +491,10 @@
         copy.wait()
 
 
-SCRATCH = ("vis_hbm", "others", "vis", "pairing_ref", "vis_sems", "pairing_sem")
-
-
-def cross_call(pairing, block, received, early, late, chan_count, block_bits):
+SCRATCH = ("vis_hbm", "others", "vis", "vis_sems")
+
+
+def cross_call(pairing, block, visibilities, received, early, late, chan_count, block_bits):
     _, half, slices, rows, _ = block.shape
     filled_shape = (len(early),) + block.shape[1:]
     cost = functools.partial(pl.CostEstimate, transcendentals=0)
@@ -499,7 +506,7 @@
                 functools.partial(fill_parity_kernel, chan_count, parity),
                 [filled_shape],
                 [received[mask][1][parity] for mask in early] + list(filled),
-                cost=cost(flops=(1 << 29, 4 << 28)[parity], bytes_accessed=(1 << 10, 1 << 20)[parity]),
+                cost=cost(flops=FILL_FLOPS[parity], bytes_accessed=1 << 20),
                 aliases={len(early): 0} if parity else None,
             )
     else:
@@ -513,16 +520,15 @@
     vis_shape = (2, count, half, rows, rows)
     return pl.pallas_call(
         functools.partial(cross_kernel, chan_count, block_bits, early, late, layout),
-        out_shape=jax.ShapeDtypeStruct(vis_shape, jnp.float32),
-        in_specs=[pl.BlockSpec(memory_space=pltpu.HBM)]
-        + [pl.BlockSpec(memory_space=pltpu.VMEM)] * (2 + len(operands)),
+        out_shape=jax.ShapeDtypeStruct(visibilities.shape, jnp.float32),
+        in_specs=[pl.BlockSpec(memory_space=pltpu.VMEM)] * (3 + len(operands))
+        + [pl.BlockSpec(memory_space=pltpu.HBM)],
         out_specs=pl.BlockSpec(memory_space=pltpu.HBM),
+        input_output_aliases={3 + len(operands): 0},
         scratch_shapes=[
             pltpu.VMEM((len(late), half, slices, rows, LANES), jnp.bfloat16),
             pltpu.VMEM(vis_shape, jnp.float32),
-            pltpu.SMEM(pairing.shape, jnp.int32),
             pltpu.SemaphoreType.DMA(vis_shape[:2]),
-            pltpu.SemaphoreType.DMA(()),
         ],
         compiler_params=pltpu.CompilerParams(vmem_limit_bytes=16 * MIB),
         cost_estimate=pl.CostEstimate(
@@ -531,10 +537,11 @@
             transcendentals=0,
         ),
         name="cross",
-    )(pairing, block, filled, *operands)
+    )(pairing, block, filled, *operands, visibilities)
 
 
 def on_device(voltages, filter_taps, pairing):
+    pairing = pairing[None, :]
     chan_count = lax.axis_size("chan")
     inp_count = lax.axis_size("inp")
     block_bits = top_bit(inp_count)
@@ -559,7 +566,7 @@
     direct = along(direct)
     relay_other = exchange(relay_other, "chan", 1)
     far_own, *onward = vmem_call(
-        "split", split_kernel, [part] * (chan_count // 2), [relay_moving], []
+        "split", split_kernel, [part] * (chan_count // 2), [relay_moving]
     )
     onward = along(onward)
     near, far = [own_moving] + direct, [far_own] + onward
@@ -575,9 +582,9 @@
             return jnp.take(jnp.stack(parts, axis=2), sources, axis=2).reshape(laid)
 
         near, far = [merge(near)], [merge(far)]
-    (near,) = vmem_call("near", lay_kernel, [laid], near, [])
+    (near,) = vmem_call("near", lay_kernel, [laid], near)
     crossed = [exchange(near, "inp", top_mask)]
-    (far,) = vmem_call("far", lay_kernel, [laid], far, [])
+    (far,) = vmem_call("far", lay_kernel, [laid], far)
     crossed.append(exchange(far, "inp", top_mask))
     rest = vmem_call(
         "hand_on",
@@ -601,7 +608,6 @@
         other_kernel,
         [laid] * 2 + [(2,) + laid] * (block_bits - 1),
         [near, far] + others,
-        [],
     )
     masks = list(range(1, inp_count))
     received = {top_mask: ("pair", crossed)}
@@ -631,12 +637,18 @@
 
         block = [interleave(entry) for entry in block]
         received = {mask: interleave(entry) for mask, entry in received.items()}
-    early = [mask for mask in masks if top_bit(mask) == block_bits - 1]
-    late = [mask for mask in masks if top_bit(mask) != block_bits - 1]
-    rows, autos = autos_call(
-        [value for _, values in block for value in values], chan_count, block_bits, []
-    )
-    visibilities = cross_call(pairing, rows, received, early, late, chan_count, block_bits)
+    early = [mask for mask in masks if mask > top_mask]
+    late = [mask for mask in masks if mask < top_mask]
+    rows, autos, visibilities = first_call(
+        pairing,
+        [value for _, values in block + [received[top_mask]] for value in values],
+        top_mask,
+        chan_count,
+        block_bits,
+    )
+    visibilities = cross_call(
+        pairing, rows, visibilities, received, early, late, chan_count, block_bits
+    )
     return (visibilities, autos)
 
 

time: 41.2 us -> 40.7 us (0.988)
    pallas_call x1, Pallas kernels: 1.92 us -> 1.4 us  [cross_call(): pl.pallas_call(functools.partial(cross_kernel, chan_count, block_bits, ea...]
  transfers between devices with their start and end apart: 16 -> 16, of which waited for: 5 -> 4; matrix products, arithmetic and copies ran while one was open for 0% -> 0% of each run, Pallas kernels for 4% -> 5%
where the time goes in v5:
time: 40.7 us; the launch traced here: 40.5 us
  starting transfers between devices  21.6 us (53%)
  Pallas kernels  10.3 us (25%)
  waiting for transfers between devices  7.86 us (19%)
  between operations  0.75 us (2%)
    ppermute x16, starting transfers between devices, exchange(): return lax.ppermute(value, axis, [(i, i ^ mask) for i in range(count)])  21.6 us
    ppermute x16, waiting for transfers between devices, exchange(): return lax.ppermute(value, axis, [(i, i ^ mask) for i in range(count)])  7.86 us
    pallas_call x1, Pallas kernels, spectra_pieces(): pl.pallas_call(functools.partial(spectra_kernel, chan_count, spectra_coun...  6.93 us
    pallas_call x1, Pallas kernels, first_call(): pl.pallas_call(functools.partial(first_kernel, chan_count, block_bits, co...  1.69 us
    pallas_call x1, Pallas kernels, cross_call(): pl.pallas_call(functools.partial(cross_kernel, chan_count, block_bits, ea...  1.4 us
  transfers between devices with their start and end apart: 16, of which 4 were waited for; matrix products, arithmetic and copies ran while one was open for 0% of the time, Pallas kernels for 5%

profile of v5, /device:TPU:0, one launch (start us, length us, event | category | flops | bytes accessed | tf_op | source)
XLA Modules:
  0.0 40.5 jit_solution(14370750155961632284)
XLA Ops:
  0.6 6.9 %spectra.1 = (bf16[4,4,16,128]{3,2,1,0:T(8,128)(2,1)S(1)}, bf16[4,4,16,128]{3,2,1,0:T(8,128)(2,1)S(1)}, bf16[4,4,16,128]{3,2,1,0:T(8,128)(2,1)S(1)}, bf16[4,4,16...) custom-call(bf16[2,16,77824]{2,1,0:T(8,128)(2,1)} %volt_hbm.1, ...), custom_call_target="tpu_custom_call" | custom-call | tf_op jit(solution)/shard_map/spectra/pallas_call | solution.py:242
  7.6 3.0 %collective-permute-start.3 = (bf16[4,4,4,16,128]{4,3,2,1,0:T(8,128)(2,1)S(1)}, bf16[4,4,4,16,128]{4,3,2,1,0:T(8,128)(2,1)S(1)}, u32[]{:S(2)}, u32[]{:S(2)}) collective-permute-start(bf16[4,4,4,16,128]{4,3,2,1,0:T(8,128)(2,1)S(1)} %get-tuple-element.27), channel_id=1, source_target_pairs={{0,1},{1,0},{2,3},{3,2},{4,5},{5,4},{6,7},{7,6},{8,9},{9,8},{10,11... | collective-permute-start | bytes 786440 | tf_op jit(solution)/shard_map/ppermute | solution.py:553
  10.6 0.1 collective-permute-start.7
  10.7 3.0 %collective-permute-start = (bf16[4,4,16,128]{3,2,1,0:T(8,128)(2,1)S(1)}, bf16[4,4,16,128]{3,2,1,0:T(8,128)(2,1)S(1)}, u32[]{:S(2)}, u32[]{:S(2)}) collective-permute-start(bf16[4,4,16,128]{3,2,1,0:T(8,128)(2,1)S(1)} %get-tuple-element.24), channel_id=1, source_target_pairs={{0,4},{1,5},{2,6},{3,7},{4,0},{5,1},{6,2},{7,3},{8,12},{9,13},{10,... | collective-permute-start | bytes 196616 | tf_op jit(solution)/shard_map/ppermute | solution.py:553
  13.7 1.3 %collective-permute-start.1 = (bf16[4,4,16,128]{3,2,1,0:T(8,128)(2,1)S(1)}, bf16[4,4,16,128]{3,2,1,0:T(8,128)(2,1)S(1)}, u32[]{:S(2)}, u32[]{:S(2)}) collective-permute-start(bf16[4,4,16,128]{3,2,1,0:T(8,128)(2,1)S(1)} %get-tuple-element.25), channel_id=1, source_target_pairs={{0,6},{1,7},{2,4},{3,5},{4,2},{5,3},{6,0},{7,1},{8,14},{9,15},{10,... | collective-permute-start | bytes 196616 | tf_op jit(solution)/shard_map/ppermute | solution.py:553
  15.0 0.2 collective-permute-start.2
  15.3 2.5 %collective-permute-done.3.refs_0_ = bf16[4,4,4,16,128]{4,3,2,1,0:T(8,128)(2,1)S(1)} collective-permute-done((bf16[4,4,4,16,128]{4,3,2,1,0:T(8,128)(2,1)S(1)}, bf16[4,4,4,16,128]{4,3,2,1,0:T(8,128)(2,1)S(1)}, u32[]{:S(2)}, u32[]{:S(2)}) %collective-permute-start.3) | collective-permute-done | bytes 262176 | tf_op jit(solution)/shard_map/ppermute | solution.py:553
  17.8 0.0 copy-start
  17.8 3.2 %collective-permute-start.4 = (bf16[4,4,16,128]{3,2,1,0:T(8,128)(2,1)S(1)}, bf16[4,4,16,128]{3,2,1,0:T(8,128)(2,1)S(1)}, u32[]{:S(2)}, u32[]{:S(2)}) collective-permute-start(bf16[4,4,16,128]{3,2,1,0:T(8,128)(2,1)S(1)} %get-tuple-element.29), channel_id=1, source_target_pairs={{0,4},{1,5},{2,6},{3,7},{4,0},{5,1},{6,2},{7,3},{8,12},{9,13},{10,... | collective-permute-start | bytes 196616 | tf_op jit(solution)/shard_map/ppermute | solution.py:553
  21.0 0.0 collective-permute-done.refs_1_
  21.0 1.4 %collective-permute-start.5 = (bf16[4,4,16,128]{3,2,1,0:T(8,128)(2,1)S(1)}, bf16[4,4,16,128]{3,2,1,0:T(8,128)(2,1)S(1)}, u32[]{:S(2)}, u32[]{:S(2)}) collective-permute-start(bf16[4,4,16,128]{3,2,1,0:T(8,128)(2,1)S(1)} %get-tuple-element.30), channel_id=1, source_target_pairs={{0,6},{1,7},{2,4},{3,5},{4,2},{5,3},{6,0},{7,1},{8,14},{9,15},{10,... | collective-permute-start | bytes 196616 | tf_op jit(solution)/shard_map/ppermute | solution.py:553
  22.3 0.0 collective-permute-done.1.refs_2_
  22.3 0.3 collective-permute-start.6
  22.6 0.0 collective-permute-done.2.refs_3_
  22.7 1.6 %collective-permute-start.11 = (bf16[4,4,64,128]{3,2,1,0:T(8,128)(2,1)S(1)}, bf16[4,4,64,128]{3,2,1,0:T(8,128)(2,1)S(1)}, u32[]{:S(2)}, u32[]{:S(2)}) collective-permute-start(bf16[4,4,64,128]{3,2,1,0:T(8,128)(2,1)S(1)} %near.1.refs_2_.refs_0_), channel_id=1, source_target_pairs={{0,16},{8,24},{16,0},{24,8},{1,17},{9,25},{17,1},{25,9},{2,18},{10... | collective-permute-start | bytes 786440 | tf_op jit(solution)/shard_map/ppermute | solution.py:553
  24.2 0.0 collective-permute-done.7.refs_1_.refs_3_
  24.3 2.8 %collective-permute-start.8 = (bf16[2,4,4,16,128]{4,3,2,1,0:T(8,128)(2,1)S(1)}, bf16[2,4,4,16,128]{4,3,2,1,0:T(8,128)(2,1)S(1)}, u32[]{:S(2)}, u32[]{:S(2)}) collective-permute-start(bf16[2,4,4,16,128]{4,3,2,1,0:T(8,128)(2,1)S(1)} %get-tuple-element.35), channel_id=1, source_target_pairs={{0,4},{1,5},{2,6},{3,7},{4,0},{5,1},{6,2},{7,3},{8,12},{9,13},{10,... | collective-permute-start | bytes 393224 | tf_op jit(solution)/shard_map/ppermute | solution.py:553
  27.1 0.0 collective-permute-done.4.refs_1_
  27.1 1.3 %collective-permute-start.9 = (bf16[2,4,4,16,128]{4,3,2,1,0:T(8,128)(2,1)S(1)}, bf16[2,4,4,16,128]{4,3,2,1,0:T(8,128)(2,1)S(1)}, u32[]{:S(2)}, u32[]{:S(2)}) collective-permute-start(bf16[2,4,4,16,128]{4,3,2,1,0:T(8,128)(2,1)S(1)} %get-tuple-element.36), channel_id=1, source_target_pairs={{0,6},{1,7},{2,4},{3,5},{4,2},{5,3},{6,0},{7,1},{8,14},{9,15},{10,... | collective-permute-start | bytes 393224 | tf_op jit(solution)/shard_map/ppermute | solution.py:553
  28.4 0.0 collective-permute-done.5.refs_2_
  28.4 1.0 %collective-permute-start.10 = (bf16[2,4,4,16,128]{4,3,2,1,0:T(8,128)(2,1)S(1)}, bf16[2,4,4,16,128]{4,3,2,1,0:T(8,128)(2,1)S(1)}, u32[]{:S(2)}, u32[]{:S(2)}) collective-permute-start(bf16[2,4,4,16,128]{4,3,2,1,0:T(8,128)(2,1)S(1)} %get-tuple-element.37), channel_id=1, source_target_pairs={{0,2},{1,3},{2,0},{3,1},{4,6},{5,7},{6,4},{7,5},{8,10},{9,11},{10,... | collective-permute-start | bytes 393224 | tf_op jit(solution)/shard_map/ppermute | solution.py:553
  29.4 0.0 collective-permute-done.6.refs_3_
  29.5 1.7 %collective-permute-start.12 = (bf16[4,4,64,128]{3,2,1,0:T(8,128)(2,1)S(1)}, bf16[4,4,64,128]{3,2,1,0:T(8,128)(2,1)S(1)}, u32[]{:S(2)}, u32[]{:S(2)}) collective-permute-start(bf16[4,4,64,128]{3,2,1,0:T(8,128)(2,1)S(1)} %far.1.refs_1_), channel_id=1, source_target_pairs={{0,16},{8,24},{16,0},{24,8},{1,17},{9,25},{17,1},{25,9},{2,18},{10... | collective-permute-start | bytes 786440 | tf_op jit(solution)/shard_map/ppermute | solution.py:553
  31.1 4.9 %collective-permute-done.8.refs_4_ = bf16[2,4,4,16,128]{4,3,2,1,0:T(8,128)(2,1)S(1)} collective-permute-done((bf16[2,4,4,16,128]{4,3,2,1,0:T(8,128)(2,1)S(1)}, bf16[2,4,4,16,128]{4,3,2,1,0:T(8,128)(2,1)S(1)}, u32[]{:S(2)}, u32[]{:S(2)}) %collective-permute-start.8) | collective-permute-done | bytes 131104 | tf_op jit(solution)/shard_map/ppermute | solution.py:553
  36.1 0.0 collective-permute-done.9.refs_5_
  36.1 0.1 collective-permute-done.10.refs_6_
  36.2 0.1 other.1
  36.3 0.1 collective-permute-start.15
  36.4 0.0 collective-permute-done.11.refs_4_
  36.4 0.5 %collective-permute-start.14 = (bf16[4,4,64,128]{3,2,1,0:T(8,128)(2,1)S(1)}, bf16[4,4,64,128]{3,2,1,0:T(8,128)(2,1)S(1)}, u32[]{:S(2)}, u32[]{:S(2)}) collective-permute-start(bf16[4,4,64,128]{3,2,1,0:T(8,128)(2,1)S(1)} %collective-permute-done.11.refs_4_), channel_id=1, source_target_pairs={{0,8},{8,0},{16,24},{24,16},{1,9},{9,1},{17,25},{25,17},{2,10},{10... | collective-permute-start | bytes 786440 | tf_op jit(solution)/shard_map/ppermute | solution.py:553
  36.9 0.0 collective-permute-done.12.refs_5_
  36.9 0.1 collective-permute-start.13
  37.0 0.0 copy-done
  37.0 1.7 %correlate_first.1 = (bf16[2,4,4,128,128]{4,3,2,1,0:T(8,128)(2,1)S(1)}, f32[2,8,128,128]{3,2,1,0:T(8,128)}, f32[2,3,4,128,128]{4,3,2,1,0:T(8,128)}) custom-call(s32[1,3]{1,0:T(1,128)S(1)} %bitcast.1, bf16[4,4,64,128]{3,2,1,0:T(8,128)(2,1)S(1)} %near.1.refs_2_.refs_0_, bf16[4,4,64,128]{3,2,1,0:T(8,128)(2,1)S(1)} %far.1.refs_1_, ...), custom_call_target="tpu_custom_call" | custom-call | flops 1048576 | bytes 4194304 | tf_op jit(solution)/shard_map/correlate_first/pallas_call | solution.py:419
  38.7 0.0 collective-permute-done.14.refs_0_
  38.7 0.3 collective-permute-done.13.refs_0_
  39.1 0.0 collective-permute-done.15.refs_0_
  39.1 1.4 %cross.1 = f32[2,3,4,128,128]{4,3,2,1,0:T(8,128)} custom-call(s32[1,3]{1,0:T(1,128)S(1)} %bitcast.2, bf16[2,4,4,128,128]{4,3,2,1,0:T(8,128)(2,1)S(1)} %get-tuple-element.40.block, bf16[1,4,4,128,128]{4,3,2,1,0:T(8,128)(2,1)S(1)} %fill_far.1.filled, bf16[2,4,4,64,128]{4,3,2,1,0:T(8,128)(2,1)S(1)} %collective-permute-done.15.refs_0_, ...), custom_call_target="tpu_custom_call", output_to_operand_aliasing={{}: (4, {})} | custom-call | flops 1073741824 | bytes 4194304 | tf_op jit(solution)/shard_map/cross/pallas_call | solution.py:521
  (6 shorter events, 0.2 us)
Async XLA Ops:
  7.6 10.2 %collective-permute-start.3 = (bf16[4,4,4,16,128]{4,3,2,1,0:T(8,128)(2,1)S(1)}, bf16[4,4,4,16,128]{4,3,2,1,0:T(8,128)(2,1)S(1)}, u32[]{:S(2)}, u32[]{:S(2)}) collective-permute-start(bf16[4,4,4,16,128]{4,3,2,1,0:T(8,128)(2,1)S(1)} %get-tuple-element.27), channel_id=1, source_target_pairs={{0,1},{1,0},{2,3},{3,2},{4,5},{5,4},{6,7},{7,6},{8,9},{9,8},{10,11... | collective-permute-start | bytes 786440 | tf_op jit(solution)/shard_map/ppermute | solution.py:553
  10.6 13.6 %collective-permute-start.7 = (bf16[4,4,4,16,128]{4,3,2,1,0:T(8,128)(2,1)}, bf16[4,4,4,16,128]{4,3,2,1,0:T(8,128)(2,1)S(1)}, u32[]{:S(2)}, u32[]{:S(2)}) collective-permute-start(bf16[4,4,4,16,128]{4,3,2,1,0:T(8,128)(2,1)} %get-tuple-element.33), channel_id=1, source_target_pairs={{0,1},{1,0},{2,3},{3,2},{4,5},{5,4},{6,7},{7,6},{8,9},{9,8},{10,11... | collective-permute-start | bytes 786440 | tf_op jit(solution)/shard_map/ppermute | solution.py:553
  10.7 10.3 %collective-permute-start = (bf16[4,4,16,128]{3,2,1,0:T(8,128)(2,1)S(1)}, bf16[4,4,16,128]{3,2,1,0:T(8,128)(2,1)S(1)}, u32[]{:S(2)}, u32[]{:S(2)}) collective-permute-start(bf16[4,4,16,128]{3,2,1,0:T(8,128)(2,1)S(1)} %get-tuple-element.24), channel_id=1, source_target_pairs={{0,4},{1,5},{2,6},{3,7},{4,0},{5,1},{6,2},{7,3},{8,12},{9,13},{10,... | collective-permute-start | bytes 196616 | tf_op jit(solution)/shard_map/ppermute | solution.py:553
  13.7 8.6 %collective-permute-start.1 = (bf16[4,4,16,128]{3,2,1,0:T(8,128)(2,1)S(1)}, bf16[4,4,16,128]{3,2,1,0:T(8,128)(2,1)S(1)}, u32[]{:S(2)}, u32[]{:S(2)}) collective-permute-start(bf16[4,4,16,128]{3,2,1,0:T(8,128)(2,1)S(1)} %get-tuple-element.25), channel_id=1, source_target_pairs={{0,6},{1,7},{2,4},{3,5},{4,2},{5,3},{6,0},{7,1},{8,14},{9,15},{10,... | collective-permute-start | bytes 196616 | tf_op jit(solution)/shard_map/ppermute | solution.py:553
  15.0 7.6 %collective-permute-start.2 = (bf16[4,4,16,128]{3,2,1,0:T(8,128)(2,1)S(1)}, bf16[4,4,16,128]{3,2,1,0:T(8,128)(2,1)S(1)}, u32[]{:S(2)}, u32[]{:S(2)}) collective-permute-start(bf16[4,4,16,128]{3,2,1,0:T(8,128)(2,1)S(1)} %get-tuple-element.26), channel_id=1, source_target_pairs={{0,2},{1,3},{2,0},{3,1},{4,6},{5,7},{6,4},{7,5},{8,10},{9,11},{10,... | collective-permute-start | bytes 196616 | tf_op jit(solution)/shard_map/ppermute | solution.py:553
  17.8 19.2 %copy-start = (s32[3]{0:T(128)S(1)}, s32[3]{0:T(128)}, u32[]{:S(2)}) copy-start(s32[3]{0:T(128)} %param.6) | copy-start | bytes 40
  17.8 9.3 %collective-permute-start.4 = (bf16[4,4,16,128]{3,2,1,0:T(8,128)(2,1)S(1)}, bf16[4,4,16,128]{3,2,1,0:T(8,128)(2,1)S(1)}, u32[]{:S(2)}, u32[]{:S(2)}) collective-permute-start(bf16[4,4,16,128]{3,2,1,0:T(8,128)(2,1)S(1)} %get-tuple-element.29), channel_id=1, source_target_pairs={{0,4},{1,5},{2,6},{3,7},{4,0},{5,1},{6,2},{7,3},{8,12},{9,13},{10,... | collective-permute-start | bytes 196616 | tf_op jit(solution)/shard_map/ppermute | solution.py:553
  21.0 7.4 %collective-permute-start.5 = (bf16[4,4,16,128]{3,2,1,0:T(8,128)(2,1)S(1)}, bf16[4,4,16,128]{3,2,1,0:T(8,128)(2,1)S(1)}, u32[]{:S(2)}, u32[]{:S(2)}) collective-permute-start(bf16[4,4,16,128]{3,2,1,0:T(8,128)(2,1)S(1)} %get-tuple-element.30), channel_id=1, source_target_pairs={{0,6},{1,7},{2,4},{3,5},{4,2},{5,3},{6,0},{7,1},{8,14},{9,15},{10,... | collective-permute-start | bytes 196616 | tf_op jit(solution)/shard_map/ppermute | solution.py:553
  22.3 7.1 %collective-permute-start.6 = (bf16[4,4,16,128]{3,2,1,0:T(8,128)(2,1)S(1)}, bf16[4,4,16,128]{3,2,1,0:T(8,128)(2,1)S(1)}, u32[]{:S(2)}, u32[]{:S(2)}) collective-permute-start(bf16[4,4,16,128]{3,2,1,0:T(8,128)(2,1)S(1)} %get-tuple-element.31), channel_id=1, source_target_pairs={{0,2},{1,3},{2,0},{3,1},{4,6},{5,7},{6,4},{7,5},{8,10},{9,11},{10,... | collective-permute-start | bytes 196616 | tf_op jit(solution)/shard_map/ppermute | solution.py:553
  22.7 13.7 %collective-permute-start.11 = (bf16[4,4,64,128]{3,2,1,0:T(8,128)(2,1)S(1)}, bf16[4,4,64,128]{3,2,1,0:T(8,128)(2,1)S(1)}, u32[]{:S(2)}, u32[]{:S(2)}) collective-permute-start(bf16[4,4,64,128]{3,2,1,0:T(8,128)(2,1)S(1)} %near.1.refs_2_.refs_0_), channel_id=1, source_target_pairs={{0,16},{8,24},{16,0},{24,8},{1,17},{9,25},{17,1},{25,9},{2,18},{10... | collective-permute-start | bytes 786440 | tf_op jit(solution)/shard_map/ppermute | solution.py:553
  24.3 11.8 %collective-permute-start.8 = (bf16[2,4,4,16,128]{4,3,2,1,0:T(8,128)(2,1)S(1)}, bf16[2,4,4,16,128]{4,3,2,1,0:T(8,128)(2,1)S(1)}, u32[]{:S(2)}, u32[]{:S(2)}) collective-permute-start(bf16[2,4,4,16,128]{4,3,2,1,0:T(8,128)(2,1)S(1)} %get-tuple-element.35), channel_id=1, source_target_pairs={{0,4},{1,5},{2,6},{3,7},{4,0},{5,1},{6,2},{7,3},{8,12},{9,13},{10,... | collective-permute-start | bytes 393224 | tf_op jit(solution)/shard_map/ppermute | solution.py:553
  27.1 9.0 %collective-permute-start.9 = (bf16[2,4,4,16,128]{4,3,2,1,0:T(8,128)(2,1)S(1)}, bf16[2,4,4,16,128]{4,3,2,1,0:T(8,128)(2,1)S(1)}, u32[]{:S(2)}, u32[]{:S(2)}) collective-permute-start(bf16[2,4,4,16,128]{4,3,2,1,0:T(8,128)(2,1)S(1)} %get-tuple-element.36), channel_id=1, source_target_pairs={{0,6},{1,7},{2,4},{3,5},{4,2},{5,3},{6,0},{7,1},{8,14},{9,15},{10,... | collective-permute-start | bytes 393224 | tf_op jit(solution)/shard_map/ppermute | solution.py:553
  28.4 7.8 %collective-permute-start.10 = (bf16[2,4,4,16,128]{4,3,2,1,0:T(8,128)(2,1)S(1)}, bf16[2,4,4,16,128]{4,3,2,1,0:T(8,128)(2,1)S(1)}, u32[]{:S(2)}, u32[]{:S(2)}) collective-permute-start(bf16[2,4,4,16,128]{4,3,2,1,0:T(8,128)(2,1)S(1)} %get-tuple-element.37), channel_id=1, source_target_pairs={{0,2},{1,3},{2,0},{3,1},{4,6},{5,7},{6,4},{7,5},{8,10},{9,11},{10,... | collective-permute-start | bytes 393224 | tf_op jit(solution)/shard_map/ppermute | solution.py:553
  29.5 7.4 %collective-permute-start.12 = (bf16[4,4,64,128]{3,2,1,0:T(8,128)(2,1)S(1)}, bf16[4,4,64,128]{3,2,1,0:T(8,128)(2,1)S(1)}, u32[]{:S(2)}, u32[]{:S(2)}) collective-permute-start(bf16[4,4,64,128]{3,2,1,0:T(8,128)(2,1)S(1)} %far.1.refs_1_), channel_id=1, source_target_pairs={{0,16},{8,24},{16,0},{24,8},{1,17},{9,25},{17,1},{25,9},{2,18},{10... | collective-permute-start | bytes 786440 | tf_op jit(solution)/shard_map/ppermute | solution.py:553
  36.3 2.8 %collective-permute-start.15 = (bf16[2,4,4,64,128]{4,3,2,1,0:T(8,128)(2,1)S(1)}, bf16[2,4,4,64,128]{4,3,2,1,0:T(8,128)(2,1)S(1)}, u32[]{:S(2)}, u32[]{:S(2)}) collective-permute-start(bf16[2,4,4,64,128]{4,3,2,1,0:T(8,128)(2,1)S(1)} %get-tuple-element.41), channel_id=1, source_target_pairs={{0,8},{8,0},{16,24},{24,16},{1,9},{9,1},{17,25},{25,17},{2,10},{10... | collective-permute-start | bytes 1572872 | tf_op jit(solution)/shard_map/ppermute | solution.py:553
  36.4 2.3 %collective-permute-start.14 = (bf16[4,4,64,128]{3,2,1,0:T(8,128)(2,1)S(1)}, bf16[4,4,64,128]{3,2,1,0:T(8,128)(2,1)S(1)}, u32[]{:S(2)}, u32[]{:S(2)}) collective-permute-start(bf16[4,4,64,128]{3,2,1,0:T(8,128)(2,1)S(1)} %collective-permute-done.11.refs_4_), channel_id=1, source_target_pairs={{0,8},{8,0},{16,24},{24,16},{1,9},{9,1},{17,25},{25,17},{2,10},{10... | collective-permute-start | bytes 786440 | tf_op jit(solution)/shard_map/ppermute | solution.py:553
  36.9 2.1 %collective-permute-start.13 = (bf16[4,4,64,128]{3,2,1,0:T(8,128)(2,1)S(1)}, bf16[4,4,64,128]{3,2,1,0:T(8,128)(2,1)S(1)}, u32[]{:S(2)}, u32[]{:S(2)}) collective-permute-start(bf16[4,4,64,128]{3,2,1,0:T(8,128)(2,1)S(1)} %collective-permute-done.12.refs_5_), channel_id=1, source_target_pairs={{0,8},{8,0},{16,24},{24,16},{1,9},{9,1},{17,25},{25,17},{2,10},{10... | collective-permute-start | bytes 786440 | tf_op jit(solution)/shard_map/ppermute | solution.py:553

commit v6 on v5

--- a/solution.py
+++ b/solution.py
@@ -143,7 +143,7 @@
                     filtered[s, part, p] = total
             return carry
 
-        lax.fori_loop(0, OUTER, filter_column, 0, unroll=4)
+        lax.fori_loop(0, OUTER, filter_column, 0, unroll=8)
     table_copies[1].wait()
     table = table_ref[pl.ds(0, 2 * LANES), :]
     matrix_ref[0] = table.astype(jnp.bfloat16)
@@ -478,12 +478,11 @@
         slot = 1
         if bit != block_bits - 1:
             slot = (bit_of(own, bit) == top).astype(jnp.int32)
+        place = round_of(pairing_ref, mask)
         for group in range(half):
             vis[0, index, group], vis[1, index, group] = products(block[slot, group], other[group])
-        place = round_of(pairing_ref, mask)
-        for part in range(2):
             copy = pltpu.make_async_copy(
-                vis.at[part, index], vis_hbm.at[part, place], vis_sems.at[part, index]
+                vis.at[:, index, group], vis_hbm.at[:, place, group], vis_sems.at[index, group]
             )
             copy.start()
             copies.append(copy)
@@ -528,7 +527,7 @@
         scratch_shapes=[
             pltpu.VMEM((len(late), half, slices, rows, LANES), jnp.bfloat16),
             pltpu.VMEM(vis_shape, jnp.float32),
-            pltpu.SemaphoreType.DMA(vis_shape[:2]),
+            pltpu.SemaphoreType.DMA(vis_shape[1:3]),
         ],
         compiler_params=pltpu.CompilerParams(vmem_limit_bytes=16 * MIB),
         cost_estimate=pl.CostEstimate(
@@ -591,7 +590,7 @@
         hand_on_kernel,
         [(2,) + part] * len(evens),
         [held, relay_other],
-        [near],
+        [direct[0]],
     )
     rest = along(rest)
     if whole_tiles:

time: 40.7 us -> 40.5 us (level)
  no operation moved by 1% of the time
where the time goes in v6:
time: 40.5 us; the launch traced here: 40.4 us
  starting transfers between devices  21.6 us (53%)
  Pallas kernels  10.2 us (25%)
  waiting for transfers between devices  7.91 us (20%)
  between operations  0.75 us (2%)
    ppermute x16, starting transfers between devices, exchange(): return lax.ppermute(value, axis, [(i, i ^ mask) for i in range(count)])  21.6 us
    ppermute x16, waiting for transfers between devices, exchange(): return lax.ppermute(value, axis, [(i, i ^ mask) for i in range(count)])  7.91 us
    pallas_call x1, Pallas kernels, spectra_pieces(): pl.pallas_call(functools.partial(spectra_kernel, chan_count, spectra_coun...  6.87 us
    pallas_call x1, Pallas kernels, first_call(): pl.pallas_call(functools.partial(first_kernel, chan_count, block_bits, co...  1.69 us
    pallas_call x1, Pallas kernels, cross_call(): pl.pallas_call(functools.partial(cross_kernel, chan_count, block_bits, ea...  1.34 us
  transfers between devices with their start and end apart: 16, of which 4 were waited for; matrix products, arithmetic and copies ran while one was open for 0% of the time, Pallas kernels for 5%

profile of v6, /device:TPU:0, one launch (start us, length us, event | category | flops | bytes accessed | tf_op | source)
XLA Modules:
  0.0 40.4 jit_solution(669919694738372045)
XLA Ops:
  0.6 6.9 %spectra.1 = (bf16[4,4,16,128]{3,2,1,0:T(8,128)(2,1)S(1)}, bf16[4,4,16,128]{3,2,1,0:T(8,128)(2,1)S(1)}, bf16[4,4,16,128]{3,2,1,0:T(8,128)(2,1)S(1)}, bf16[4,4,16...) custom-call(bf16[2,16,77824]{2,1,0:T(8,128)(2,1)} %volt_hbm.1, ...), custom_call_target="tpu_custom_call" | custom-call | tf_op jit(solution)/shard_map/spectra/pallas_call | solution.py:242
  7.5 0.0 copy-start
  7.5 3.0 %collective-permute-start.3 = (bf16[4,4,4,16,128]{4,3,2,1,0:T(8,128)(2,1)S(1)}, bf16[4,4,4,16,128]{4,3,2,1,0:T(8,128)(2,1)S(1)}, u32[]{:S(2)}, u32[]{:S(2)}) collective-permute-start(bf16[4,4,4,16,128]{4,3,2,1,0:T(8,128)(2,1)S(1)} %get-tuple-element.27), channel_id=1, source_target_pairs={{0,1},{1,0},{2,3},{3,2},{4,5},{5,4},{6,7},{7,6},{8,9},{9,8},{10,11... | collective-permute-start | bytes 786440 | tf_op jit(solution)/shard_map/ppermute | solution.py:552
  10.6 0.1 collective-permute-start.7
  10.6 3.0 %collective-permute-start = (bf16[4,4,16,128]{3,2,1,0:T(8,128)(2,1)S(1)}, bf16[4,4,16,128]{3,2,1,0:T(8,128)(2,1)S(1)}, u32[]{:S(2)}, u32[]{:S(2)}) collective-permute-start(bf16[4,4,16,128]{3,2,1,0:T(8,128)(2,1)S(1)} %get-tuple-element.24), channel_id=1, source_target_pairs={{0,4},{1,5},{2,6},{3,7},{4,0},{5,1},{6,2},{7,3},{8,12},{9,13},{10,... | collective-permute-start | bytes 196616 | tf_op jit(solution)/shard_map/ppermute | solution.py:552
  13.6 1.3 %collective-permute-start.1 = (bf16[4,4,16,128]{3,2,1,0:T(8,128)(2,1)S(1)}, bf16[4,4,16,128]{3,2,1,0:T(8,128)(2,1)S(1)}, u32[]{:S(2)}, u32[]{:S(2)}) collective-permute-start(bf16[4,4,16,128]{3,2,1,0:T(8,128)(2,1)S(1)} %get-tuple-element.25), channel_id=1, source_target_pairs={{0,6},{1,7},{2,4},{3,5},{4,2},{5,3},{6,0},{7,1},{8,14},{9,15},{10,... | collective-permute-start | bytes 196616 | tf_op jit(solution)/shard_map/ppermute | solution.py:552
  15.0 0.2 collective-permute-start.2
  15.2 2.5 %collective-permute-done.3.refs_0_ = bf16[4,4,4,16,128]{4,3,2,1,0:T(8,128)(2,1)S(1)} collective-permute-done((bf16[4,4,4,16,128]{4,3,2,1,0:T(8,128)(2,1)S(1)}, bf16[4,4,4,16,128]{4,3,2,1,0:T(8,128)(2,1)S(1)}, u32[]{:S(2)}, u32[]{:S(2)}) %collective-permute-start.3) | collective-permute-done | bytes 262176 | tf_op jit(solution)/shard_map/ppermute | solution.py:552
  17.7 3.2 %collective-permute-start.4 = (bf16[4,4,16,128]{3,2,1,0:T(8,128)(2,1)S(1)}, bf16[4,4,16,128]{3,2,1,0:T(8,128)(2,1)S(1)}, u32[]{:S(2)}, u32[]{:S(2)}) collective-permute-start(bf16[4,4,16,128]{3,2,1,0:T(8,128)(2,1)S(1)} %get-tuple-element.29), channel_id=1, source_target_pairs={{0,4},{1,5},{2,6},{3,7},{4,0},{5,1},{6,2},{7,3},{8,12},{9,13},{10,... | collective-permute-start | bytes 196616 | tf_op jit(solution)/shard_map/ppermute | solution.py:552
  20.9 0.0 collective-permute-done.refs_1_.refs_2_
  20.9 1.3 %collective-permute-start.5 = (bf16[4,4,16,128]{3,2,1,0:T(8,128)(2,1)S(1)}, bf16[4,4,16,128]{3,2,1,0:T(8,128)(2,1)S(1)}, u32[]{:S(2)}, u32[]{:S(2)}) collective-permute-start(bf16[4,4,16,128]{3,2,1,0:T(8,128)(2,1)S(1)} %get-tuple-element.30), channel_id=1, source_target_pairs={{0,6},{1,7},{2,4},{3,5},{4,2},{5,3},{6,0},{7,1},{8,14},{9,15},{10,... | collective-permute-start | bytes 196616 | tf_op jit(solution)/shard_map/ppermute | solution.py:552
  22.3 0.0 collective-permute-done.1.refs_2_
  22.3 0.3 collective-permute-start.6
  22.6 0.0 collective-permute-done.2.refs_3_
  22.6 1.6 %collective-permute-start.11 = (bf16[4,4,64,128]{3,2,1,0:T(8,128)(2,1)S(1)}, bf16[4,4,64,128]{3,2,1,0:T(8,128)(2,1)S(1)}, u32[]{:S(2)}, u32[]{:S(2)}) collective-permute-start(bf16[4,4,64,128]{3,2,1,0:T(8,128)(2,1)S(1)} %near.1.refs_0_), channel_id=1, source_target_pairs={{0,16},{8,24},{16,0},{24,8},{1,17},{9,25},{17,1},{25,9},{2,18},{10... | collective-permute-start | bytes 786440 | tf_op jit(solution)/shard_map/ppermute | solution.py:552
  24.2 0.0 collective-permute-done.7.refs_1_.refs_3_
  24.2 2.8 %collective-permute-start.8 = (bf16[2,4,4,16,128]{4,3,2,1,0:T(8,128)(2,1)S(1)}, bf16[2,4,4,16,128]{4,3,2,1,0:T(8,128)(2,1)S(1)}, u32[]{:S(2)}, u32[]{:S(2)}) collective-permute-start(bf16[2,4,4,16,128]{4,3,2,1,0:T(8,128)(2,1)S(1)} %get-tuple-element.35), channel_id=1, source_target_pairs={{0,4},{1,5},{2,6},{3,7},{4,0},{5,1},{6,2},{7,3},{8,12},{9,13},{10,... | collective-permute-start | bytes 393224 | tf_op jit(solution)/shard_map/ppermute | solution.py:552
  27.0 0.0 collective-permute-done.4.refs_1_
  27.0 1.3 %collective-permute-start.9 = (bf16[2,4,4,16,128]{4,3,2,1,0:T(8,128)(2,1)S(1)}, bf16[2,4,4,16,128]{4,3,2,1,0:T(8,128)(2,1)S(1)}, u32[]{:S(2)}, u32[]{:S(2)}) collective-permute-start(bf16[2,4,4,16,128]{4,3,2,1,0:T(8,128)(2,1)S(1)} %get-tuple-element.36), channel_id=1, source_target_pairs={{0,6},{1,7},{2,4},{3,5},{4,2},{5,3},{6,0},{7,1},{8,14},{9,15},{10,... | collective-permute-start | bytes 393224 | tf_op jit(solution)/shard_map/ppermute | solution.py:552
  28.3 0.0 collective-permute-done.5.refs_2_
  28.3 1.0 %collective-permute-start.10 = (bf16[2,4,4,16,128]{4,3,2,1,0:T(8,128)(2,1)S(1)}, bf16[2,4,4,16,128]{4,3,2,1,0:T(8,128)(2,1)S(1)}, u32[]{:S(2)}, u32[]{:S(2)}) collective-permute-start(bf16[2,4,4,16,128]{4,3,2,1,0:T(8,128)(2,1)S(1)} %get-tuple-element.37), channel_id=1, source_target_pairs={{0,2},{1,3},{2,0},{3,1},{4,6},{5,7},{6,4},{7,5},{8,10},{9,11},{10,... | collective-permute-start | bytes 393224 | tf_op jit(solution)/shard_map/ppermute | solution.py:552
  29.4 0.0 collective-permute-done.6.refs_3_
  29.4 1.6 %collective-permute-start.12 = (bf16[4,4,64,128]{3,2,1,0:T(8,128)(2,1)S(1)}, bf16[4,4,64,128]{3,2,1,0:T(8,128)(2,1)S(1)}, u32[]{:S(2)}, u32[]{:S(2)}) collective-permute-start(bf16[4,4,64,128]{3,2,1,0:T(8,128)(2,1)S(1)} %far.1.refs_1_), channel_id=1, source_target_pairs={{0,16},{8,24},{16,0},{24,8},{1,17},{9,25},{17,1},{25,9},{2,18},{10... | collective-permute-start | bytes 786440 | tf_op jit(solution)/shard_map/ppermute | solution.py:552
  31.0 5.0 %collective-permute-done.8.refs_4_ = bf16[2,4,4,16,128]{4,3,2,1,0:T(8,128)(2,1)S(1)} collective-permute-done((bf16[2,4,4,16,128]{4,3,2,1,0:T(8,128)(2,1)S(1)}, bf16[2,4,4,16,128]{4,3,2,1,0:T(8,128)(2,1)S(1)}, u32[]{:S(2)}, u32[]{:S(2)}) %collective-permute-start.8) | collective-permute-done | bytes 131104 | tf_op jit(solution)/shard_map/ppermute | solution.py:552
  36.0 0.0 collective-permute-done.9.refs_5_
  36.0 0.1 collective-permute-done.10.refs_6_
  36.2 0.1 other.1
  36.3 0.1 collective-permute-start.15
  36.3 0.0 collective-permute-done.11.refs_4_
  36.4 0.5 %collective-permute-start.14 = (bf16[4,4,64,128]{3,2,1,0:T(8,128)(2,1)S(1)}, bf16[4,4,64,128]{3,2,1,0:T(8,128)(2,1)S(1)}, u32[]{:S(2)}, u32[]{:S(2)}) collective-permute-start(bf16[4,4,64,128]{3,2,1,0:T(8,128)(2,1)S(1)} %collective-permute-done.11.refs_4_), channel_id=1, source_target_pairs={{0,8},{8,0},{16,24},{24,16},{1,9},{9,1},{17,25},{25,17},{2,10},{10... | collective-permute-start | bytes 786440 | tf_op jit(solution)/shard_map/ppermute | solution.py:552
  36.8 0.0 collective-permute-done.12.refs_5_
  36.9 0.1 collective-permute-start.13
  36.9 0.0 copy-done
  36.9 1.7 %correlate_first.1 = (bf16[2,4,4,128,128]{4,3,2,1,0:T(8,128)(2,1)S(1)}, f32[2,8,128,128]{3,2,1,0:T(8,128)}, f32[2,3,4,128,128]{4,3,2,1,0:T(8,128)}) custom-call(s32[1,3]{1,0:T(1,128)S(1)} %bitcast.1, bf16[4,4,64,128]{3,2,1,0:T(8,128)(2,1)S(1)} %near.1.refs_0_, bf16[4,4,64,128]{3,2,1,0:T(8,128)(2,1)S(1)} %far.1.refs_1_, ...), custom_call_target="tpu_custom_call" | custom-call | flops 1048576 | bytes 4194304 | tf_op jit(solution)/shard_map/correlate_first/pallas_call | solution.py:419
  38.6 0.0 collective-permute-done.14.refs_0_
  38.7 0.3 collective-permute-done.13.refs_0_
  39.0 0.0 collective-permute-done.15.refs_0_
  39.0 1.3 %cross.1 = f32[2,3,4,128,128]{4,3,2,1,0:T(8,128)} custom-call(s32[1,3]{1,0:T(1,128)S(1)} %bitcast.2, bf16[2,4,4,128,128]{4,3,2,1,0:T(8,128)(2,1)S(1)} %get-tuple-element.40.block, bf16[1,4,4,128,128]{4,3,2,1,0:T(8,128)(2,1)S(1)} %fill_far.1.filled, bf16[2,4,4,64,128]{4,3,2,1,0:T(8,128)(2,1)S(1)} %collective-permute-done.15.refs_0_, ...), custom_call_target="tpu_custom_call", output_to_operand_aliasing={{}: (4, {})} | custom-call | flops 1073741824 | bytes 4194304 | tf_op jit(solution)/shard_map/cross/pallas_call | solution.py:520
  (6 shorter events, 0.2 us)
Async XLA Ops:
  7.5 29.4 %copy-start = (s32[3]{0:T(128)S(1)}, s32[3]{0:T(128)}, u32[]{:S(2)}) copy-start(s32[3]{0:T(128)} %param.6) | copy-start | bytes 40
  7.5 10.2 %collective-permute-start.3 = (bf16[4,4,4,16,128]{4,3,2,1,0:T(8,128)(2,1)S(1)}, bf16[4,4,4,16,128]{4,3,2,1,0:T(8,128)(2,1)S(1)}, u32[]{:S(2)}, u32[]{:S(2)}) collective-permute-start(bf16[4,4,4,16,128]{4,3,2,1,0:T(8,128)(2,1)S(1)} %get-tuple-element.27), channel_id=1, source_target_pairs={{0,1},{1,0},{2,3},{3,2},{4,5},{5,4},{6,7},{7,6},{8,9},{9,8},{10,11... | collective-permute-start | bytes 786440 | tf_op jit(solution)/shard_map/ppermute | solution.py:552
  10.6 13.6 %collective-permute-start.7 = (bf16[4,4,4,16,128]{4,3,2,1,0:T(8,128)(2,1)}, bf16[4,4,4,16,128]{4,3,2,1,0:T(8,128)(2,1)S(1)}, u32[]{:S(2)}, u32[]{:S(2)}) collective-permute-start(bf16[4,4,4,16,128]{4,3,2,1,0:T(8,128)(2,1)} %get-tuple-element.33), channel_id=1, source_target_pairs={{0,1},{1,0},{2,3},{3,2},{4,5},{5,4},{6,7},{7,6},{8,9},{9,8},{10,11... | collective-permute-start | bytes 786440 | tf_op jit(solution)/shard_map/ppermute | solution.py:552
  10.6 10.3 %collective-permute-start = (bf16[4,4,16,128]{3,2,1,0:T(8,128)(2,1)S(1)}, bf16[4,4,16,128]{3,2,1,0:T(8,128)(2,1)S(1)}, u32[]{:S(2)}, u32[]{:S(2)}) collective-permute-start(bf16[4,4,16,128]{3,2,1,0:T(8,128)(2,1)S(1)} %get-tuple-element.24), channel_id=1, source_target_pairs={{0,4},{1,5},{2,6},{3,7},{4,0},{5,1},{6,2},{7,3},{8,12},{9,13},{10,... | collective-permute-start | bytes 196616 | tf_op jit(solution)/shard_map/ppermute | solution.py:552
  13.6 8.6 %collective-permute-start.1 = (bf16[4,4,16,128]{3,2,1,0:T(8,128)(2,1)S(1)}, bf16[4,4,16,128]{3,2,1,0:T(8,128)(2,1)S(1)}, u32[]{:S(2)}, u32[]{:S(2)}) collective-permute-start(bf16[4,4,16,128]{3,2,1,0:T(8,128)(2,1)S(1)} %get-tuple-element.25), channel_id=1, source_target_pairs={{0,6},{1,7},{2,4},{3,5},{4,2},{5,3},{6,0},{7,1},{8,14},{9,15},{10,... | collective-permute-start | bytes 196616 | tf_op jit(solution)/shard_map/ppermute | solution.py:552
  15.0 7.6 %collective-permute-start.2 = (bf16[4,4,16,128]{3,2,1,0:T(8,128)(2,1)S(1)}, bf16[4,4,16,128]{3,2,1,0:T(8,128)(2,1)S(1)}, u32[]{:S(2)}, u32[]{:S(2)}) collective-permute-start(bf16[4,4,16,128]{3,2,1,0:T(8,128)(2,1)S(1)} %get-tuple-element.26), channel_id=1, source_target_pairs={{0,2},{1,3},{2,0},{3,1},{4,6},{5,7},{6,4},{7,5},{8,10},{9,11},{10,... | collective-permute-start | bytes 196616 | tf_op jit(solution)/shard_map/ppermute | solution.py:552
  17.7 9.3 %collective-permute-start.4 = (bf16[4,4,16,128]{3,2,1,0:T(8,128)(2,1)S(1)}, bf16[4,4,16,128]{3,2,1,0:T(8,128)(2,1)S(1)}, u32[]{:S(2)}, u32[]{:S(2)}) collective-permute-start(bf16[4,4,16,128]{3,2,1,0:T(8,128)(2,1)S(1)} %get-tuple-element.29), channel_id=1, source_target_pairs={{0,4},{1,5},{2,6},{3,7},{4,0},{5,1},{6,2},{7,3},{8,12},{9,13},{10,... | collective-permute-start | bytes 196616 | tf_op jit(solution)/shard_map/ppermute | solution.py:552
  20.9 7.4 %collective-permute-start.5 = (bf16[4,4,16,128]{3,2,1,0:T(8,128)(2,1)S(1)}, bf16[4,4,16,128]{3,2,1,0:T(8,128)(2,1)S(1)}, u32[]{:S(2)}, u32[]{:S(2)}) collective-permute-start(bf16[4,4,16,128]{3,2,1,0:T(8,128)(2,1)S(1)} %get-tuple-element.30), channel_id=1, source_target_pairs={{0,6},{1,7},{2,4},{3,5},{4,2},{5,3},{6,0},{7,1},{8,14},{9,15},{10,... | collective-permute-start | bytes 196616 | tf_op jit(solution)/shard_map/ppermute | solution.py:552
  22.3 7.1 %collective-permute-start.6 = (bf16[4,4,16,128]{3,2,1,0:T(8,128)(2,1)S(1)}, bf16[4,4,16,128]{3,2,1,0:T(8,128)(2,1)S(1)}, u32[]{:S(2)}, u32[]{:S(2)}) collective-permute-start(bf16[4,4,16,128]{3,2,1,0:T(8,128)(2,1)S(1)} %get-tuple-element.31), channel_id=1, source_target_pairs={{0,2},{1,3},{2,0},{3,1},{4,6},{5,7},{6,4},{7,5},{8,10},{9,11},{10,... | collective-permute-start | bytes 196616 | tf_op jit(solution)/shard_map/ppermute | solution.py:552
  22.6 13.8 %collective-permute-start.11 = (bf16[4,4,64,128]{3,2,1,0:T(8,128)(2,1)S(1)}, bf16[4,4,64,128]{3,2,1,0:T(8,128)(2,1)S(1)}, u32[]{:S(2)}, u32[]{:S(2)}) collective-permute-start(bf16[4,4,64,128]{3,2,1,0:T(8,128)(2,1)S(1)} %near.1.refs_0_), channel_id=1, source_target_pairs={{0,16},{8,24},{16,0},{24,8},{1,17},{9,25},{17,1},{25,9},{2,18},{10... | collective-permute-start | bytes 786440 | tf_op jit(solution)/shard_map/ppermute | solution.py:552
  24.2 11.8 %collective-permute-start.8 = (bf16[2,4,4,16,128]{4,3,2,1,0:T(8,128)(2,1)S(1)}, bf16[2,4,4,16,128]{4,3,2,1,0:T(8,128)(2,1)S(1)}, u32[]{:S(2)}, u32[]{:S(2)}) collective-permute-start(bf16[2,4,4,16,128]{4,3,2,1,0:T(8,128)(2,1)S(1)} %get-tuple-element.35), channel_id=1, source_target_pairs={{0,4},{1,5},{2,6},{3,7},{4,0},{5,1},{6,2},{7,3},{8,12},{9,13},{10,... | collective-permute-start | bytes 393224 | tf_op jit(solution)/shard_map/ppermute | solution.py:552
  27.0 9.0 %collective-permute-start.9 = (bf16[2,4,4,16,128]{4,3,2,1,0:T(8,128)(2,1)S(1)}, bf16[2,4,4,16,128]{4,3,2,1,0:T(8,128)(2,1)S(1)}, u32[]{:S(2)}, u32[]{:S(2)}) collective-permute-start(bf16[2,4,4,16,128]{4,3,2,1,0:T(8,128)(2,1)S(1)} %get-tuple-element.36), channel_id=1, source_target_pairs={{0,6},{1,7},{2,4},{3,5},{4,2},{5,3},{6,0},{7,1},{8,14},{9,15},{10,... | collective-permute-start | bytes 393224 | tf_op jit(solution)/shard_map/ppermute | solution.py:552
  28.3 7.8 %collective-permute-start.10 = (bf16[2,4,4,16,128]{4,3,2,1,0:T(8,128)(2,1)S(1)}, bf16[2,4,4,16,128]{4,3,2,1,0:T(8,128)(2,1)S(1)}, u32[]{:S(2)}, u32[]{:S(2)}) collective-permute-start(bf16[2,4,4,16,128]{4,3,2,1,0:T(8,128)(2,1)S(1)} %get-tuple-element.37), channel_id=1, source_target_pairs={{0,2},{1,3},{2,0},{3,1},{4,6},{5,7},{6,4},{7,5},{8,10},{9,11},{10,... | collective-permute-start | bytes 393224 | tf_op jit(solution)/shard_map/ppermute | solution.py:552
  29.4 7.4 %collective-permute-start.12 = (bf16[4,4,64,128]{3,2,1,0:T(8,128)(2,1)S(1)}, bf16[4,4,64,128]{3,2,1,0:T(8,128)(2,1)S(1)}, u32[]{:S(2)}, u32[]{:S(2)}) collective-permute-start(bf16[4,4,64,128]{3,2,1,0:T(8,128)(2,1)S(1)} %far.1.refs_1_), channel_id=1, source_target_pairs={{0,16},{8,24},{16,0},{24,8},{1,17},{9,25},{17,1},{25,9},{2,18},{10... | collective-permute-start | bytes 786440 | tf_op jit(solution)/shard_map/ppermute | solution.py:552
  36.3 2.8 %collective-permute-start.15 = (bf16[2,4,4,64,128]{4,3,2,1,0:T(8,128)(2,1)S(1)}, bf16[2,4,4,64,128]{4,3,2,1,0:T(8,128)(2,1)S(1)}, u32[]{:S(2)}, u32[]{:S(2)}) collective-permute-start(bf16[2,4,4,64,128]{4,3,2,1,0:T(8,128)(2,1)S(1)} %get-tuple-element.41), channel_id=1, source_target_pairs={{0,8},{8,0},{16,24},{24,16},{1,9},{9,1},{17,25},{25,17},{2,10},{10... | collective-permute-start | bytes 1572872 | tf_op jit(solution)/shard_map/ppermute | solution.py:552
  36.4 2.3 %collective-permute-start.14 = (bf16[4,4,64,128]{3,2,1,0:T(8,128)(2,1)S(1)}, bf16[4,4,64,128]{3,2,1,0:T(8,128)(2,1)S(1)}, u32[]{:S(2)}, u32[]{:S(2)}) collective-permute-start(bf16[4,4,64,128]{3,2,1,0:T(8,128)(2,1)S(1)} %collective-permute-done.11.refs_4_), channel_id=1, source_target_pairs={{0,8},{8,0},{16,24},{24,16},{1,9},{9,1},{17,25},{25,17},{2,10},{10... | collective-permute-start | bytes 786440 | tf_op jit(solution)/shard_map/ppermute | solution.py:552
  36.9 2.1 %collective-permute-start.13 = (bf16[4,4,64,128]{3,2,1,0:T(8,128)(2,1)S(1)}, bf16[4,4,64,128]{3,2,1,0:T(8,128)(2,1)S(1)}, u32[]{:S(2)}, u32[]{:S(2)}) collective-permute-start(bf16[4,4,64,128]{3,2,1,0:T(8,128)(2,1)S(1)} %collective-permute-done.12.refs_5_), channel_id=1, source_target_pairs={{0,8},{8,0},{16,24},{24,16},{1,9},{9,1},{17,25},{25,17},{2,10},{10... | collective-permute-start | bytes 786440 | tf_op jit(solution)/shard_map/ppermute | solution.py:552

commit v7 on v6

--- a/solution.py
+++ b/solution.py
@@ -113,8 +113,8 @@
             [(taps_hbm, taps_ref), (table_hbm, table_ref)]
         )
     ]
+    table_copies[0].start()
     volt_copies[0].start()
-    table_copies[0].start()
     for copy in volt_copies[1:]:
         copy.start()
     table_copies[1].start()

time: 40.5 us -> 40.5 us (level)
  no operation moved by 1% of the time
where the time goes in v7:
time: 40.5 us; the launch traced here: 40.4 us
  starting transfers between devices  21.6 us (53%)
  Pallas kernels  10.2 us (25%)
  waiting for transfers between devices  7.91 us (20%)
  between operations  0.75 us (2%)
    ppermute x16, starting transfers between devices, exchange(): return lax.ppermute(value, axis, [(i, i ^ mask) for i in range(count)])  21.6 us
    ppermute x16, waiting for transfers between devices, exchange(): return lax.ppermute(value, axis, [(i, i ^ mask) for i in range(count)])  7.91 us
    pallas_call x1, Pallas kernels, spectra_pieces(): pl.pallas_call(functools.partial(spectra_kernel, chan_count, spectra_coun...  6.87 us
    pallas_call x1, Pallas kernels, first_call(): pl.pallas_call(functools.partial(first_kernel, chan_count, block_bits, co...  1.69 us
    pallas_call x1, Pallas kernels, cross_call(): pl.pallas_call(functools.partial(cross_kernel, chan_count, block_bits, ea...  1.34 us
  transfers between devices with their start and end apart: 16, of which 4 were waited for; matrix products, arithmetic and copies ran while one was open for 0% of the time, Pallas kernels for 5%

profile of v7, /device:TPU:0, one launch (start us, length us, event | category | flops | bytes accessed | tf_op | source)
XLA Modules:
  0.0 40.4 jit_solution(669919694738372045)
XLA Ops:
  0.6 6.9 %spectra.1 = (bf16[4,4,16,128]{3,2,1,0:T(8,128)(2,1)S(1)}, bf16[4,4,16,128]{3,2,1,0:T(8,128)(2,1)S(1)}, bf16[4,4,16,128]{3,2,1,0:T(8,128)(2,1)S(1)}, bf16[4,4,16...) custom-call(bf16[2,16,77824]{2,1,0:T(8,128)(2,1)} %volt_hbm.1, ...), custom_call_target="tpu_custom_call" | custom-call | tf_op jit(solution)/shard_map/spectra/pallas_call | solution.py:242
  7.5 0.0 copy-start
  7.5 3.0 %collective-permute-start.3 = (bf16[4,4,4,16,128]{4,3,2,1,0:T(8,128)(2,1)S(1)}, bf16[4,4,4,16,128]{4,3,2,1,0:T(8,128)(2,1)S(1)}, u32[]{:S(2)}, u32[]{:S(2)}) collective-permute-start(bf16[4,4,4,16,128]{4,3,2,1,0:T(8,128)(2,1)S(1)} %get-tuple-element.27), channel_id=1, source_target_pairs={{0,1},{1,0},{2,3},{3,2},{4,5},{5,4},{6,7},{7,6},{8,9},{9,8},{10,11... | collective-permute-start | bytes 786440 | tf_op jit(solution)/shard_map/ppermute | solution.py:552
  10.6 0.1 collective-permute-start.7
  10.6 3.0 %collective-permute-start = (bf16[4,4,16,128]{3,2,1,0:T(8,128)(2,1)S(1)}, bf16[4,4,16,128]{3,2,1,0:T(8,128)(2,1)S(1)}, u32[]{:S(2)}, u32[]{:S(2)}) collective-permute-start(bf16[4,4,16,128]{3,2,1,0:T(8,128)(2,1)S(1)} %get-tuple-element.24), channel_id=1, source_target_pairs={{0,4},{1,5},{2,6},{3,7},{4,0},{5,1},{6,2},{7,3},{8,12},{9,13},{10,... | collective-permute-start | bytes 196616 | tf_op jit(solution)/shard_map/ppermute | solution.py:552
  13.6 1.3 %collective-permute-start.1 = (bf16[4,4,16,128]{3,2,1,0:T(8,128)(2,1)S(1)}, bf16[4,4,16,128]{3,2,1,0:T(8,128)(2,1)S(1)}, u32[]{:S(2)}, u32[]{:S(2)}) collective-permute-start(bf16[4,4,16,128]{3,2,1,0:T(8,128)(2,1)S(1)} %get-tuple-element.25), channel_id=1, source_target_pairs={{0,6},{1,7},{2,4},{3,5},{4,2},{5,3},{6,0},{7,1},{8,14},{9,15},{10,... | collective-permute-start | bytes 196616 | tf_op jit(solution)/shard_map/ppermute | solution.py:552
  15.0 0.2 collective-permute-start.2
  15.2 2.5 %collective-permute-done.3.refs_0_ = bf16[4,4,4,16,128]{4,3,2,1,0:T(8,128)(2,1)S(1)} collective-permute-done((bf16[4,4,4,16,128]{4,3,2,1,0:T(8,128)(2,1)S(1)}, bf16[4,4,4,16,128]{4,3,2,1,0:T(8,128)(2,1)S(1)}, u32[]{:S(2)}, u32[]{:S(2)}) %collective-permute-start.3) | collective-permute-done | bytes 262176 | tf_op jit(solution)/shard_map/ppermute | solution.py:552
  17.7 3.2 %collective-permute-start.4 = (bf16[4,4,16,128]{3,2,1,0:T(8,128)(2,1)S(1)}, bf16[4,4,16,128]{3,2,1,0:T(8,128)(2,1)S(1)}, u32[]{:S(2)}, u32[]{:S(2)}) collective-permute-start(bf16[4,4,16,128]{3,2,1,0:T(8,128)(2,1)S(1)} %get-tuple-element.29), channel_id=1, source_target_pairs={{0,4},{1,5},{2,6},{3,7},{4,0},{5,1},{6,2},{7,3},{8,12},{9,13},{10,... | collective-permute-start | bytes 196616 | tf_op jit(solution)/shard_map/ppermute | solution.py:552
  20.9 0.0 collective-permute-done.refs_1_.refs_2_
  20.9 1.3 %collective-permute-start.5 = (bf16[4,4,16,128]{3,2,1,0:T(8,128)(2,1)S(1)}, bf16[4,4,16,128]{3,2,1,0:T(8,128)(2,1)S(1)}, u32[]{:S(2)}, u32[]{:S(2)}) collective-permute-start(bf16[4,4,16,128]{3,2,1,0:T(8,128)(2,1)S(1)} %get-tuple-element.30), channel_id=1, source_target_pairs={{0,6},{1,7},{2,4},{3,5},{4,2},{5,3},{6,0},{7,1},{8,14},{9,15},{10,... | collective-permute-start | bytes 196616 | tf_op jit(solution)/shard_map/ppermute | solution.py:552
  22.3 0.0 collective-permute-done.1.refs_2_
  22.3 0.3 collective-permute-start.6
  22.6 0.0 collective-permute-done.2.refs_3_
  22.6 1.6 %collective-permute-start.11 = (bf16[4,4,64,128]{3,2,1,0:T(8,128)(2,1)S(1)}, bf16[4,4,64,128]{3,2,1,0:T(8,128)(2,1)S(1)}, u32[]{:S(2)}, u32[]{:S(2)}) collective-permute-start(bf16[4,4,64,128]{3,2,1,0:T(8,128)(2,1)S(1)} %near.1.refs_0_), channel_id=1, source_target_pairs={{0,16},{8,24},{16,0},{24,8},{1,17},{9,25},{17,1},{25,9},{2,18},{10... | collective-permute-start | bytes 786440 | tf_op jit(solution)/shard_map/ppermute | solution.py:552
  24.2 0.0 collective-permute-done.7.refs_1_.refs_3_
  24.2 2.8 %collective-permute-start.8 = (bf16[2,4,4,16,128]{4,3,2,1,0:T(8,128)(2,1)S(1)}, bf16[2,4,4,16,128]{4,3,2,1,0:T(8,128)(2,1)S(1)}, u32[]{:S(2)}, u32[]{:S(2)}) collective-permute-start(bf16[2,4,4,16,128]{4,3,2,1,0:T(8,128)(2,1)S(1)} %get-tuple-element.35), channel_id=1, source_target_pairs={{0,4},{1,5},{2,6},{3,7},{4,0},{5,1},{6,2},{7,3},{8,12},{9,13},{10,... | collective-permute-start | bytes 393224 | tf_op jit(solution)/shard_map/ppermute | solution.py:552
  27.0 0.0 collective-permute-done.4.refs_1_
  27.0 1.3 %collective-permute-start.9 = (bf16[2,4,4,16,128]{4,3,2,1,0:T(8,128)(2,1)S(1)}, bf16[2,4,4,16,128]{4,3,2,1,0:T(8,128)(2,1)S(1)}, u32[]{:S(2)}, u32[]{:S(2)}) collective-permute-start(bf16[2,4,4,16,128]{4,3,2,1,0:T(8,128)(2,1)S(1)} %get-tuple-element.36), channel_id=1, source_target_pairs={{0,6},{1,7},{2,4},{3,5},{4,2},{5,3},{6,0},{7,1},{8,14},{9,15},{10,... | collective-permute-start | bytes 393224 | tf_op jit(solution)/shard_map/ppermute | solution.py:552
  28.3 0.0 collective-permute-done.5.refs_2_
  28.3 1.0 %collective-permute-start.10 = (bf16[2,4,4,16,128]{4,3,2,1,0:T(8,128)(2,1)S(1)}, bf16[2,4,4,16,128]{4,3,2,1,0:T(8,128)(2,1)S(1)}, u32[]{:S(2)}, u32[]{:S(2)}) collective-permute-start(bf16[2,4,4,16,128]{4,3,2,1,0:T(8,128)(2,1)S(1)} %get-tuple-element.37), channel_id=1, source_target_pairs={{0,2},{1,3},{2,0},{3,1},{4,6},{5,7},{6,4},{7,5},{8,10},{9,11},{10,... | collective-permute-start | bytes 393224 | tf_op jit(solution)/shard_map/ppermute | solution.py:552
  29.4 0.0 collective-permute-done.6.refs_3_
  29.4 1.6 %collective-permute-start.12 = (bf16[4,4,64,128]{3,2,1,0:T(8,128)(2,1)S(1)}, bf16[4,4,64,128]{3,2,1,0:T(8,128)(2,1)S(1)}, u32[]{:S(2)}, u32[]{:S(2)}) collective-permute-start(bf16[4,4,64,128]{3,2,1,0:T(8,128)(2,1)S(1)} %far.1.refs_1_), channel_id=1, source_target_pairs={{0,16},{8,24},{16,0},{24,8},{1,17},{9,25},{17,1},{25,9},{2,18},{10... | collective-permute-start | bytes 786440 | tf_op jit(solution)/shard_map/ppermute | solution.py:552
  31.0 5.0 %collective-permute-done.8.refs_4_ = bf16[2,4,4,16,128]{4,3,2,1,0:T(8,128)(2,1)S(1)} collective-permute-done((bf16[2,4,4,16,128]{4,3,2,1,0:T(8,128)(2,1)S(1)}, bf16[2,4,4,16,128]{4,3,2,1,0:T(8,128)(2,1)S(1)}, u32[]{:S(2)}, u32[]{:S(2)}) %collective-permute-start.8) | collective-permute-done | bytes 131104 | tf_op jit(solution)/shard_map/ppermute | solution.py:552
  36.0 0.0 collective-permute-done.9.refs_5_
  36.0 0.1 collective-permute-done.10.refs_6_
  36.2 0.1 other.1
  36.3 0.1 collective-permute-start.15
  36.3 0.0 collective-permute-done.11.refs_4_
  36.4 0.5 %collective-permute-start.14 = (bf16[4,4,64,128]{3,2,1,0:T(8,128)(2,1)S(1)}, bf16[4,4,64,128]{3,2,1,0:T(8,128)(2,1)S(1)}, u32[]{:S(2)}, u32[]{:S(2)}) collective-permute-start(bf16[4,4,64,128]{3,2,1,0:T(8,128)(2,1)S(1)} %collective-permute-done.11.refs_4_), channel_id=1, source_target_pairs={{0,8},{8,0},{16,24},{24,16},{1,9},{9,1},{17,25},{25,17},{2,10},{10... | collective-permute-start | bytes 786440 | tf_op jit(solution)/shard_map/ppermute | solution.py:552
  36.8 0.0 collective-permute-done.12.refs_5_
  36.9 0.1 collective-permute-start.13
  36.9 0.0 copy-done
  36.9 1.7 %correlate_first.1 = (bf16[2,4,4,128,128]{4,3,2,1,0:T(8,128)(2,1)S(1)}, f32[2,8,128,128]{3,2,1,0:T(8,128)}, f32[2,3,4,128,128]{4,3,2,1,0:T(8,128)}) custom-call(s32[1,3]{1,0:T(1,128)S(1)} %bitcast.1, bf16[4,4,64,128]{3,2,1,0:T(8,128)(2,1)S(1)} %near.1.refs_0_, bf16[4,4,64,128]{3,2,1,0:T(8,128)(2,1)S(1)} %far.1.refs_1_, ...), custom_call_target="tpu_custom_call" | custom-call | flops 1048576 | bytes 4194304 | tf_op jit(solution)/shard_map/correlate_first/pallas_call | solution.py:419
  38.6 0.0 collective-permute-done.14.refs_0_
  38.7 0.3 collective-permute-done.13.refs_0_
  39.0 0.0 collective-permute-done.15.refs_0_
  39.0 1.3 %cross.1 = f32[2,3,4,128,128]{4,3,2,1,0:T(8,128)} custom-call(s32[1,3]{1,0:T(1,128)S(1)} %bitcast.2, bf16[2,4,4,128,128]{4,3,2,1,0:T(8,128)(2,1)S(1)} %get-tuple-element.40.block, bf16[1,4,4,128,128]{4,3,2,1,0:T(8,128)(2,1)S(1)} %fill_far.1.filled, bf16[2,4,4,64,128]{4,3,2,1,0:T(8,128)(2,1)S(1)} %collective-permute-done.15.refs_0_, ...), custom_call_target="tpu_custom_call", output_to_operand_aliasing={{}: (4, {})} | custom-call | flops 1073741824 | bytes 4194304 | tf_op jit(solution)/shard_map/cross/pallas_call | solution.py:520
  (6 shorter events, 0.2 us)
Async XLA Ops:
  7.5 29.4 %copy-start = (s32[3]{0:T(128)S(1)}, s32[3]{0:T(128)}, u32[]{:S(2)}) copy-start(s32[3]{0:T(128)} %param.6) | copy-start | bytes 40
  7.5 10.2 %collective-permute-start.3 = (bf16[4,4,4,16,128]{4,3,2,1,0:T(8,128)(2,1)S(1)}, bf16[4,4,4,16,128]{4,3,2,1,0:T(8,128)(2,1)S(1)}, u32[]{:S(2)}, u32[]{:S(2)}) collective-permute-start(bf16[4,4,4,16,128]{4,3,2,1,0:T(8,128)(2,1)S(1)} %get-tuple-element.27), channel_id=1, source_target_pairs={{0,1},{1,0},{2,3},{3,2},{4,5},{5,4},{6,7},{7,6},{8,9},{9,8},{10,11... | collective-permute-start | bytes 786440 | tf_op jit(solution)/shard_map/ppermute | solution.py:552
  10.6 13.6 %collective-permute-start.7 = (bf16[4,4,4,16,128]{4,3,2,1,0:T(8,128)(2,1)}, bf16[4,4,4,16,128]{4,3,2,1,0:T(8,128)(2,1)S(1)}, u32[]{:S(2)}, u32[]{:S(2)}) collective-permute-start(bf16[4,4,4,16,128]{4,3,2,1,0:T(8,128)(2,1)} %get-tuple-element.33), channel_id=1, source_target_pairs={{0,1},{1,0},{2,3},{3,2},{4,5},{5,4},{6,7},{7,6},{8,9},{9,8},{10,11... | collective-permute-start | bytes 786440 | tf_op jit(solution)/shard_map/ppermute | solution.py:552
  10.6 10.3 %collective-permute-start = (bf16[4,4,16,128]{3,2,1,0:T(8,128)(2,1)S(1)}, bf16[4,4,16,128]{3,2,1,0:T(8,128)(2,1)S(1)}, u32[]{:S(2)}, u32[]{:S(2)}) collective-permute-start(bf16[4,4,16,128]{3,2,1,0:T(8,128)(2,1)S(1)} %get-tuple-element.24), channel_id=1, source_target_pairs={{0,4},{1,5},{2,6},{3,7},{4,0},{5,1},{6,2},{7,3},{8,12},{9,13},{10,... | collective-permute-start | bytes 196616 | tf_op jit(solution)/shard_map/ppermute | solution.py:552
  13.6 8.6 %collective-permute-start.1 = (bf16[4,4,16,128]{3,2,1,0:T(8,128)(2,1)S(1)}, bf16[4,4,16,128]{3,2,1,0:T(8,128)(2,1)S(1)}, u32[]{:S(2)}, u32[]{:S(2)}) collective-permute-start(bf16[4,4,16,128]{3,2,1,0:T(8,128)(2,1)S(1)} %get-tuple-element.25), channel_id=1, source_target_pairs={{0,6},{1,7},{2,4},{3,5},{4,2},{5,3},{6,0},{7,1},{8,14},{9,15},{10,... | collective-permute-start | bytes 196616 | tf_op jit(solution)/shard_map/ppermute | solution.py:552
  15.0 7.6 %collective-permute-start.2 = (bf16[4,4,16,128]{3,2,1,0:T(8,128)(2,1)S(1)}, bf16[4,4,16,128]{3,2,1,0:T(8,128)(2,1)S(1)}, u32[]{:S(2)}, u32[]{:S(2)}) collective-permute-start(bf16[4,4,16,128]{3,2,1,0:T(8,128)(2,1)S(1)} %get-tuple-element.26), channel_id=1, source_target_pairs={{0,2},{1,3},{2,0},{3,1},{4,6},{5,7},{6,4},{7,5},{8,10},{9,11},{10,... | collective-permute-start | bytes 196616 | tf_op jit(solution)/shard_map/ppermute | solution.py:552
  17.7 9.3 %collective-permute-start.4 = (bf16[4,4,16,128]{3,2,1,0:T(8,128)(2,1)S(1)}, bf16[4,4,16,128]{3,2,1,0:T(8,128)(2,1)S(1)}, u32[]{:S(2)}, u32[]{:S(2)}) collective-permute-start(bf16[4,4,16,128]{3,2,1,0:T(8,128)(2,1)S(1)} %get-tuple-element.29), channel_id=1, source_target_pairs={{0,4},{1,5},{2,6},{3,7},{4,0},{5,1},{6,2},{7,3},{8,12},{9,13},{10,... | collective-permute-start | bytes 196616 | tf_op jit(solution)/shard_map/ppermute | solution.py:552
  20.9 7.4 %collective-permute-start.5 = (bf16[4,4,16,128]{3,2,1,0:T(8,128)(2,1)S(1)}, bf16[4,4,16,128]{3,2,1,0:T(8,128)(2,1)S(1)}, u32[]{:S(2)}, u32[]{:S(2)}) collective-permute-start(bf16[4,4,16,128]{3,2,1,0:T(8,128)(2,1)S(1)} %get-tuple-element.30), channel_id=1, source_target_pairs={{0,6},{1,7},{2,4},{3,5},{4,2},{5,3},{6,0},{7,1},{8,14},{9,15},{10,... | collective-permute-start | bytes 196616 | tf_op jit(solution)/shard_map/ppermute | solution.py:552
  22.3 7.1 %collective-permute-start.6 = (bf16[4,4,16,128]{3,2,1,0:T(8,128)(2,1)S(1)}, bf16[4,4,16,128]{3,2,1,0:T(8,128)(2,1)S(1)}, u32[]{:S(2)}, u32[]{:S(2)}) collective-permute-start(bf16[4,4,16,128]{3,2,1,0:T(8,128)(2,1)S(1)} %get-tuple-element.31), channel_id=1, source_target_pairs={{0,2},{1,3},{2,0},{3,1},{4,6},{5,7},{6,4},{7,5},{8,10},{9,11},{10,... | collective-permute-start | bytes 196616 | tf_op jit(solution)/shard_map/ppermute | solution.py:552
  22.6 13.8 %collective-permute-start.11 = (bf16[4,4,64,128]{3,2,1,0:T(8,128)(2,1)S(1)}, bf16[4,4,64,128]{3,2,1,0:T(8,128)(2,1)S(1)}, u32[]{:S(2)}, u32[]{:S(2)}) collective-permute-start(bf16[4,4,64,128]{3,2,1,0:T(8,128)(2,1)S(1)} %near.1.refs_0_), channel_id=1, source_target_pairs={{0,16},{8,24},{16,0},{24,8},{1,17},{9,25},{17,1},{25,9},{2,18},{10... | collective-permute-start | bytes 786440 | tf_op jit(solution)/shard_map/ppermute | solution.py:552
  24.2 11.8 %collective-permute-start.8 = (bf16[2,4,4,16,128]{4,3,2,1,0:T(8,128)(2,1)S(1)}, bf16[2,4,4,16,128]{4,3,2,1,0:T(8,128)(2,1)S(1)}, u32[]{:S(2)}, u32[]{:S(2)}) collective-permute-start(bf16[2,4,4,16,128]{4,3,2,1,0:T(8,128)(2,1)S(1)} %get-tuple-element.35), channel_id=1, source_target_pairs={{0,4},{1,5},{2,6},{3,7},{4,0},{5,1},{6,2},{7,3},{8,12},{9,13},{10,... | collective-permute-start | bytes 393224 | tf_op jit(solution)/shard_map/ppermute | solution.py:552
  27.0 9.0 %collective-permute-start.9 = (bf16[2,4,4,16,128]{4,3,2,1,0:T(8,128)(2,1)S(1)}, bf16[2,4,4,16,128]{4,3,2,1,0:T(8,128)(2,1)S(1)}, u32[]{:S(2)}, u32[]{:S(2)}) collective-permute-start(bf16[2,4,4,16,128]{4,3,2,1,0:T(8,128)(2,1)S(1)} %get-tuple-element.36), channel_id=1, source_target_pairs={{0,6},{1,7},{2,4},{3,5},{4,2},{5,3},{6,0},{7,1},{8,14},{9,15},{10,... | collective-permute-start | bytes 393224 | tf_op jit(solution)/shard_map/ppermute | solution.py:552
  28.3 7.8 %collective-permute-start.10 = (bf16[2,4,4,16,128]{4,3,2,1,0:T(8,128)(2,1)S(1)}, bf16[2,4,4,16,128]{4,3,2,1,0:T(8,128)(2,1)S(1)}, u32[]{:S(2)}, u32[]{:S(2)}) collective-permute-start(bf16[2,4,4,16,128]{4,3,2,1,0:T(8,128)(2,1)S(1)} %get-tuple-element.37), channel_id=1, source_target_pairs={{0,2},{1,3},{2,0},{3,1},{4,6},{5,7},{6,4},{7,5},{8,10},{9,11},{10,... | collective-permute-start | bytes 393224 | tf_op jit(solution)/shard_map/ppermute | solution.py:552
  29.4 7.4 %collective-permute-start.12 = (bf16[4,4,64,128]{3,2,1,0:T(8,128)(2,1)S(1)}, bf16[4,4,64,128]{3,2,1,0:T(8,128)(2,1)S(1)}, u32[]{:S(2)}, u32[]{:S(2)}) collective-permute-start(bf16[4,4,64,128]{3,2,1,0:T(8,128)(2,1)S(1)} %far.1.refs_1_), channel_id=1, source_target_pairs={{0,16},{8,24},{16,0},{24,8},{1,17},{9,25},{17,1},{25,9},{2,18},{10... | collective-permute-start | bytes 786440 | tf_op jit(solution)/shard_map/ppermute | solution.py:552
  36.3 2.8 %collective-permute-start.15 = (bf16[2,4,4,64,128]{4,3,2,1,0:T(8,128)(2,1)S(1)}, bf16[2,4,4,64,128]{4,3,2,1,0:T(8,128)(2,1)S(1)}, u32[]{:S(2)}, u32[]{:S(2)}) collective-permute-start(bf16[2,4,4,64,128]{4,3,2,1,0:T(8,128)(2,1)S(1)} %get-tuple-element.41), channel_id=1, source_target_pairs={{0,8},{8,0},{16,24},{24,16},{1,9},{9,1},{17,25},{25,17},{2,10},{10... | collective-permute-start | bytes 1572872 | tf_op jit(solution)/shard_map/ppermute | solution.py:552
  36.4 2.3 %collective-permute-start.14 = (bf16[4,4,64,128]{3,2,1,0:T(8,128)(2,1)S(1)}, bf16[4,4,64,128]{3,2,1,0:T(8,128)(2,1)S(1)}, u32[]{:S(2)}, u32[]{:S(2)}) collective-permute-start(bf16[4,4,64,128]{3,2,1,0:T(8,128)(2,1)S(1)} %collective-permute-done.11.refs_4_), channel_id=1, source_target_pairs={{0,8},{8,0},{16,24},{24,16},{1,9},{9,1},{17,25},{25,17},{2,10},{10... | collective-permute-start | bytes 786440 | tf_op jit(solution)/shard_map/ppermute | solution.py:552
  36.9 2.1 %collective-permute-start.13 = (bf16[4,4,64,128]{3,2,1,0:T(8,128)(2,1)S(1)}, bf16[4,4,64,128]{3,2,1,0:T(8,128)(2,1)S(1)}, u32[]{:S(2)}, u32[]{:S(2)}) collective-permute-start(bf16[4,4,64,128]{3,2,1,0:T(8,128)(2,1)S(1)} %collective-permute-done.12.refs_5_), channel_id=1, source_target_pairs={{0,8},{8,0},{16,24},{24,16},{1,9},{9,1},{17,25},{25,17},{2,10},{10... | collective-permute-start | bytes 786440 | tf_op jit(solution)/shard_map/ppermute | solution.py:552

commit v8 on v6

--- a/solution.py
+++ b/solution.py
@@ -401,11 +401,10 @@
         for part in range(2):
             store(autos.at[part, slot], autos_hbm.at[part, place], sems.at[part, slot])
     fill(partner, inputs[2], chan_count)
+    place = round_of(pairing_ref, mask)
     for group in range(half):
         vis[0, group], vis[1, group] = products(block[1, group], partner[group])
-    place = round_of(pairing_ref, mask)
-    for part in range(2):
-        store(vis.at[part], vis_hbm.at[part, place], vis_sems.at[part])
+        store(vis.at[:, group], vis_hbm.at[:, place, group], vis_sems.at[group])
     for copy in copies:
         copy.wait()
 
@@ -431,7 +430,7 @@
             pltpu.VMEM(auto_shape, jnp.float32),
             pltpu.VMEM((2, half, rows, rows), jnp.float32),
             pltpu.SemaphoreType.DMA((2, 2)),
-            pltpu.SemaphoreType.DMA((2,)),
+            pltpu.SemaphoreType.DMA((half,)),
         ],
         compiler_params=pltpu.CompilerParams(vmem_limit_bytes=12 * MIB),
         cost_estimate=pl.CostEstimate(flops=1 << 20, bytes_accessed=4 << 20, transcendentals=0),

time: 40.5 us -> 40.5 us (level)
  no operation moved by 1% of the time
where the time goes in v8:
time: 40.5 us; the launch traced here: 40.4 us
  starting transfers between devices  21.6 us (53%)
  Pallas kernels  10.2 us (25%)
  waiting for transfers between devices  7.9 us (20%)
  between operations  0.75 us (2%)
    ppermute x16, starting transfers between devices, exchange(): return lax.ppermute(value, axis, [(i, i ^ mask) for i in range(count)])  21.6 us
    ppermute x16, waiting for transfers between devices, exchange(): return lax.ppermute(value, axis, [(i, i ^ mask) for i in range(count)])  7.9 us
    pallas_call x1, Pallas kernels, spectra_pieces(): pl.pallas_call(functools.partial(spectra_kernel, chan_count, spectra_coun...  6.87 us
    pallas_call x1, Pallas kernels, first_call(): pl.pallas_call(functools.partial(first_kernel, chan_count, block_bits, co...  1.7 us
    pallas_call x1, Pallas kernels, cross_call(): pl.pallas_call(functools.partial(cross_kernel, chan_count, block_bits, ea...  1.34 us
  transfers between devices with their start and end apart: 16, of which 4 were waited for; matrix products, arithmetic and copies ran while one was open for 0% of the time, Pallas kernels for 5%

profile of v8, /device:TPU:0, one launch (start us, length us, event | category | flops | bytes accessed | tf_op | source)
XLA Modules:
  0.0 40.4 jit_solution(2313184575215638538)
XLA Ops:
  0.6 6.9 %spectra.1 = (bf16[4,4,16,128]{3,2,1,0:T(8,128)(2,1)S(1)}, bf16[4,4,16,128]{3,2,1,0:T(8,128)(2,1)S(1)}, bf16[4,4,16,128]{3,2,1,0:T(8,128)(2,1)S(1)}, bf16[4,4,16...) custom-call(bf16[2,16,77824]{2,1,0:T(8,128)(2,1)} %volt_hbm.1, ...), custom_call_target="tpu_custom_call" | custom-call | tf_op jit(solution)/shard_map/spectra/pallas_call | solution.py:242
  7.5 0.0 copy-start
  7.5 3.0 %collective-permute-start.3 = (bf16[4,4,4,16,128]{4,3,2,1,0:T(8,128)(2,1)S(1)}, bf16[4,4,4,16,128]{4,3,2,1,0:T(8,128)(2,1)S(1)}, u32[]{:S(2)}, u32[]{:S(2)}) collective-permute-start(bf16[4,4,4,16,128]{4,3,2,1,0:T(8,128)(2,1)S(1)} %get-tuple-element.27), channel_id=1, source_target_pairs={{0,1},{1,0},{2,3},{3,2},{4,5},{5,4},{6,7},{7,6},{8,9},{9,8},{10,11... | collective-permute-start | bytes 786440 | tf_op jit(solution)/shard_map/ppermute | solution.py:551
  10.6 0.1 collective-permute-start.7
  10.6 3.0 %collective-permute-start = (bf16[4,4,16,128]{3,2,1,0:T(8,128)(2,1)S(1)}, bf16[4,4,16,128]{3,2,1,0:T(8,128)(2,1)S(1)}, u32[]{:S(2)}, u32[]{:S(2)}) collective-permute-start(bf16[4,4,16,128]{3,2,1,0:T(8,128)(2,1)S(1)} %get-tuple-element.24), channel_id=1, source_target_pairs={{0,4},{1,5},{2,6},{3,7},{4,0},{5,1},{6,2},{7,3},{8,12},{9,13},{10,... | collective-permute-start | bytes 196616 | tf_op jit(solution)/shard_map/ppermute | solution.py:551
  13.6 1.3 %collective-permute-start.1 = (bf16[4,4,16,128]{3,2,1,0:T(8,128)(2,1)S(1)}, bf16[4,4,16,128]{3,2,1,0:T(8,128)(2,1)S(1)}, u32[]{:S(2)}, u32[]{:S(2)}) collective-permute-start(bf16[4,4,16,128]{3,2,1,0:T(8,128)(2,1)S(1)} %get-tuple-element.25), channel_id=1, source_target_pairs={{0,6},{1,7},{2,4},{3,5},{4,2},{5,3},{6,0},{7,1},{8,14},{9,15},{10,... | collective-permute-start | bytes 196616 | tf_op jit(solution)/shard_map/ppermute | solution.py:551
  15.0 0.2 collective-permute-start.2
  15.2 2.5 %collective-permute-done.3.refs_0_ = bf16[4,4,4,16,128]{4,3,2,1,0:T(8,128)(2,1)S(1)} collective-permute-done((bf16[4,4,4,16,128]{4,3,2,1,0:T(8,128)(2,1)S(1)}, bf16[4,4,4,16,128]{4,3,2,1,0:T(8,128)(2,1)S(1)}, u32[]{:S(2)}, u32[]{:S(2)}) %collective-permute-start.3) | collective-permute-done | bytes 262176 | tf_op jit(solution)/shard_map/ppermute | solution.py:551
  17.7 3.2 %collective-permute-start.4 = (bf16[4,4,16,128]{3,2,1,0:T(8,128)(2,1)S(1)}, bf16[4,4,16,128]{3,2,1,0:T(8,128)(2,1)S(1)}, u32[]{:S(2)}, u32[]{:S(2)}) collective-permute-start(bf16[4,4,16,128]{3,2,1,0:T(8,128)(2,1)S(1)} %get-tuple-element.29), channel_id=1, source_target_pairs={{0,4},{1,5},{2,6},{3,7},{4,0},{5,1},{6,2},{7,3},{8,12},{9,13},{10,... | collective-permute-start | bytes 196616 | tf_op jit(solution)/shard_map/ppermute | solution.py:551
  20.9 0.0 collective-permute-done.refs_1_.refs_2_
  20.9 1.3 %collective-permute-start.5 = (bf16[4,4,16,128]{3,2,1,0:T(8,128)(2,1)S(1)}, bf16[4,4,16,128]{3,2,1,0:T(8,128)(2,1)S(1)}, u32[]{:S(2)}, u32[]{:S(2)}) collective-permute-start(bf16[4,4,16,128]{3,2,1,0:T(8,128)(2,1)S(1)} %get-tuple-element.30), channel_id=1, source_target_pairs={{0,6},{1,7},{2,4},{3,5},{4,2},{5,3},{6,0},{7,1},{8,14},{9,15},{10,... | collective-permute-start | bytes 196616 | tf_op jit(solution)/shard_map/ppermute | solution.py:551
  22.3 0.0 collective-permute-done.1.refs_2_
  22.3 0.3 collective-permute-start.6
  22.6 0.0 collective-permute-done.2.refs_3_
  22.6 1.6 %collective-permute-start.11 = (bf16[4,4,64,128]{3,2,1,0:T(8,128)(2,1)S(1)}, bf16[4,4,64,128]{3,2,1,0:T(8,128)(2,1)S(1)}, u32[]{:S(2)}, u32[]{:S(2)}) collective-permute-start(bf16[4,4,64,128]{3,2,1,0:T(8,128)(2,1)S(1)} %near.1.refs_0_), channel_id=1, source_target_pairs={{0,16},{8,24},{16,0},{24,8},{1,17},{9,25},{17,1},{25,9},{2,18},{10... | collective-permute-start | bytes 786440 | tf_op jit(solution)/shard_map/ppermute | solution.py:551
  24.2 0.0 collective-permute-done.7.refs_1_.refs_3_
  24.2 2.8 %collective-permute-start.8 = (bf16[2,4,4,16,128]{4,3,2,1,0:T(8,128)(2,1)S(1)}, bf16[2,4,4,16,128]{4,3,2,1,0:T(8,128)(2,1)S(1)}, u32[]{:S(2)}, u32[]{:S(2)}) collective-permute-start(bf16[2,4,4,16,128]{4,3,2,1,0:T(8,128)(2,1)S(1)} %get-tuple-element.35), channel_id=1, source_target_pairs={{0,4},{1,5},{2,6},{3,7},{4,0},{5,1},{6,2},{7,3},{8,12},{9,13},{10,... | collective-permute-start | bytes 393224 | tf_op jit(solution)/shard_map/ppermute | solution.py:551
  27.0 0.0 collective-permute-done.4.refs_1_
  27.0 1.3 %collective-permute-start.9 = (bf16[2,4,4,16,128]{4,3,2,1,0:T(8,128)(2,1)S(1)}, bf16[2,4,4,16,128]{4,3,2,1,0:T(8,128)(2,1)S(1)}, u32[]{:S(2)}, u32[]{:S(2)}) collective-permute-start(bf16[2,4,4,16,128]{4,3,2,1,0:T(8,128)(2,1)S(1)} %get-tuple-element.36), channel_id=1, source_target_pairs={{0,6},{1,7},{2,4},{3,5},{4,2},{5,3},{6,0},{7,1},{8,14},{9,15},{10,... | collective-permute-start | bytes 393224 | tf_op jit(solution)/shard_map/ppermute | solution.py:551
  28.3 0.0 collective-permute-done.5.refs_2_
  28.3 1.0 %collective-permute-start.10 = (bf16[2,4,4,16,128]{4,3,2,1,0:T(8,128)(2,1)S(1)}, bf16[2,4,4,16,128]{4,3,2,1,0:T(8,128)(2,1)S(1)}, u32[]{:S(2)}, u32[]{:S(2)}) collective-permute-start(bf16[2,4,4,16,128]{4,3,2,1,0:T(8,128)(2,1)S(1)} %get-tuple-element.37), channel_id=1, source_target_pairs={{0,2},{1,3},{2,0},{3,1},{4,6},{5,7},{6,4},{7,5},{8,10},{9,11},{10,... | collective-permute-start | bytes 393224 | tf_op jit(solution)/shard_map/ppermute | solution.py:551
  29.4 0.0 collective-permute-done.6.refs_3_
  29.4 1.6 %collective-permute-start.12 = (bf16[4,4,64,128]{3,2,1,0:T(8,128)(2,1)S(1)}, bf16[4,4,64,128]{3,2,1,0:T(8,128)(2,1)S(1)}, u32[]{:S(2)}, u32[]{:S(2)}) collective-permute-start(bf16[4,4,64,128]{3,2,1,0:T(8,128)(2,1)S(1)} %far.1.refs_1_), channel_id=1, source_target_pairs={{0,16},{8,24},{16,0},{24,8},{1,17},{9,25},{17,1},{25,9},{2,18},{10... | collective-permute-start | bytes 786440 | tf_op jit(solution)/shard_map/ppermute | solution.py:551
  31.0 5.0 %collective-permute-done.8.refs_4_ = bf16[2,4,4,16,128]{4,3,2,1,0:T(8,128)(2,1)S(1)} collective-permute-done((bf16[2,4,4,16,128]{4,3,2,1,0:T(8,128)(2,1)S(1)}, bf16[2,4,4,16,128]{4,3,2,1,0:T(8,128)(2,1)S(1)}, u32[]{:S(2)}, u32[]{:S(2)}) %collective-permute-start.8) | collective-permute-done | bytes 131104 | tf_op jit(solution)/shard_map/ppermute | solution.py:551
  36.0 0.0 collective-permute-done.9.refs_5_
  36.0 0.1 collective-permute-done.10.refs_6_
  36.2 0.1 other.1
  36.3 0.1 collective-permute-start.15
  36.3 0.0 collective-permute-done.11.refs_4_
  36.4 0.5 %collective-permute-start.14 = (bf16[4,4,64,128]{3,2,1,0:T(8,128)(2,1)S(1)}, bf16[4,4,64,128]{3,2,1,0:T(8,128)(2,1)S(1)}, u32[]{:S(2)}, u32[]{:S(2)}) collective-permute-start(bf16[4,4,64,128]{3,2,1,0:T(8,128)(2,1)S(1)} %collective-permute-done.11.refs_4_), channel_id=1, source_target_pairs={{0,8},{8,0},{16,24},{24,16},{1,9},{9,1},{17,25},{25,17},{2,10},{10... | collective-permute-start | bytes 786440 | tf_op jit(solution)/shard_map/ppermute | solution.py:551
  36.8 0.0 collective-permute-done.12.refs_5_
  36.9 0.1 collective-permute-start.13
  36.9 0.0 copy-done
  36.9 1.7 %correlate_first.1 = (bf16[2,4,4,128,128]{4,3,2,1,0:T(8,128)(2,1)S(1)}, f32[2,8,128,128]{3,2,1,0:T(8,128)}, f32[2,3,4,128,128]{4,3,2,1,0:T(8,128)}) custom-call(s32[1,3]{1,0:T(1,128)S(1)} %bitcast.1, bf16[4,4,64,128]{3,2,1,0:T(8,128)(2,1)S(1)} %near.1.refs_0_, bf16[4,4,64,128]{3,2,1,0:T(8,128)(2,1)S(1)} %far.1.refs_1_, ...), custom_call_target="tpu_custom_call" | custom-call | flops 1048576 | bytes 4194304 | tf_op jit(solution)/shard_map/correlate_first/pallas_call | solution.py:418
  38.6 0.0 collective-permute-done.14.refs_0_
  38.7 0.3 collective-permute-done.13.refs_0_
  39.0 0.0 collective-permute-done.15.refs_0_
  39.0 1.3 %cross.1 = f32[2,3,4,128,128]{4,3,2,1,0:T(8,128)} custom-call(s32[1,3]{1,0:T(1,128)S(1)} %bitcast.2, bf16[2,4,4,128,128]{4,3,2,1,0:T(8,128)(2,1)S(1)} %get-tuple-element.40.block, bf16[1,4,4,128,128]{4,3,2,1,0:T(8,128)(2,1)S(1)} %fill_far.1.filled, bf16[2,4,4,64,128]{4,3,2,1,0:T(8,128)(2,1)S(1)} %collective-permute-done.15.refs_0_, ...), custom_call_target="tpu_custom_call", output_to_operand_aliasing={{}: (4, {})} | custom-call | flops 1073741824 | bytes 4194304 | tf_op jit(solution)/shard_map/cross/pallas_call | solution.py:519
  (6 shorter events, 0.2 us)
Async XLA Ops:
  7.5 29.4 %copy-start = (s32[3]{0:T(128)S(1)}, s32[3]{0:T(128)}, u32[]{:S(2)}) copy-start(s32[3]{0:T(128)} %param.6) | copy-start | bytes 40
  7.5 10.2 %collective-permute-start.3 = (bf16[4,4,4,16,128]{4,3,2,1,0:T(8,128)(2,1)S(1)}, bf16[4,4,4,16,128]{4,3,2,1,0:T(8,128)(2,1)S(1)}, u32[]{:S(2)}, u32[]{:S(2)}) collective-permute-start(bf16[4,4,4,16,128]{4,3,2,1,0:T(8,128)(2,1)S(1)} %get-tuple-element.27), channel_id=1, source_target_pairs={{0,1},{1,0},{2,3},{3,2},{4,5},{5,4},{6,7},{7,6},{8,9},{9,8},{10,11... | collective-permute-start | bytes 786440 | tf_op jit(solution)/shard_map/ppermute | solution.py:551
  10.6 13.6 %collective-permute-start.7 = (bf16[4,4,4,16,128]{4,3,2,1,0:T(8,128)(2,1)}, bf16[4,4,4,16,128]{4,3,2,1,0:T(8,128)(2,1)S(1)}, u32[]{:S(2)}, u32[]{:S(2)}) collective-permute-start(bf16[4,4,4,16,128]{4,3,2,1,0:T(8,128)(2,1)} %get-tuple-element.33), channel_id=1, source_target_pairs={{0,1},{1,0},{2,3},{3,2},{4,5},{5,4},{6,7},{7,6},{8,9},{9,8},{10,11... | collective-permute-start | bytes 786440 | tf_op jit(solution)/shard_map/ppermute | solution.py:551
  10.6 10.3 %collective-permute-start = (bf16[4,4,16,128]{3,2,1,0:T(8,128)(2,1)S(1)}, bf16[4,4,16,128]{3,2,1,0:T(8,128)(2,1)S(1)}, u32[]{:S(2)}, u32[]{:S(2)}) collective-permute-start(bf16[4,4,16,128]{3,2,1,0:T(8,128)(2,1)S(1)} %get-tuple-element.24), channel_id=1, source_target_pairs={{0,4},{1,5},{2,6},{3,7},{4,0},{5,1},{6,2},{7,3},{8,12},{9,13},{10,... | collective-permute-start | bytes 196616 | tf_op jit(solution)/shard_map/ppermute | solution.py:551
  13.6 8.6 %collective-permute-start.1 = (bf16[4,4,16,128]{3,2,1,0:T(8,128)(2,1)S(1)}, bf16[4,4,16,128]{3,2,1,0:T(8,128)(2,1)S(1)}, u32[]{:S(2)}, u32[]{:S(2)}) collective-permute-start(bf16[4,4,16,128]{3,2,1,0:T(8,128)(2,1)S(1)} %get-tuple-element.25), channel_id=1, source_target_pairs={{0,6},{1,7},{2,4},{3,5},{4,2},{5,3},{6,0},{7,1},{8,14},{9,15},{10,... | collective-permute-start | bytes 196616 | tf_op jit(solution)/shard_map/ppermute | solution.py:551
  15.0 7.6 %collective-permute-start.2 = (bf16[4,4,16,128]{3,2,1,0:T(8,128)(2,1)S(1)}, bf16[4,4,16,128]{3,2,1,0:T(8,128)(2,1)S(1)}, u32[]{:S(2)}, u32[]{:S(2)}) collective-permute-start(bf16[4,4,16,128]{3,2,1,0:T(8,128)(2,1)S(1)} %get-tuple-element.26), channel_id=1, source_target_pairs={{0,2},{1,3},{2,0},{3,1},{4,6},{5,7},{6,4},{7,5},{8,10},{9,11},{10,... | collective-permute-start | bytes 196616 | tf_op jit(solution)/shard_map/ppermute | solution.py:551
  17.7 9.3 %collective-permute-start.4 = (bf16[4,4,16,128]{3,2,1,0:T(8,128)(2,1)S(1)}, bf16[4,4,16,128]{3,2,1,0:T(8,128)(2,1)S(1)}, u32[]{:S(2)}, u32[]{:S(2)}) collective-permute-start(bf16[4,4,16,128]{3,2,1,0:T(8,128)(2,1)S(1)} %get-tuple-element.29), channel_id=1, source_target_pairs={{0,4},{1,5},{2,6},{3,7},{4,0},{5,1},{6,2},{7,3},{8,12},{9,13},{10,... | collective-permute-start | bytes 196616 | tf_op jit(solution)/shard_map/ppermute | solution.py:551
  20.9 7.4 %collective-permute-start.5 = (bf16[4,4,16,128]{3,2,1,0:T(8,128)(2,1)S(1)}, bf16[4,4,16,128]{3,2,1,0:T(8,128)(2,1)S(1)}, u32[]{:S(2)}, u32[]{:S(2)}) collective-permute-start(bf16[4,4,16,128]{3,2,1,0:T(8,128)(2,1)S(1)} %get-tuple-element.30), channel_id=1, source_target_pairs={{0,6},{1,7},{2,4},{3,5},{4,2},{5,3},{6,0},{7,1},{8,14},{9,15},{10,... | collective-permute-start | bytes 196616 | tf_op jit(solution)/shard_map/ppermute | solution.py:551
  22.3 7.1 %collective-permute-start.6 = (bf16[4,4,16,128]{3,2,1,0:T(8,128)(2,1)S(1)}, bf16[4,4,16,128]{3,2,1,0:T(8,128)(2,1)S(1)}, u32[]{:S(2)}, u32[]{:S(2)}) collective-permute-start(bf16[4,4,16,128]{3,2,1,0:T(8,128)(2,1)S(1)} %get-tuple-element.31), channel_id=1, source_target_pairs={{0,2},{1,3},{2,0},{3,1},{4,6},{5,7},{6,4},{7,5},{8,10},{9,11},{10,... | collective-permute-start | bytes 196616 | tf_op jit(solution)/shard_map/ppermute | solution.py:551
  22.6 13.8 %collective-permute-start.11 = (bf16[4,4,64,128]{3,2,1,0:T(8,128)(2,1)S(1)}, bf16[4,4,64,128]{3,2,1,0:T(8,128)(2,1)S(1)}, u32[]{:S(2)}, u32[]{:S(2)}) collective-permute-start(bf16[4,4,64,128]{3,2,1,0:T(8,128)(2,1)S(1)} %near.1.refs_0_), channel_id=1, source_target_pairs={{0,16},{8,24},{16,0},{24,8},{1,17},{9,25},{17,1},{25,9},{2,18},{10... | collective-permute-start | bytes 786440 | tf_op jit(solution)/shard_map/ppermute | solution.py:551
  24.2 11.8 %collective-permute-start.8 = (bf16[2,4,4,16,128]{4,3,2,1,0:T(8,128)(2,1)S(1)}, bf16[2,4,4,16,128]{4,3,2,1,0:T(8,128)(2,1)S(1)}, u32[]{:S(2)}, u32[]{:S(2)}) collective-permute-start(bf16[2,4,4,16,128]{4,3,2,1,0:T(8,128)(2,1)S(1)} %get-tuple-element.35), channel_id=1, source_target_pairs={{0,4},{1,5},{2,6},{3,7},{4,0},{5,1},{6,2},{7,3},{8,12},{9,13},{10,... | collective-permute-start | bytes 393224 | tf_op jit(solution)/shard_map/ppermute | solution.py:551
  27.0 9.0 %collective-permute-start.9 = (bf16[2,4,4,16,128]{4,3,2,1,0:T(8,128)(2,1)S(1)}, bf16[2,4,4,16,128]{4,3,2,1,0:T(8,128)(2,1)S(1)}, u32[]{:S(2)}, u32[]{:S(2)}) collective-permute-start(bf16[2,4,4,16,128]{4,3,2,1,0:T(8,128)(2,1)S(1)} %get-tuple-element.36), channel_id=1, source_target_pairs={{0,6},{1,7},{2,4},{3,5},{4,2},{5,3},{6,0},{7,1},{8,14},{9,15},{10,... | collective-permute-start | bytes 393224 | tf_op jit(solution)/shard_map/ppermute | solution.py:551
  28.3 7.8 %collective-permute-start.10 = (bf16[2,4,4,16,128]{4,3,2,1,0:T(8,128)(2,1)S(1)}, bf16[2,4,4,16,128]{4,3,2,1,0:T(8,128)(2,1)S(1)}, u32[]{:S(2)}, u32[]{:S(2)}) collective-permute-start(bf16[2,4,4,16,128]{4,3,2,1,0:T(8,128)(2,1)S(1)} %get-tuple-element.37), channel_id=1, source_target_pairs={{0,2},{1,3},{2,0},{3,1},{4,6},{5,7},{6,4},{7,5},{8,10},{9,11},{10,... | collective-permute-start | bytes 393224 | tf_op jit(solution)/shard_map/ppermute | solution.py:551
  29.4 7.4 %collective-permute-start.12 = (bf16[4,4,64,128]{3,2,1,0:T(8,128)(2,1)S(1)}, bf16[4,4,64,128]{3,2,1,0:T(8,128)(2,1)S(1)}, u32[]{:S(2)}, u32[]{:S(2)}) collective-permute-start(bf16[4,4,64,128]{3,2,1,0:T(8,128)(2,1)S(1)} %far.1.refs_1_), channel_id=1, source_target_pairs={{0,16},{8,24},{16,0},{24,8},{1,17},{9,25},{17,1},{25,9},{2,18},{10... | collective-permute-start | bytes 786440 | tf_op jit(solution)/shard_map/ppermute | solution.py:551
  36.3 2.8 %collective-permute-start.15 = (bf16[2,4,4,64,128]{4,3,2,1,0:T(8,128)(2,1)S(1)}, bf16[2,4,4,64,128]{4,3,2,1,0:T(8,128)(2,1)S(1)}, u32[]{:S(2)}, u32[]{:S(2)}) collective-permute-start(bf16[2,4,4,64,128]{4,3,2,1,0:T(8,128)(2,1)S(1)} %get-tuple-element.41), channel_id=1, source_target_pairs={{0,8},{8,0},{16,24},{24,16},{1,9},{9,1},{17,25},{25,17},{2,10},{10... | collective-permute-start | bytes 1572872 | tf_op jit(solution)/shard_map/ppermute | solution.py:551
  36.4 2.3 %collective-permute-start.14 = (bf16[4,4,64,128]{3,2,1,0:T(8,128)(2,1)S(1)}, bf16[4,4,64,128]{3,2,1,0:T(8,128)(2,1)S(1)}, u32[]{:S(2)}, u32[]{:S(2)}) collective-permute-start(bf16[4,4,64,128]{3,2,1,0:T(8,128)(2,1)S(1)} %collective-permute-done.11.refs_4_), channel_id=1, source_target_pairs={{0,8},{8,0},{16,24},{24,16},{1,9},{9,1},{17,25},{25,17},{2,10},{10... | collective-permute-start | bytes 786440 | tf_op jit(solution)/shard_map/ppermute | solution.py:551
  36.9 2.1 %collective-permute-start.13 = (bf16[4,4,64,128]{3,2,1,0:T(8,128)(2,1)S(1)}, bf16[4,4,64,128]{3,2,1,0:T(8,128)(2,1)S(1)}, u32[]{:S(2)}, u32[]{:S(2)}) collective-permute-start(bf16[4,4,64,128]{3,2,1,0:T(8,128)(2,1)S(1)} %collective-permute-done.12.refs_5_), channel_id=1, source_target_pairs={{0,8},{8,0},{16,24},{24,16},{1,9},{9,1},{17,25},{25,17},{2,10},{10... | collective-permute-start | bytes 786440 | tf_op jit(solution)/shard_map/ppermute | solution.py:551
